TPU v7x, 32 devices: a whole 2x2x4 slice. The times are simulated.
32 devices in a mesh: dp: 8 (over z, core), tensor: 4 (over y, x).
Axes of the slice: x: 2, y: 2, z: 4, core: 2. Of those that a mesh axis runs over, the one named last changes fastest.
Arguments:
- streams: bfloat16 [8192, 4, 2048], P('dp', None, 'tensor'), may hold values from -6 to 6
- segments: int32 [8192], P('dp'), may hold values from 0 to 3, as said below
- positions: int32 [8192], P('dp'), may hold values from 0 to 511, as said below
- mix_in1: float32 [4], replicated, may hold values from 0.2 to 0.8
- mix_res1: float32 [4, 4], replicated, may hold values from -0.6 to 0.6
- mix_out1: float32 [4], replicated, may hold values from 0.5 to 1.5
- mix_in2: float32 [4], replicated, may hold values from 0.2 to 0.8
- mix_res2: float32 [4, 4], replicated, may hold values from -0.6 to 0.6
- mix_out2: float32 [4], replicated, may hold values from 0.5 to 1.5
- w_query: bfloat16 [2048, 2048], P(None, 'tensor'), may hold values from -0.125 to 0.125
- w_key: bfloat16 [2048, 2048], P(None, 'tensor'), may hold values from -0.125 to 0.125
- w_value: bfloat16 [2048, 2048], P(None, 'tensor'), may hold values from -0.125 to 0.125
- w_output: bfloat16 [2048, 2048], P('tensor'), may hold values from -0.375 to 0.375
- w_gate: bfloat16 [2048, 8192], P(None, 'tensor'), may hold values from -0.125 to 0.125
- w_up: bfloat16 [2048, 8192], P(None, 'tensor'), may hold values from -0.125 to 0.125
- w_down: bfloat16 [8192, 2048], P('tensor'), may hold values from -0.0625 to 0.0625
- cotangent: bfloat16 [8192, 4, 2048], P('dp', None, 'tensor'), may hold values from -6 to 6
Outputs:
- new_streams: bfloat16 [8192, 4, 2048], P('dp', None, 'tensor')
- stream_grad: float32 [8192, 4, 2048], P('dp', None, 'tensor')
- grad_w_query: float32 [2048, 2048], P('dp', 'tensor')
- grad_w_key: float32 [2048, 2048], P('dp', 'tensor')
- grad_w_value: float32 [2048, 2048], P('dp', 'tensor')
- grad_w_output: float32 [2048, 2048], P('tensor', 'dp')
- grad_w_gate: float32 [2048, 8192], P('dp', 'tensor')
- grad_w_up: float32 [2048, 8192], P('dp', 'tensor')
- grad_w_down: float32 [8192, 2048], P('tensor', 'dp')
- grad_mix_in1: float32 [4], replicated
- grad_mix_res1: float32 [4, 4], replicated
- grad_mix_out1: float32 [4], replicated
- grad_mix_in2: float32 [4], replicated
- grad_mix_res2: float32 [4, 4], replicated
- grad_mix_out2: float32 [4], replicated
Inputs may be any that keep to these rules, and one draw needn't show every extreme that they name: `segments`: within each sequence of 1024 tokens the document numbers never fall, start at 0 and end at 3; every document has at least one token and at most 512, and in every sequence document 1 has exactly 512 tokens. `positions`: each token's place within its document, 0 at the document's first token.
All inputs are finite; a program needn't handle non-finite values.
Results may differ from a plain program's by a relative error of at most 0.025.
Values may be sent and summed in bfloat16 or wider, within the bound.
A program may use at most 320 MiB of HBM per device.

v0:
```python
import jax
import jax.numpy as jnp
from jax import lax
from jax.sharding import PartitionSpec as P

HEAD = 128
LENGTH = 1024
WINDOW = 1024


EPS = 1e-05
PRECISE = lax.Precision.HIGHEST
MASKED = -1e30


def contract_rows(left, right):
    return lax.dot_general(
        left, right, (((0,), (0,)), ((), ())), preferred_element_type=jnp.float32
    )


def times_transposed(left, right):
    return lax.dot_general(
        left, right, (((1,), (1,)), ((), ())), preferred_element_type=jnp.float32
    )


def normalize(field):
    average = jnp.mean(field, axis=-1, keepdims=True)
    centered = field - average
    variance = jnp.mean(centered * centered, axis=-1, keepdims=True)
    scaling = lax.rsqrt(variance + EPS)
    return (centered * scaling, scaling)


def norm_back(grad_field, standard, scaling):
    first = jnp.mean(grad_field, axis=-1, keepdims=True)
    second = jnp.mean(grad_field * standard, axis=-1, keepdims=True)
    return scaling * (grad_field - first - standard * second)


def rotary_tables(positions):
    half_size = HEAD // 2
    inverse = 1.0 / 10000.0 ** (jnp.arange(half_size, dtype=jnp.float32) * 2.0 / HEAD)
    angles = positions.astype(jnp.float32)[:, None] * inverse[None, :]
    cos_table = jnp.concatenate([jnp.cos(angles), jnp.cos(angles)], axis=-1)[:, None, :]
    sin_table = jnp.concatenate([jnp.sin(angles), jnp.sin(angles)], axis=-1)[:, None, :]
    return (cos_table, sin_table)


def rotate_forward(field, cos_table, sin_table):
    half_size = HEAD // 2
    pieces = field.reshape(field.shape[0], -1, HEAD)
    turned = jnp.concatenate([-pieces[..., half_size:], pieces[..., :half_size]], axis=-1)
    return (pieces * cos_table + turned * sin_table).reshape(field.shape)


def rotate_backward(grad_field, cos_table, sin_table):
    half_size = HEAD // 2
    pieces = grad_field.reshape(grad_field.shape[0], -1, HEAD)
    scaled = pieces * sin_table
    turned = jnp.concatenate([scaled[..., half_size:], -scaled[..., :half_size]], axis=-1)
    return (pieces * cos_table + turned).reshape(grad_field.shape)


def masked_scores(queries, keys_rot, segment):
    length = queries.shape[0]
    scores = jnp.einsum(
        "qhe,khe->hqk", queries, keys_rot, preferred_element_type=jnp.float32
    ) * HEAD ** (-0.5)
    places = jnp.arange(length)
    allowed = (places[:, None] >= places[None, :]) & (places[:, None] - places[None, :] < WINDOW)
    allowed = allowed & (segment[:, None] == segment[None, :])
    return jnp.where(allowed[None], scores, MASKED)


def attend_forward(inputs):
    queries, keys_rot, values, segment = inputs
    scores = masked_scores(queries, keys_rot, segment)
    row_max = jnp.max(scores, axis=-1, keepdims=True)
    raised = jnp.exp(scores - row_max)
    row_total = jnp.sum(raised, axis=-1, keepdims=True)
    prob_rows = (raised / row_total).astype(jnp.bfloat16)
    mixture = jnp.einsum("hqk,khe->qhe", prob_rows, values, preferred_element_type=jnp.float32)
    return (mixture.astype(jnp.bfloat16), row_max + jnp.log(row_total))


def attend_backward(inputs):
    queries, keys_rot, values, segment, log_total, grad_mix = inputs
    scores = masked_scores(queries, keys_rot, segment)
    prob_full = jnp.exp(scores - log_total)
    grad_probs = jnp.einsum("qhe,khe->hqk", grad_mix, values, preferred_element_type=jnp.float32)
    centre = jnp.sum(prob_full * grad_probs, axis=-1, keepdims=True)
    grad_scores = (prob_full * (grad_probs - centre)).astype(jnp.bfloat16)
    grad_values = jnp.einsum(
        "hqk,qhe->khe", prob_full.astype(jnp.bfloat16), grad_mix, preferred_element_type=jnp.float32
    )
    factor = HEAD ** (-0.5)
    grad_queries = (
        jnp.einsum("hqk,khe->qhe", grad_scores, keys_rot, preferred_element_type=jnp.float32)
        * factor
    )
    grad_keys = (
        jnp.einsum("hqk,qhe->khe", grad_scores, queries, preferred_element_type=jnp.float32)
        * factor
    )
    return (grad_queries, grad_keys, grad_values)


def on_device(
    streams,
    segments,
    positions,
    mix_in1,
    mix_res1,
    mix_out1,
    mix_in2,
    mix_res2,
    mix_out2,
    w_query,
    w_key,
    w_value,
    w_output,
    w_gate,
    w_up,
    w_down,
    cotangent,
):
    tokens, stream_count, slice_width = streams.shape
    seq_count = tokens // LENGTH
    heads_here = w_query.shape[1] // HEAD
    offset = lax.axis_index("tensor") * slice_width
    widened = streams.astype(jnp.float32)
    cos_table, sin_table = rotary_tables(positions)
    seg_rows = segments.reshape(seq_count, LENGTH)

    def by_sequence(field):
        return field.reshape(seq_count, LENGTH, heads_here, HEAD)

    entry1 = jnp.einsum("i,tid->td", mix_in1, widened, precision=PRECISE)
    whole1 = lax.all_gather(entry1, "tensor", axis=1, tiled=True)
    stand1, scale1 = normalize(whole1)
    normed1 = stand1.astype(jnp.bfloat16)
    queries = rotate_forward(
        jnp.dot(normed1, w_query, preferred_element_type=jnp.float32), cos_table, sin_table
    ).astype(jnp.bfloat16)
    keys_rot = rotate_forward(
        jnp.dot(normed1, w_key, preferred_element_type=jnp.float32), cos_table, sin_table
    ).astype(jnp.bfloat16)
    values = jnp.dot(normed1, w_value, preferred_element_type=jnp.float32).astype(jnp.bfloat16)
    attended, log_total = lax.map(
        attend_forward, (by_sequence(queries), by_sequence(keys_rot), by_sequence(values), seg_rows)
    )
    attended = attended.reshape(tokens, heads_here * HEAD)
    branch1 = lax.psum_scatter(
        jnp.dot(attended, w_output, preferred_element_type=jnp.float32),
        "tensor",
        scatter_dimension=1,
        tiled=True,
    )
    middle = (
        jnp.einsum("ij,tid->tjd", mix_res1, widened, precision=PRECISE)
        + mix_out1[None, :, None] * branch1[:, None, :]
    )
    entry2 = jnp.einsum("i,tid->td", mix_in2, middle, precision=PRECISE)
    whole2 = lax.all_gather(entry2, "tensor", axis=1, tiled=True)
    stand2, scale2 = normalize(whole2)
    normed2 = stand2.astype(jnp.bfloat16)
    gate_pre = jnp.dot(normed2, w_gate, preferred_element_type=jnp.float32)
    up_pre = jnp.dot(normed2, w_up, preferred_element_type=jnp.float32)
    activated = jax.nn.silu(gate_pre)
    hidden = (activated * up_pre).astype(jnp.bfloat16)
    branch2 = lax.psum_scatter(
        jnp.dot(hidden, w_down, preferred_element_type=jnp.float32),
        "tensor",
        scatter_dimension=1,
        tiled=True,
    )
    result = (
        jnp.einsum("ij,tid->tjd", mix_res2, middle, precision=PRECISE)
        + mix_out2[None, :, None] * branch2[:, None, :]
    )
    new_streams = result.astype(jnp.bfloat16)
    cot_full = cotangent.astype(jnp.float32)
    branch2_grad_here = jnp.einsum("j,tjd->td", mix_out2, cot_full, precision=PRECISE).astype(
        jnp.bfloat16
    )
    grad_branch2 = lax.all_gather(branch2_grad_here, "tensor", axis=1, tiled=True)
    grad_mix_out2 = jnp.einsum("tjd,td->j", cot_full, branch2, precision=PRECISE)
    grad_mix_res2 = jnp.einsum("tid,tjd->ij", middle, cot_full, precision=PRECISE)
    grad_w_down = contract_rows(hidden, grad_branch2)
    grad_hidden = times_transposed(grad_branch2, w_down)
    sig_gate = jax.nn.sigmoid(gate_pre)
    grad_gate_act = (grad_hidden * up_pre * sig_gate * (1.0 + gate_pre * (1.0 - sig_gate))).astype(
        jnp.bfloat16
    )
    grad_up_act = (grad_hidden * activated).astype(jnp.bfloat16)
    grad_w_gate = contract_rows(normed2, grad_gate_act)
    grad_w_up = contract_rows(normed2, grad_up_act)
    partial2 = times_transposed(grad_gate_act, w_gate) + times_transposed(grad_up_act, w_up)
    grad_normed2 = lax.psum(partial2, "tensor")
    grad_entry2 = lax.dynamic_slice_in_dim(
        norm_back(grad_normed2, stand2, scale2), offset, slice_width, 1
    )
    grad_mix_in2 = jnp.einsum("tid,td->i", middle, grad_entry2, precision=PRECISE)
    grad_middle = (
        jnp.einsum("ij,tjd->tid", mix_res2, cot_full, precision=PRECISE)
        + mix_in2[None, :, None] * grad_entry2[:, None, :]
    )
    branch1_grad_here = jnp.einsum("j,tjd->td", mix_out1, grad_middle, precision=PRECISE).astype(
        jnp.bfloat16
    )
    grad_branch1 = lax.all_gather(branch1_grad_here, "tensor", axis=1, tiled=True)
    grad_mix_out1 = jnp.einsum("tjd,td->j", grad_middle, branch1, precision=PRECISE)
    grad_mix_res1 = jnp.einsum("tid,tjd->ij", widened, grad_middle, precision=PRECISE)
    grad_w_output = contract_rows(attended, grad_branch1)
    grad_attended = times_transposed(grad_branch1, w_output).astype(jnp.bfloat16)
    grad_queries, grad_keys, grad_values = lax.map(
        attend_backward,
        (
            by_sequence(queries),
            by_sequence(keys_rot),
            by_sequence(values),
            seg_rows,
            log_total,
            by_sequence(grad_attended),
        ),
    )
    width_here = heads_here * HEAD
    grad_query_lin = rotate_backward(
        grad_queries.reshape(tokens, width_here), cos_table, sin_table
    ).astype(jnp.bfloat16)
    grad_key_lin = rotate_backward(
        grad_keys.reshape(tokens, width_here), cos_table, sin_table
    ).astype(jnp.bfloat16)
    grad_value_lin = grad_values.reshape(tokens, width_here).astype(jnp.bfloat16)
    grad_w_query = contract_rows(normed1, grad_query_lin)
    grad_w_key = contract_rows(normed1, grad_key_lin)
    grad_w_value = contract_rows(normed1, grad_value_lin)
    partial1 = (
        times_transposed(grad_query_lin, w_query)
        + times_transposed(grad_key_lin, w_key)
        + times_transposed(grad_value_lin, w_value)
    )
    grad_normed1 = lax.psum(partial1, "tensor")
    grad_entry1 = lax.dynamic_slice_in_dim(
        norm_back(grad_normed1, stand1, scale1), offset, slice_width, 1
    )
    grad_mix_in1 = jnp.einsum("tid,td->i", widened, grad_entry1, precision=PRECISE)
    stream_grad = (
        jnp.einsum("ij,tjd->tid", mix_res1, grad_middle, precision=PRECISE)
        + mix_in1[None, :, None] * grad_entry1[:, None, :]
    )
    summed = (
        lax.psum_scatter(grad_w_query, "dp", scatter_dimension=0, tiled=True),
        lax.psum_scatter(grad_w_key, "dp", scatter_dimension=0, tiled=True),
        lax.psum_scatter(grad_w_value, "dp", scatter_dimension=0, tiled=True),
        lax.psum_scatter(grad_w_output, "dp", scatter_dimension=1, tiled=True),
        lax.psum_scatter(grad_w_gate, "dp", scatter_dimension=0, tiled=True),
        lax.psum_scatter(grad_w_up, "dp", scatter_dimension=0, tiled=True),
        lax.psum_scatter(grad_w_down, "dp", scatter_dimension=1, tiled=True),
    )
    mixing = lax.psum(
        (grad_mix_in1, grad_mix_res1, grad_mix_out1, grad_mix_in2, grad_mix_res2, grad_mix_out2),
        ("dp", "tensor"),
    )
    return (
        new_streams,
        stream_grad,
        summed[0],
        summed[1],
        summed[2],
        summed[3],
        summed[4],
        summed[5],
        summed[6],
        mixing[0],
        mixing[1],
        mixing[2],
        mixing[3],
        mixing[4],
        mixing[5],
    )


def solution(mesh):
    return jax.shard_map(
        on_device,
        mesh=mesh,
        in_specs=(
            P("dp", None, "tensor"),
            P("dp"),
            P("dp"),
            P(),
            P(),
            P(),
            P(),
            P(),
            P(),
            P(None, "tensor"),
            P(None, "tensor"),
            P(None, "tensor"),
            P("tensor", None),
            P(None, "tensor"),
            P(None, "tensor"),
            P("tensor", None),
            P("dp", None, "tensor"),
        ),
        out_specs=(
            P("dp", None, "tensor"),
            P("dp", None, "tensor"),
            P("dp", "tensor"),
            P("dp", "tensor"),
            P("dp", "tensor"),
            P("tensor", "dp"),
            P("dp", "tensor"),
            P("dp", "tensor"),
            P("tensor", "dp"),
            P(),
            P(),
            P(),
            P(),
            P(),
            P(),
        ),
        check_vma=False,
    )
```

profile of v0, /device:TPU:0, one launch (start us, length us, event | category | flops | bytes accessed | tf_op | source)
XLA Modules:
  0.0 1718.4 jit_solution(10170171127055385760)
XLA Ops:
  7.2 8.6 fusion.54
  22.6 85.3 %all-gather.5.cloned.1.call-done = f32[1024,2048]{1,0:T(8,128)} async-done(((f32[1024,512]{1,0:T(8,128)}), f32[1024,2048]{1,0:T(8,128)}) %all-gather.5.cloned.1.call-update) | async-done | bytes 8388624 | tf_op jit(solution)/shard_map/all_gather | solution.py:141
  132.8 8.0 fusion.62
  140.7 8.0 fusion
  148.8 7.6 fusion.28
  163.2 86.5 %reduce-scatter.10.cloned.1.call-done = f32[1024,512]{1,0:T(8,128)} async-done(((f32[1024,2048]{1,0:T(8,128)}), f32[1024,512]{1,0:T(8,128)}) %reduce-scatter.10.cloned.1.call-update) | async-done | bytes 2097168 | tf_op jit(solution)/shard_map/reduce_scatter | solution.py:155
  249.7 10.2 bitcast_add_fusion.3
  259.9 14.9 fusion.50
  276.4 8.5 fusion.52
  286.2 77.8 %all-gather.7.cloned.1.call-done = f32[1024,2048]{1,0:T(8,128)} async-done(((f32[1024,512]{1,0:T(8,128)}), f32[1024,2048]{1,0:T(8,128)}) %all-gather.7.cloned.1.call-update) | async-done | bytes 8388624 | tf_op jit(solution)/shard_map/all_gather | solution.py:166
  378.2 14.8 fusion.67
  393.0 11.0 fusion.66
  404.0 15.1 all-gather.9.cloned.1.call-done
  419.0 21.9 %multiply_convert_fusion.1 = (bf16[1024,2048]{1,0:T(8,128)(2,1)}, bf16[1024,2048]{1,0:T(8,128)(2,1)}, bf16[1024,2048]{1,0:T(8,128)(2,1)}) fusion(f32[1024,2048]{1,0:T(8,128)} %fusion.66, f32[1024,2048]{1,0:T(8,128)} %fusion.67, bf16[1024,2048]{1,0:T(8,128)(2,1)} %all-gather.9.cloned.1.call-done, bf16[2048,2048]{1,0:T(8,128)(2,1)} %param.32), kind=kOutput, calls=%fused_computation.18 | convolution fusion | flops 8621391872 | bytes 41943040 | tf_op jit(solution)/shard_map/dot_general | solution.py:23
  440.9 13.1 fusion.69
  454.1 13.5 convolution_add_fusion
  467.6 172.2 %all-reduce.4.cloned.1.call-done = f32[1024,2048]{1,0:T(8,128)} async-done(((f32[1024,2048]{1,0:T(8,128)}), f32[1024,2048]{1,0:T(8,128)}) %all-reduce.4.cloned.1.call-update) | async-done | bytes 8388624 | tf_op jit(solution)/shard_map/psum | solution.py:201
  639.9 7.0 fusion.57
  649.7 10.9 bitcast_add_fusion.1
  660.5 15.0 fusion.48
  676.8 14.7 fusion.68
  692.3 37.9 %all-gather.11.cloned.1.call-done = bf16[1024,2048]{1,0:T(8,128)(2,1)} async-done(((bf16[1024,512]{1,0:T(8,128)(2,1)}), bf16[1024,2048]{1,0:T(8,128)(2,1)}) %all-gather.11.cloned.1.call-update) | async-done | bytes 4194320 | tf_op jit(solution)/shard_map/all_gather | solution.py:213
  734.8 11.9 multiply_reduce_fusion
  746.7 13.3 multiply_convert_fusion
  775.4 9.3 fusion.29
  784.7 9.9 add_add_fusion
  795.8 6.6 fusion.76
  802.5 6.8 fusion.75
  810.4 6.6 fusion.74
  818.3 6.7 fusion.73
  825.1 15.4 fusion.79
  840.5 15.2 fusion.78
  855.8 15.6 fusion.77
  871.5 21.1 %convolution_bitcast_fusion = f32[4,4]{1,0:T(4,128)S(1)} fusion(f32[1024,4,512]{2,1,0:T(4,128)} %copy-done.2, bf16[1024,4,512]{2,1,0:T(4,128)(2,1)} %param.33), kind=kOutput, calls=%fused_computation.73 | convolution fusion | flops 100663296 | bytes 12582976 | tf_op jit(solution)/shard_map/tid,tjd->ij/dot_general | solution.py:190
  892.6 42.3 %fusion.41 = f32[4]{0:T(128)S(1)} fusion(f32[1024,4,512]{2,1,0:T(4,128)} %copy-done.2, f32[1024,512,1]{1,0,2:T(8,128)S(1)} %bitcast.179), kind=kOutput, calls=%fused_computation.78 | convolution fusion | flops 25165824 | bytes 10485776 | tf_op jit(solution)/shard_map/tid,td->i/dot_general | solution.py:205
  934.9 42.3 %fusion.38 = f32[4]{0:T(128)S(1)} fusion(f32[1024,4,512]{2,1,0:T(4,128)} %copy-done.3, f32[1024,512,1]{1,0,2:T(8,128)S(1)} %bitcast.194), kind=kOutput, calls=%fused_computation.77 | convolution fusion | flops 25165824 | bytes 10485776 | tf_op jit(solution)/shard_map/tjd,td->j/dot_general | solution.py:214
  977.3 18.8 %convolution_bitcast_fusion.1 = f32[4,4]{0,1:T(4,128)S(1)} fusion(f32[1024,4,512]{2,1,0:T(4,128)S(1)} %bitcast.174, bf16[1024,4,512]{2,1,0:T(4,128)(2,1)S(1)} %copy-done.14), kind=kOutput, calls=%fused_computation.74 | convolution fusion | flops 100663296 | bytes 12582976 | tf_op jit(solution)/shard_map/tid,tjd->ij/dot_general | solution.py:215
  996.0 22.0 %fusion.35 = f32[4]{0:T(128)S(1)} fusion(bf16[1024,4,512]{2,1,0:T(4,128)(2,1)} %param.33, f32[1024,512,1]{1,0,2:T(8,128)} %bitcast.187), kind=kOutput, calls=%fused_computation.76 | convolution fusion | flops 25165824 | bytes 6291472 | tf_op jit(solution)/shard_map/tjd,td->j/dot_general | solution.py:189
  1018.0 7.2 fusion.56
  1028.8 18.8 %fusion.32 = f32[4]{0:T(128)S(1)} fusion(bf16[1024,4,512]{2,1,0:T(4,128)(2,1)S(1)} %copy-done.15, f32[1024,512,1]{1,0,2:T(8,128)S(1)} %bitcast.180), kind=kOutput, calls=%fused_computation.75 | convolution fusion | flops 25165824 | bytes 6291472 | tf_op jit(solution)/shard_map/tid,td->i/dot_general | solution.py:249
  1047.7 19.7 %fusion.4 = bf16[1024,4,512]{2,1,0:T(4,128)(2,1)} fusion(f32[1024,4,512]{2,1,0:T(4,128)S(1)} %bitcast.172, f32[1024,512]{1,0:T(8,128)S(1)} %copy-done.13, f32[4]{0:T(128)S(1)} %copy-done.46, f32[4,4]{1,0:T(4,128)S(1)} %copy-done.39), kind=kOutput, calls=%fused_computation.12 | convolution fusion | flops 106954752 | bytes 14680144 | tf_op jit(solution)/shard_map/ij,tid->tjd/dot_general | solution.py:180
  1067.4 40.8 %all-reduce = (f32[4]{0:T(128)}, f32[4,4]{0,1:T(4,128)S(1)}, f32[4]{0:T(128)}, f32[4]{0:T(128)}, f32[4,4]{1,0:T(4,128)}, /*index=5*/f32[4]{0:T(128)}) all-reduce(f32[4]{0:T(128)S(1)} %fusion.32, f32[4,4]{0,1:T(4,128)S(1)} %convolution_bitcast_fusion.1, f32[4]{0:T(128)S(1)} %fusion.38, ...), channel_id=1, replica_groups=mesh['dp'=8,'tensor'=4] {'dp','tensor'}, use_global_device_ids=true, to_apply=%region_22.23 | all-reduce | flops 48 | bytes 384 | tf_op jit(solution)/shard_map/psum | solution.py:263
  1108.9 20.4 %bitcast_add_fusion = f32[1024,4,512]{2,1,0:T(4,128)} fusion(f32[1024,4,512]{2,1,0:T(4,128)} %copy-done.3, f32[1024,512]{1,0:T(8,128)} %copy-done.12, f32[4]{0:T(128)S(1)} %copy-done.47, f32[4,4]{1,0:T(4,128)S(1)} %copy-done.41), kind=kOutput, calls=%fused_computation.9 | convolution fusion | flops 104857600 | bytes 18874448 | tf_op jit(solution)/shard_map/ij,tjd->tid/dot_general | solution.py:251
  1129.3 23.1 %reduce-scatter.16.cloned.1.call-done = f32[256,512]{1,0:T(8,128)} async-done(((f32[2048,512]{1,0:T(8,128)}), f32[256,512]{1,0:T(8,128)}) %reduce-scatter.16.cloned.1.call-update) | async-done | bytes 524304 | tf_op jit(solution)/shard_map/reduce_scatter | solution.py:256
  1152.4 50.9 %reduce-scatter.14.cloned.1.call-done = f32[256,512]{1,0:T(8,128)} async-done(((f32[2048,512]{1,0:T(8,128)}), f32[256,512]{1,0:T(8,128)}) %reduce-scatter.14.cloned.1.call-update) | async-done | bytes 524304 | tf_op jit(solution)/shard_map/reduce_scatter | solution.py:255
  1203.3 169.3 %reduce-scatter.26.cloned.1.call-done = f32[2048,256]{1,0:T(8,128)} async-done(((f32[2048,2048]{1,0:T(8,128)}), f32[2048,256]{1,0:T(8,128)}) %reduce-scatter.26.cloned.1.call-update) | async-done | bytes 2097168 | tf_op jit(solution)/shard_map/reduce_scatter | solution.py:261
  1372.6 169.4 %reduce-scatter.24.cloned.1.call-done = f32[256,2048]{1,0:T(8,128)} async-done(((f32[2048,2048]{1,0:T(8,128)}), f32[256,2048]{1,0:T(8,128)}) %reduce-scatter.24.cloned.1.call-update) | async-done | bytes 2097168 | tf_op jit(solution)/shard_map/reduce_scatter | solution.py:260
  1542.0 169.4 %reduce-scatter.22.cloned.1.call-done = f32[256,2048]{1,0:T(8,128)} async-done(((f32[2048,2048]{1,0:T(8,128)}), f32[256,2048]{1,0:T(8,128)}) %reduce-scatter.22.cloned.1.call-update) | async-done | bytes 2097168 | tf_op jit(solution)/shard_map/reduce_scatter | solution.py:259
  (202 shorter events, 88.3 us)
Async XLA Ops:
  7.2 150.2 %copy-start = (bf16[512,2048]{1,0:T(8,128)(2,1)S(1)}, bf16[512,2048]{1,0:T(8,128)(2,1)}, u32[]{:S(2)}) copy-start(bf16[512,2048]{1,0:T(8,128)(2,1)} %param.29) | copy-start | bytes 6291460
  7.2 100.6 %all-gather.5.cloned.1.call-start = ((), (), s32[]{:S(2)}) async-start(), calls=%async_computation.9 | async-start | bytes 10485760 | tf_op jit(solution)/shard_map/all_gather | solution.py:141
  17.4 232.3 %reduce-scatter.10.cloned.1.call-start = ((), (), s32[]{:S(2)}) async-start(), calls=%async_computation.10 | async-start | bytes 10485760 | tf_op jit(solution)/shard_map/reduce_scatter | solution.py:155
  124.6 24.2 %copy-start.18 = (bf16[1024,512]{0,1:T(8,128)(2,1)}, bf16[1024,512]{0,1:T(8,128)(2,1)S(1)}, u32[]{:S(2)}) copy-start(bf16[1024,512]{0,1:T(8,128)(2,1)S(1)} %convolution_convert_fusion.1) | copy-start | bytes 3145732
  132.7 8.0 copy-start.6
  132.7 8.0 copy-start.8
  140.7 8.0 copy-start.31
  148.8 7.6 copy-start.33
  163.1 86.6 %copy-start.40 = (f32[4,4]{1,0:T(4,128)S(1)}, f32[4,4]{1,0:T(4,128)}, u32[]{:S(2)}) copy-start(f32[4,4]{1,0:T(4,128)} %param.21) | copy-start | bytes 196
  163.1 86.6 %copy-start.44 = (f32[4]{0:T(128)S(1)}, f32[4]{0:T(128)}, u32[]{:S(2)}) copy-start(f32[4]{0:T(128)} %param.22) | copy-start | bytes 52
  163.1 96.7 %copy-start.43 = (f32[4]{0:T(128)S(1)}, f32[4]{0:T(128)}, u32[]{:S(2)}) copy-start(f32[4]{0:T(128)} %param.23) | copy-start | bytes 52
  163.1 200.9 %all-gather.7.cloned.1.call-start = ((), (), s32[]{:S(2)}) async-start(), calls=%async_computation.11 | async-start | bytes 10485760 | tf_op jit(solution)/shard_map/all_gather | solution.py:166
  259.8 14.9 copy-start.2
  276.3 142.8 %all-gather.9.cloned.1.call-start = ((), (), s32[]{:S(2)}) async-start(), calls=%async_computation.13 | async-start | bytes 5242880 | tf_op jit(solution)/shard_map/all_gather | solution.py:188
  286.2 353.7 %all-reduce.4.cloned.1.call-start = ((), (), s32[]{:S(2)}) async-start(), calls=%async_computation.14 | async-start | bytes 16777216 | tf_op jit(solution)/shard_map/psum | solution.py:201
  373.9 19.0 %slice-start.4 = ((s8[8388608]{0:T(1024)(128)(4,1)}), s8[4194304]{0:T(1024)(128)(4,1)S(1)}, s32[]{:S(2)}) async-start(s8[8388608]{0:T(1024)(128)(4,1)} %bitcast.199), calls=%async_computation.28 | async-start | bytes 8388608
  378.2 14.8 copy-start.17
  378.2 14.8 slice-start.5
  440.9 13.2 copy-start.54
  467.6 262.6 %all-gather.11.cloned.1.call-start = ((), (), s32[]{:S(2)}) async-start(), calls=%async_computation.15 | async-start | bytes 5242880 | tf_op jit(solution)/shard_map/all_gather | solution.py:213
  649.6 10.9 copy-start.10
  660.5 15.0 copy-start.3
  676.8 319.2 %reduce-scatter.12.cloned.1.call-start = ((), (), s32[]{:S(2)}) async-start(), calls=%async_computation.12 | async-start | bytes 10485760 | tf_op jit(solution)/shard_map/reduce_scatter | solution.py:173
  691.5 326.4 %all-reduce.6.cloned.1.call-start = ((), (), s32[]{:S(2)}) async-start(), calls=%async_computation.16 | async-start | bytes 16777216 | tf_op jit(solution)/shard_map/psum | solution.py:245
  746.7 13.3 copy-start.9
  775.4 9.3 copy-start.21
  794.6 334.6 %reduce-scatter.20.cloned.1.call-start = ((), (), s32[]{:S(2)}) async-start(), calls=%async_computation.20 | async-start | bytes 4718592 | tf_op jit(solution)/shard_map/reduce_scatter | solution.py:258
  802.4 326.9 %reduce-scatter.18.cloned.1.call-start = ((), (), s32[]{:S(2)}) async-start(), calls=%async_computation.19 | async-start | bytes 4718592 | tf_op jit(solution)/shard_map/reduce_scatter | solution.py:257
  809.2 343.1 %reduce-scatter.16.cloned.1.call-start = ((), (), s32[]{:S(2)}) async-start(), calls=%async_computation.18 | async-start | bytes 4718592 | tf_op jit(solution)/shard_map/reduce_scatter | solution.py:256
  817.1 386.2 %reduce-scatter.14.cloned.1.call-start = ((), (), s32[]{:S(2)}) async-start(), calls=%async_computation.17 | async-start | bytes 4718592 | tf_op jit(solution)/shard_map/reduce_scatter | solution.py:255
  825.0 547.6 %reduce-scatter.26.cloned.1.call-start = ((), (), s32[]{:S(2)}) async-start(), calls=%async_computation.23 | async-start | bytes 18874368 | tf_op jit(solution)/shard_map/reduce_scatter | solution.py:261
  840.5 701.5 %reduce-scatter.24.cloned.1.call-start = ((), (), s32[]{:S(2)}) async-start(), calls=%async_computation.22 | async-start | bytes 18874368 | tf_op jit(solution)/shard_map/reduce_scatter | solution.py:260
  855.8 855.6 %reduce-scatter.22.cloned.1.call-start = ((), (), s32[]{:S(2)}) async-start(), calls=%async_computation.21 | async-start | bytes 18874368 | tf_op jit(solution)/shard_map/reduce_scatter | solution.py:259
  871.5 21.2 %copy-start.11 = (f32[1024,512]{1,0:T(8,128)S(1)}, f32[1024,512]{1,0:T(8,128)}, u32[]{:S(2)}) copy-start(f32[1024,512]{1,0:T(8,128)} %copy-done.10) | copy-start | bytes 6291460
  892.6 42.3 %copy-start.22 = (f32[1024,512]{1,0:T(8,128)S(1)}, f32[1024,512]{1,0:T(8,128)}, u32[]{:S(2)}) copy-start(f32[1024,512]{1,0:T(8,128)} %reduce-scatter.10.cloned.1.call-done) | copy-start | bytes 6291460
  892.6 84.6 %slice-start.2 = ((s8[8388608]{0:T(1024)(128)(4,1)}), s8[4194304]{0:T(1024)(128)(4,1)S(1)}, s32[]{:S(2)}) async-start(s8[8388608]{0:T(1024)(128)(4,1)} %bitcast.173), calls=%async_computation.26 | async-start | bytes 8388608
  934.9 42.3 %slice-start.3 = ((s8[8388608]{0:T(1024)(128)(4,1)}), s8[4194304]{0:T(1024)(128)(4,1)S(1)}, s32[]{:S(2)}) async-start(s8[8388608]{0:T(1024)(128)(4,1)} %bitcast.173), calls=%async_computation.27 | async-start | bytes 8388608
  934.9 42.3 %copy-start.14 = (bf16[1024,4,512]{2,1,0:T(4,128)(2,1)S(1)}, bf16[1024,4,512]{2,1,0:T(4,128)(2,1)}, u32[]{:S(2)}) copy-start(bf16[1024,4,512]{2,1,0:T(4,128)(2,1)} %param.17) | copy-start | bytes 12582916
  1018.0 7.3 copy-start.36
  1025.3 22.3 %slice-start = ((s8[8388608]{0:T(1024)(128)(4,1)}), s8[4194304]{0:T(1024)(128)(4,1)S(1)}, s32[]{:S(2)}) async-start(s8[8388608]{0:T(1024)(128)(4,1)} %bitcast.171), calls=%async_computation.24 | async-start | bytes 8388608
  1028.2 19.4 %copy-start.12 = (f32[1024,512]{1,0:T(8,128)}, f32[1024,512]{1,0:T(8,128)S(1)}, u32[]{:S(2)}) copy-start(f32[1024,512]{1,0:T(8,128)S(1)} %fusion.15) | copy-start | bytes 6291460
  1028.8 18.8 %slice-start.1 = ((s8[8388608]{0:T(1024)(128)(4,1)}), s8[4194304]{0:T(1024)(128)(4,1)S(1)}, s32[]{:S(2)}) async-start(s8[8388608]{0:T(1024)(128)(4,1)} %bitcast.171), calls=%async_computation.25 | async-start | bytes 8388608
  1028.8 18.8 %copy-start.13 = (f32[1024,512]{1,0:T(8,128)S(1)}, f32[1024,512]{1,0:T(8,128)}, u32[]{:S(2)}) copy-start(f32[1024,512]{1,0:T(8,128)} %reduce-scatter.12.cloned.1.call-done) | copy-start | bytes 6291460
  1028.8 18.9 %copy-start.39 = (f32[4,4]{1,0:T(4,128)S(1)}, f32[4,4]{1,0:T(4,128)}, u32[]{:S(2)}) copy-start(f32[4,4]{1,0:T(4,128)} %param.24) | copy-start | bytes 196
  1028.8 18.9 %copy-start.46 = (f32[4]{0:T(128)S(1)}, f32[4]{0:T(128)}, u32[]{:S(2)}) copy-start(f32[4]{0:T(128)} %param.25) | copy-start | bytes 52
  1047.7 61.2 %copy-start.41 = (f32[4,4]{1,0:T(4,128)S(1)}, f32[4,4]{1,0:T(4,128)}, u32[]{:S(2)}) copy-start(f32[4,4]{1,0:T(4,128)} %param.21) | copy-start | bytes 196
  1047.7 61.2 %copy-start.47 = (f32[4]{0:T(128)S(1)}, f32[4]{0:T(128)}, u32[]{:S(2)}) copy-start(f32[4]{0:T(128)} %param.20) | copy-start | bytes 52
  1108.9 602.6 %copy-start.1 = (bf16[512,2048]{1,0:T(8,128)(2,1)S(1)}, bf16[512,2048]{1,0:T(8,128)(2,1)}, u32[]{:S(2)}) copy-start(bf16[512,2048]{1,0:T(8,128)(2,1)} %param.29) | copy-start | bytes 6291460
  (28 other events, 72.1 us)
Sparse Core Ops, SparseCore 0:
  17.5 90.2 all-gather.4
  163.2 86.3 reduce-scatter.9
  276.4 87.5 all-gather.6
  366.4 52.5 all-gather.8
  467.7 172.1 all-reduce.3
  676.9 53.2 all-gather.10
  733.3 86.3 reduce-scatter.11
  823.6 172.0 all-reduce.5
  998.6 50.6 reduce-scatter.19
  1052.1 49.1 reduce-scatter.17
  1104.1 48.2 reduce-scatter.15
  1155.1 48.1 reduce-scatter.13
  1206.2 166.3 reduce-scatter.25
  1375.4 166.6 reduce-scatter.23
  1544.8 166.5 reduce-scatter.21
where the time goes:
time: 1720 us
  waiting for transfers between devices  1060 us (62%)
  matrix products  512 us (30%)
  other arithmetic  75.2 us (4%)
  blocking collectives  40.8 us (2%)
  local copies, waits for them, and re-layouts  17.8 us (1%)
    psum x1, waiting for transfers between devices, on_device(): grad_normed2 = lax.psum(partial2, 'tensor')  172 us
    reduce_scatter x1, waiting for transfers between devices, on_device(): lax.psum_scatter(grad_w_up, 'dp', scatter_dimension=0, tiled=True)  169 us
    reduce_scatter x1, waiting for transfers between devices, on_device(): lax.psum_scatter(grad_w_gate, 'dp', scatter_dimension=0, tiled=True)  169 us
    reduce_scatter x1, waiting for transfers between devices, on_device(): lax.psum_scatter(grad_w_down, 'dp', scatter_dimension=1, tiled=True)  169 us
    reduce_scatter x1, waiting for transfers between devices, on_device(): lax.psum_scatter(jnp.dot(attended, w_output, preferred_element_type=jnp.f...  86.5 us
    all_gather x1, waiting for transfers between devices, on_device(): whole1 = lax.all_gather(entry1, 'tensor', axis=1, tiled=True)  85.3 us
    all_gather x1, waiting for transfers between devices, on_device(): whole2 = lax.all_gather(entry2, 'tensor', axis=1, tiled=True)  77.8 us
    dot_general x7, matrix products, contract_rows(): lax.dot_general(left, right, (((0,), (0,)), ((), ())), preferred_element_...  72.9 us
  transfers between devices with their start and end apart: 15, of which 11 were waited for; matrix products, arithmetic and copies ran while one was open for 24% of the time, Pallas kernels for 0%

commit v1 on v0

v1 whole, which is shorter than its diff:
```python
import functools

import jax
import jax.numpy as jnp
from jax import lax
from jax.experimental import pallas as pl
from jax.experimental.pallas import tpu as pltpu
from jax.sharding import PartitionSpec as P

HEAD = 128
LENGTH = 1024
LONGEST = 512
EPS = 1e-05
PRECISE = lax.Precision.HIGHEST
MASKED = -1e30
MESH = pl.DeviceIdType.MESH
BF16 = jnp.bfloat16
F32 = jnp.float32
CHUNK = 256
ROWS = 32
MIB = 1 << 20

IN1, OUT2, ENTRY, ENTRY_B, BRANCH, BRANCH_E, MIXED = 0, 4, 8, 12, 13, 17, 18


def contract_rows(left, right):
    return lax.dot_general(
        left, right, (((0,), (0,)), ((), ())), preferred_element_type=F32
    )


def dot_nn(left, right):
    return jnp.dot(left, right, preferred_element_type=F32)


def dot_nt(left, right):
    return lax.dot_general(
        left, right, (((1,), (1,)), ((), ())), preferred_element_type=F32
    )


def partners(n):
    me = lax.axis_index("tensor")
    if n == 4:
        both = (me + 1 - 2 * lax.rem(me, 2), lax.rem(me + 2, 4), 3 - me)
        return me, both, both
    to = tuple(lax.rem(me + k, n) for k in range(1, n))
    source = tuple(lax.rem(me + n - k, n) for k in range(1, n))
    return me, to, source


def enter(n, to):
    barrier = pltpu.get_barrier_semaphore()
    for target in to:
        pl.semaphore_signal(
            barrier, inc=1, device_id={"tensor": target}, device_id_type=MESH
        )
    pl.semaphore_wait(barrier, n - 1)


def remote(source, target, send_sem, recv_sem, device):
    return pltpu.make_async_remote_copy(
        src_ref=source,
        dst_ref=target,
        send_sem=send_sem,
        recv_sem=recv_sem,
        device_id={"tensor": device},
        device_id_type=MESH,
    )


def columns(index, width):
    return pl.ds(pl.multiple_of(index * width, 128), width)


def chunk_rows(c):
    return pl.ds(pl.multiple_of(c * CHUNK, CHUNK), CHUNK)


class Gather:
    def __init__(self, n, buf, width, send_sem, recv_sem):
        self.n, self.buf, self.width = n, buf, width
        self.me, self.to, self.source = partners(n)
        self.send_sem, self.recv_sem = send_sem, recv_sem

    def own(self):
        return columns(self.me, self.width)

    def start(self, c):
        view = self.buf.at[chunk_rows(c), self.own()]
        for k in range(self.n - 1):
            remote(view, view, self.send_sem.at[k, c], self.recv_sem.at[k, c], self.to[k]).start()

    def arrive(self, c):
        for k in range(self.n - 1):
            view = self.buf.at[chunk_rows(c), columns(self.source[k], self.width)]
            remote(view, view, self.send_sem.at[k, c], self.recv_sem.at[k, c], self.to[k]).wait_recv()

    def finish(self, c):
        view = self.buf.at[chunk_rows(c), self.own()]
        for k in range(self.n - 1):
            remote(view, view, self.send_sem.at[k, c], self.recv_sem.at[k, c], self.to[k]).wait_send()


class Scatter:
    def __init__(self, n, part, came, width, send_sem, recv_sem):
        self.n, self.part, self.came, self.width = n, part, came, width
        self.me, self.to, self.source = partners(n)
        self.send_sem, self.recv_sem = send_sem, recv_sem

    def copy(self, c, k):
        return remote(
            self.part.at[chunk_rows(c), columns(self.to[k], self.width)],
            self.came.at[k, chunk_rows(c)],
            self.send_sem.at[k, c],
            self.recv_sem.at[k, c],
            self.to[k],
        )

    def start(self, c):
        for k in range(self.n - 1):
            self.copy(c, k).start()

    def arrive(self, c):
        for k in range(self.n - 1):
            self.copy(c, k).wait_recv()

    def finish(self, c):
        for k in range(self.n - 1):
            self.copy(c, k).wait_send()

    def total(self, rows):
        total = self.part[rows, columns(self.me, self.width)].astype(F32)
        for k in range(self.n - 1):
            total += self.came[k, rows].astype(F32)
        return total


class Stats:
    def __init__(self, n, mine, came, send_sem, recv_sem):
        self.n, self.mine, self.came = n, mine, came
        self.me, self.to, self.source = partners(n)
        self.send_sem, self.recv_sem = send_sem, recv_sem

    def copy(self, c, k):
        return remote(
            self.mine.at[c], self.came.at[k, c], self.send_sem.at[k, c], self.recv_sem.at[k, c], self.to[k]
        )

    start, arrive, finish = Scatter.start, Scatter.arrive, Scatter.finish

    def put(self, c, first, second):
        ones = jnp.ones((8, 128), F32)
        for place, field in ((0, first), (8, second)):
            self.mine[c, place : place + 8] = lax.dot_general(
                ones, field, (((1,), (1,)), ((), ())), precision=PRECISE, preferred_element_type=F32
            )

    def means(self, c, features):
        total = self.mine[c]
        for k in range(self.n - 1):
            total += self.came[k, c]
        share = jnp.full((8, 128), 1.0 / (8 * features), F32)
        return tuple(
            lax.dot_general(
                total[place : place + 8],
                share,
                (((0,), (0,)), ((), ())),
                precision=PRECISE,
                preferred_element_type=F32,
            )
            for place in (0, 8)
        )


def loop(count, body):
    def step(i, carry):
        body(i)
        return carry

    lax.fori_loop(0, count, step, 0)


def sub_rows(c, r):
    return pl.ds(pl.multiple_of(c * CHUNK + r * ROWS, ROWS), ROWS)


def normalize_rows(source, rows, target, target_rows, scale_ref):
    field = source[rows, :].astype(F32)
    features = field.shape[1]
    average = jnp.sum(field, axis=1, keepdims=True) * (1.0 / features)
    centered = field - average
    variance = jnp.sum(centered * centered, axis=1, keepdims=True) * (1.0 / features)
    scaling = lax.rsqrt(variance + EPS)
    target[target_rows, :] = (centered * scaling).astype(BF16)
    scale_ref[rows, :] = jnp.broadcast_to(scaling, (field.shape[0], 128))


def repeat_lanes(field, width):
    return jnp.concatenate([field] * (width // 128), axis=1)


def fold_lanes(field):
    total = field[:, 0:128]
    for j in range(1, field.shape[1] // 128):
        total += field[:, 128 * j : 128 * (j + 1)]
    return total


def rotate(field, cos_rows, sin_rows, sign):
    turned = pltpu.roll(field, HEAD // 2, 1)
    return field * cos_rows + (sign * turned) * sin_rows


def project_kernel(
    n, coef, cos_ref, sin_ref, s_hbm, c_hbm, wq_hbm, wk_hbm, wv_hbm,
    normed_hbm, q_ref, k_ref, v_ref, scale_ref, gb2_hbm,
    s_buf, c_buf, w_buf, all1, all2, normed, in_sem, w_sem, out_sem,
    send1, recv1, send2, recv2,
):
    _, tokens, width = s_buf.shape
    count = tokens // CHUNK
    heads = width // HEAD
    weights = (wq_hbm, wk_hbm, wv_hbm)

    def s_in(c):
        return pltpu.make_async_copy(
            s_hbm.at[:, chunk_rows(c)], s_buf.at[:, chunk_rows(c)], in_sem.at[0, c]
        )

    def c_in(c):
        return pltpu.make_async_copy(
            c_hbm.at[:, chunk_rows(c)], c_buf.at[:, chunk_rows(c)], in_sem.at[1, c]
        )

    def w_in(j):
        return pltpu.make_async_copy(weights[j], w_buf.at[j], w_sem.at[j])

    def normed_out(c):
        return pltpu.make_async_copy(
            normed.at[chunk_rows(c)], normed_hbm.at[chunk_rows(c)], out_sem.at[0, c]
        )

    def gb2_out(c):
        return pltpu.make_async_copy(
            all2.at[chunk_rows(c)], gb2_hbm.at[chunk_rows(c)], out_sem.at[1, c]
        )

    loop(count, lambda c: s_in(c).start())
    for j in range(3):
        w_in(j).start()
    loop(count, lambda c: c_in(c).start())
    first = Gather(n, all1, width, send1, recv1)
    second = Gather(n, all2, width, send2, recv2)
    enter(n, first.to)

    def mix(buf, base, target, gather, c):
        def part(r):
            rows = sub_rows(c, r)
            total = coef[base] * buf[0, rows].astype(F32)
            for i in range(1, buf.shape[0]):
                total += coef[base + i] * buf[i, rows].astype(F32)
            target[rows, gather.own()] = total.astype(BF16)

        loop(CHUNK // ROWS, part)
        gather.start(c)

    def send_first(c):
        s_in(c).wait()
        mix(s_buf, IN1, all1, first, c)

    loop(count, send_first)
    for j in range(3):
        w_in(j).wait()

    def work(c):
        c_in(c).wait()
        mix(c_buf, OUT2, all2, second, c)
        first.arrive(c)
        loop(
            CHUNK // ROWS,
            lambda r: normalize_rows(all1, sub_rows(c, r), normed, sub_rows(c, r), scale_ref),
        )
        normed_out(c).start()
        rows = chunk_rows(c)
        block = normed[rows, :]
        cos_rows, sin_rows = cos_ref[rows, :], sin_ref[rows, :]
        for j, target in ((0, q_ref), (1, k_ref)):
            lin = dot_nn(block, w_buf[j])
            for h in range(heads):
                place = slice(HEAD * h, HEAD * (h + 1))
                target[rows, place] = rotate(lin[:, place], cos_rows, sin_rows, 1.0).astype(BF16)
        v_ref[rows, :] = dot_nn(block, w_buf[2]).astype(BF16)

    loop(count, work)

    def end(c):
        second.arrive(c)
        gb2_out(c).start()

    loop(count, end)

    def drain(c):
        gb2_out(c).wait()
        normed_out(c).wait()
        first.finish(c)
        second.finish(c)

    loop(count, drain)


def window_bias(c, start, extent, segc_ref, segr_ref, bias):
    def part(r):
        rows = pl.ds(pl.multiple_of(r * ROWS, ROWS), ROWS)
        row = c * CHUNK + r * ROWS + lax.broadcasted_iota(jnp.int32, (ROWS, extent), 0)
        column = start + lax.broadcasted_iota(jnp.int32, (ROWS, extent), 1)
        same = segc_ref[sub_rows(c, r), 0:1] == segr_ref[0:1, pl.ds(start, extent)]
        bias[rows, :] = jnp.where((row >= column) & same, 0.0, MASKED)

    loop(CHUNK // ROWS, part)


def window(c, tokens):
    extent = min(tokens, CHUNK * (-(-(LONGEST - 1) // CHUNK) + 1))
    back = extent // CHUNK - 1
    return pl.multiple_of(jnp.maximum(c - back, 0) * CHUNK, CHUNK), extent


def attend_kernel(
    n, coef, q_ref, k_ref, v_ref, segc_ref, segr_ref, wo_ref, s_hbm,
    attended_ref, branch_ref, normed_hbm, scale_ref,
    s_buf, part, came, all2, normed, bias, in_sem, out_sem, send1, recv1, send2, recv2,
):
    tokens, width = q_ref.shape
    count = tokens // CHUNK
    heads = width // HEAD
    s_in = pltpu.make_async_copy(s_hbm, s_buf, in_sem)
    s_in.start()
    scatter = Scatter(n, part, came, width, send1, recv1)
    gather = Gather(n, all2, width, send2, recv2)
    enter(n, gather.to)

    def attend(c):
        rows = chunk_rows(c)
        start, extent = window(c, tokens)
        window_bias(c, start, extent, segc_ref, segr_ref, bias)
        for h in range(heads):
            place = slice(HEAD * h, HEAD * (h + 1))
            scores = dot_nt(q_ref[rows, place], k_ref[pl.ds(start, extent), place])
            scores = scores * HEAD ** (-0.5) + bias[...]
            raised = jnp.exp(scores - jnp.max(scores, axis=1, keepdims=True))
            inverse = 1.0 / jnp.sum(raised, axis=1, keepdims=True)
            probs = (raised * inverse).astype(BF16)
            attended_ref[rows, place] = dot_nn(probs, v_ref[pl.ds(start, extent), place]).astype(BF16)
        part[rows, :] = dot_nn(attended_ref[rows, :], wo_ref[...]).astype(BF16)
        scatter.start(c)

    loop(count, attend)
    s_in.wait()

    def middle(c):
        scatter.arrive(c)

        def piece(r):
            rows = sub_rows(c, r)
            branch = scatter.total(rows)
            branch_ref[rows, :] = branch
            entry = coef[ENTRY_B] * branch
            for i in range(s_buf.shape[0]):
                entry += coef[ENTRY + i] * s_buf[i, rows].astype(F32)
            all2[rows, gather.own()] = entry.astype(BF16)

        loop(CHUNK // ROWS, piece)
        gather.start(c)

    loop(count, middle)

    def normed_out(c):
        return pltpu.make_async_copy(
            normed.at[chunk_rows(c)], normed_hbm.at[chunk_rows(c)], out_sem.at[c]
        )

    def last(c):
        gather.arrive(c)
        loop(
            CHUNK // ROWS,
            lambda r: normalize_rows(all2, sub_rows(c, r), normed, sub_rows(c, r), scale_ref),
        )
        normed_out(c).start()

    loop(count, last)

    def drain(c):
        normed_out(c).wait()
        scatter.finish(c)
        gather.finish(c)

    loop(count, drain)


def units_kernel(normed_ref, grad_ref, wg_ref, wu_ref, wd_ref, hidden_ref, gate_ref, up_ref):
    block = normed_ref[...]
    gate = dot_nn(block, wg_ref[...])
    up = dot_nn(block, wu_ref[...])
    grad = dot_nt(grad_ref[...], wd_ref[...])
    sig = jax.nn.sigmoid(gate)
    act = gate * sig
    hidden_ref[...] = (act * up).astype(BF16)
    gate_ref[...] = (grad * up * sig * (1.0 + gate * (1.0 - sig))).astype(BF16)
    up_ref[...] = (grad * act).astype(BF16)


def stats_part(part32, normed, normed_rows, part, c, first, second):
    def piece(r):
        rows = pl.ds(pl.multiple_of(r * ROWS, ROWS), ROWS)
        field = part32[rows, :]
        first[rows, :] = fold_lanes(field)
        second[rows, :] = fold_lanes(field * normed[normed_rows(r), :].astype(F32))
        part[sub_rows(c, r), :] = field.astype(BF16)

    loop(CHUNK // ROWS, piece)


def units_back_kernel(
    n, coef, gate_ref, up_ref, wg_ref, wu_ref, normed_ref, scale_ref, c_hbm,
    entry_ref, gb1_hbm,
    c_buf, part32, first, second, part, came, mine, others, all1, in_sem, out_sem,
    send1, recv1, send2, recv2, send3, recv3,
):
    tokens, features = normed_ref.shape
    width = entry_ref.shape[1]
    count = tokens // CHUNK
    c_in = pltpu.make_async_copy(c_hbm, c_buf, in_sem)
    c_in.start()
    scatter = Scatter(n, part, came, width, send1, recv1)
    stats = Stats(n, mine, others, send2, recv2)
    gather = Gather(n, all1, width, send3, recv3)
    enter(n, gather.to)

    def work(c):
        rows = chunk_rows(c)
        part32[...] = dot_nt(gate_ref[rows, :], wg_ref[...])
        part32[...] += dot_nt(up_ref[rows, :], wu_ref[...])
        stats_part(part32, normed_ref, lambda r: sub_rows(c, r), part, c, first, second)
        stats.put(c, first[...], second[...])
        stats.start(c)
        scatter.start(c)

    loop(count, work)
    c_in.wait()

    def middle(c):
        scatter.arrive(c)
        stats.arrive(c)
        first[...], second[...] = stats.means(c, features)

        def piece(r):
            rows = sub_rows(c, r)
            local = pl.ds(pl.multiple_of(r * ROWS, ROWS), ROWS)
            standard = normed_ref[rows, gather.own()].astype(F32)
            entry = repeat_lanes(scale_ref[rows, :], width) * (
                scatter.total(rows)
                - repeat_lanes(first[local, :], width)
                - standard * repeat_lanes(second[local, :], width)
            )
            entry_ref[rows, :] = entry
            grad = coef[BRANCH_E] * entry
            for i in range(c_buf.shape[0]):
                grad += coef[BRANCH + i] * c_buf[i, rows].astype(F32)
            all1[rows, gather.own()] = grad.astype(BF16)

        loop(CHUNK // ROWS, piece)
        gather.start(c)

    loop(count, middle)

    def gb1_out(c):
        return pltpu.make_async_copy(
            all1.at[chunk_rows(c)], gb1_hbm.at[chunk_rows(c)], out_sem.at[c]
        )

    def last(c):
        gather.arrive(c)
        gb1_out(c).start()

    loop(count, last)

    def drain(c):
        gb1_out(c).wait()
        scatter.finish(c)
        stats.finish(c)
        gather.finish(c)

    loop(count, drain)


def attend_back_kernel(
    n, q_ref, k_ref, v_ref, segc_ref, segr_ref, cos_ref, sin_ref, wo_ref, wq_ref, wk_ref, wv_ref,
    wd_ref, scale_ref, gb1_hbm, hidden_hbm, normed_hbm,
    dq_ref, dk_ref, dv_ref, branch_ref, entry_ref,
    gb1_buf, hidden_buf, normed_buf, own_buf, bias, dk_t, dv_t, part32, first, second,
    part1, came1, part2, came2, mine, others, in_sem, own_sem,
    send1, recv1, send2, recv2, send3, recv3,
):
    tokens, width = q_ref.shape
    features = part1.shape[1]
    count = tokens // CHUNK
    heads = width // HEAD
    factor = HEAD ** (-0.5)
    down = Scatter(n, part2, came2, width, send1, recv1)
    scatter = Scatter(n, part1, came1, width, send2, recv2)
    stats = Stats(n, mine, others, send3, recv3)

    def inputs(c, slot):
        return tuple(
            pltpu.make_async_copy(source.at[chunk_rows(c)], target.at[slot], in_sem.at[i, slot])
            for i, (source, target) in enumerate(
                ((gb1_hbm, gb1_buf), (hidden_hbm, hidden_buf), (normed_hbm, normed_buf))
            )
        )

    own_in = pltpu.make_async_copy(normed_hbm.at[:, columns(down.me, width)], own_buf, own_sem)
    own_in.start()
    for copy in inputs(count - 1, 0):
        copy.start()
    dk_t[...] = jnp.zeros_like(dk_t)
    dv_t[...] = jnp.zeros_like(dv_t)
    enter(n, scatter.to)

    def work(i):
        c = count - 1 - i
        slot = lax.rem(i, 2)

        @pl.when(i < count - 1)
        def _():
            for copy in inputs(c - 1, 1 - slot):
                copy.start()

        for copy in inputs(c, slot):
            copy.wait()
        rows = chunk_rows(c)
        part2[rows, :] = dot_nn(hidden_buf[slot], wd_ref[...]).astype(BF16)
        down.start(c)
        grad = dot_nt(gb1_buf[slot], wo_ref[...]).astype(BF16)
        start, extent = window(c, tokens)
        keys = pl.ds(start, extent)
        window_bias(c, start, extent, segc_ref, segr_ref, bias)
        cos_rows, sin_rows = cos_ref[rows, :], sin_ref[rows, :]
        for h in range(heads):
            place = slice(HEAD * h, HEAD * (h + 1))
            query, grad_h = q_ref[rows, place], grad[:, place]
            scores = dot_nt(query, k_ref[keys, place]) * factor + bias[...]
            raised = jnp.exp(scores - jnp.max(scores, axis=1, keepdims=True))
            inverse = 1.0 / jnp.sum(raised, axis=1, keepdims=True)
            probs = raised * inverse
            grad_probs = dot_nt(grad_h, v_ref[keys, place])
            centre = jnp.sum(probs * grad_probs, axis=1, keepdims=True)
            grad_scores = (probs * (grad_probs - centre)).astype(BF16)
            dv_t[place, keys] += dot_nn(jnp.transpose(grad_h), probs.astype(BF16))
            dk_t[place, keys] += dot_nn(jnp.transpose(query), grad_scores)
            dq = dot_nn(grad_scores, k_ref[keys, place]) * factor
            dq_ref[rows, place] = rotate(dq, cos_rows, sin_rows, -1.0).astype(BF16)
            dk = jnp.transpose(dk_t[place, rows]) * factor
            dk_ref[rows, place] = rotate(dk, cos_rows, sin_rows, -1.0).astype(BF16)
            dv_ref[rows, place] = jnp.transpose(dv_t[place, rows]).astype(BF16)
        part32[...] = dot_nt(dq_ref[rows, :], wq_ref[...])
        part32[...] += dot_nt(dk_ref[rows, :], wk_ref[...])
        part32[...] += dot_nt(dv_ref[rows, :], wv_ref[...])
        stats_part(
            part32,
            normed_buf.at[slot],
            lambda r: pl.ds(pl.multiple_of(r * ROWS, ROWS), ROWS),
            part1,
            c,
            first,
            second,
        )
        stats.put(c, first[...], second[...])
        stats.start(c)
        scatter.start(c)

    loop(count, work)
    own_in.wait()

    def last(i):
        c = count - 1 - i
        down.arrive(c)

        def sums(r):
            branch_ref[sub_rows(c, r), :] = down.total(sub_rows(c, r))

        loop(CHUNK // ROWS, sums)
        scatter.arrive(c)
        stats.arrive(c)
        first[...], second[...] = stats.means(c, features)

        def piece(r):
            rows = sub_rows(c, r)
            local = pl.ds(pl.multiple_of(r * ROWS, ROWS), ROWS)
            entry_ref[rows, :] = repeat_lanes(scale_ref[rows, :], width) * (
                scatter.total(rows)
                - repeat_lanes(first[local, :], width)
                - own_buf[rows, :].astype(F32) * repeat_lanes(second[local, :], width)
            )

        loop(CHUNK // ROWS, piece)

    loop(count, last)

    def drain(c):
        down.finish(c)
        scatter.finish(c)
        stats.finish(c)

    loop(count, drain)


def streams_kernel(
    coef, s_ref, c_ref, b1_ref, b2_ref, e1_ref, e2_ref, new_ref, grad_ref, sums_ref
):
    @pl.when(pl.program_id(0) == 0)
    def _():
        sums_ref[...] = jnp.zeros_like(sums_ref)

    count = s_ref.shape[0]

    def fold(field):
        field = fold_lanes(field)
        total = field[0:8]
        for j in range(1, field.shape[0] // 8):
            total += field[8 * j : 8 * (j + 1)]
        return total

    def piece(r):
        rows = pl.ds(pl.multiple_of(r * 16, 16), 16)
        s = [s_ref[i, rows].astype(F32) for i in range(count)]
        c = [c_ref[i, rows].astype(F32) for i in range(count)]
        b1, b2, e1, e2 = b1_ref[rows, :], b2_ref[rows, :], e1_ref[rows, :], e2_ref[rows, :]
        for j in range(count):
            new = coef[BRANCH + j] * b1 + coef[OUT2 + j] * b2
            grad = coef[ENTRY + j] * e2 + coef[IN1 + j] * e1
            for k in range(count):
                new += coef[MIXED + count * k + j] * s[k]
                grad += coef[MIXED + count * j + k] * c[k]
            new_ref[rows, j, :] = new.astype(BF16)
            grad_ref[rows, j, :] = grad
        pairs = [(s[i], c[j]) for i in range(count) for j in range(count)]
        pairs += [(s[i], e1) for i in range(count)] + [(s[i], e2) for i in range(count)]
        pairs += [(c[i], b1) for i in range(count)] + [(c[i], b2) for i in range(count)]
        pairs += [(b1, e2)]
        for place, (left, right) in enumerate(pairs):
            sums_ref[place] += fold(left * right)

    loop(s_ref.shape[1] // 16, piece)


def on_device(
    n,
    streams,
    segments,
    positions,
    mix_in1,
    mix_res1,
    mix_out1,
    mix_in2,
    mix_res2,
    mix_out2,
    w_query,
    w_key,
    w_value,
    w_output,
    w_gate,
    w_up,
    w_down,
    cotangent,
):
    tokens, stream_count, width = streams.shape
    features = w_query.shape[0]
    units = w_gate.shape[1]
    chunks = tokens // CHUNK
    assert tokens == LENGTH and stream_count == 4
    any_spec = pl.BlockSpec(memory_space=pl.ANY)
    vmem = pl.BlockSpec(memory_space=pltpu.VMEM)
    smem = pl.BlockSpec(memory_space=pltpu.SMEM)

    def array(shape, dtype):
        return jax.ShapeDtypeStruct(shape, dtype)

    def dma(*shape):
        return pltpu.SemaphoreType.DMA(shape)

    def pair():
        return [dma(n - 1, chunks), dma(n - 1, chunks)]

    def params(identity, mib):
        return pltpu.CompilerParams(
            collective_id=identity, has_side_effects=True, vmem_limit_bytes=mib * MIB
        )

    half = HEAD // 2
    inverse = 1.0 / 10000.0 ** (jnp.arange(half, dtype=F32) * 2.0 / HEAD)
    angles = positions.astype(F32)[:, None] * inverse[None, :]
    cosine, sine = jnp.cos(angles), jnp.sin(angles)
    cos_table = jnp.concatenate([cosine, cosine], axis=-1)
    sin_table = jnp.concatenate([-sine, sine], axis=-1)
    seg_column = jnp.broadcast_to(segments[:, None], (tokens, 128))
    seg_row = jnp.broadcast_to(segments[None, :], (8, tokens))

    def small(form, left, right):
        return jnp.einsum(form, left, right, precision=PRECISE)

    coef = jnp.concatenate(
        [
            mix_in1,
            mix_out2,
            small("ij,j->i", mix_res1, mix_in2),
            small("j,j->", mix_in2, mix_out1)[None],
            small("i,ij->j", mix_out1, mix_res2),
            small("i,i->", mix_out1, mix_in2)[None],
            small("ki,ij->kj", mix_res1, mix_res2).reshape(-1),
        ]
    )
    planes = jnp.transpose(streams, (1, 0, 2))
    cot_planes = jnp.transpose(cotangent, (1, 0, 2))

    normed1, queries, keys, values, scale1, grad_branch2 = pl.pallas_call(
        functools.partial(project_kernel, n),
        name="project",
        out_shape=[
            array((tokens, features), BF16),
            array((tokens, width), BF16),
            array((tokens, width), BF16),
            array((tokens, width), BF16),
            array((tokens, 128), F32),
            array((tokens, features), BF16),
        ],
        in_specs=[smem, vmem, vmem] + [any_spec] * 5,
        out_specs=[any_spec, vmem, vmem, vmem, vmem, any_spec],
        scratch_shapes=[
            pltpu.VMEM((stream_count, tokens, width), BF16),
            pltpu.VMEM((stream_count, tokens, width), BF16),
            pltpu.VMEM((3, features, width), BF16),
            pltpu.VMEM((tokens, features), BF16),
            pltpu.VMEM((tokens, features), BF16),
            pltpu.VMEM((tokens, features), BF16),
            dma(2, chunks),
            dma(3),
            dma(2, chunks),
        ]
        + pair()
        + pair(),
        compiler_params=params(0, 48),
    )(coef, cos_table, sin_table, planes, cot_planes, w_query, w_key, w_value)

    extent = window(0, tokens)[1]
    attended, branch1, normed2, scale2 = pl.pallas_call(
        functools.partial(attend_kernel, n),
        name="attend",
        out_shape=[
            array((tokens, width), BF16),
            array((tokens, width), F32),
            array((tokens, features), BF16),
            array((tokens, 128), F32),
        ],
        in_specs=[smem] + [vmem] * 6 + [any_spec],
        out_specs=[vmem, vmem, any_spec, vmem],
        scratch_shapes=[
            pltpu.VMEM((stream_count, tokens, width), BF16),
            pltpu.VMEM((tokens, features), BF16),
            pltpu.VMEM((n - 1, tokens, width), BF16),
            pltpu.VMEM((tokens, features), BF16),
            pltpu.VMEM((tokens, features), BF16),
            pltpu.VMEM((CHUNK, extent), F32),
            pltpu.SemaphoreType.DMA,
            dma(chunks),
        ]
        + pair()
        + pair(),
        compiler_params=params(1, 48),
    )(coef, queries, keys, values, seg_column, seg_row, w_output, planes)

    block = min(256, units)
    hidden, grad_gate_act, grad_up_act = pl.pallas_call(
        units_kernel,
        name="units",
        grid=(units // block,),
        out_shape=[array((tokens, units), BF16)] * 3,
        in_specs=[
            pl.BlockSpec((tokens, features), lambda f: (0, 0)),
            pl.BlockSpec((tokens, features), lambda f: (0, 0)),
            pl.BlockSpec((features, block), lambda f: (0, f)),
            pl.BlockSpec((features, block), lambda f: (0, f)),
            pl.BlockSpec((block, features), lambda f: (f, 0)),
        ],
        out_specs=[pl.BlockSpec((tokens, block), lambda f: (0, f))] * 3,
        compiler_params=pltpu.CompilerParams(vmem_limit_bytes=48 * MIB),
    )(normed2, grad_branch2, w_gate, w_up, w_down)

    def over_dp(left, right, dimension):
        partial = contract_rows(left, right).astype(BF16)
        return lax.psum_scatter(
            partial, "dp", scatter_dimension=dimension, tiled=True
        ).astype(F32)

    grad_w_down = over_dp(hidden, grad_branch2, 1)
    grad_w_gate = over_dp(normed2, grad_gate_act, 0)
    grad_w_up = over_dp(normed2, grad_up_act, 0)

    grad_entry2, grad_branch1 = pl.pallas_call(
        functools.partial(units_back_kernel, n),
        name="units_back",
        out_shape=[array((tokens, width), F32), array((tokens, features), BF16)],
        in_specs=[smem] + [vmem] * 6 + [any_spec],
        out_specs=[vmem, any_spec],
        scratch_shapes=[
            pltpu.VMEM((stream_count, tokens, width), BF16),
            pltpu.VMEM((CHUNK, features), F32),
            pltpu.VMEM((CHUNK, 128), F32),
            pltpu.VMEM((CHUNK, 128), F32),
            pltpu.VMEM((tokens, features), BF16),
            pltpu.VMEM((n - 1, tokens, width), BF16),
            pltpu.VMEM((chunks, 16, CHUNK), F32),
            pltpu.VMEM((n - 1, chunks, 16, CHUNK), F32),
            pltpu.VMEM((tokens, features), BF16),
            pltpu.SemaphoreType.DMA,
            dma(chunks),
        ]
        + pair()
        + pair()
        + pair(),
        compiler_params=params(2, 58),
    )(coef, grad_gate_act, grad_up_act, w_gate, w_up, normed2, scale2, cot_planes)

    grad_query_lin, grad_key_lin, grad_value_lin, branch2, grad_entry1 = pl.pallas_call(
        functools.partial(attend_back_kernel, n),
        name="attend_back",
        out_shape=[array((tokens, width), BF16)] * 3 + [array((tokens, width), F32)] * 2,
        in_specs=[vmem] * 13 + [any_spec] * 3,
        out_specs=[vmem] * 5,
        scratch_shapes=[
            pltpu.VMEM((2, CHUNK, features), BF16),
            pltpu.VMEM((2, CHUNK, units), BF16),
            pltpu.VMEM((2, CHUNK, features), BF16),
            pltpu.VMEM((tokens, width), BF16),
            pltpu.VMEM((CHUNK, extent), F32),
            pltpu.VMEM((width, tokens), F32),
            pltpu.VMEM((width, tokens), F32),
            pltpu.VMEM((CHUNK, features), F32),
            pltpu.VMEM((CHUNK, 128), F32),
            pltpu.VMEM((CHUNK, 128), F32),
            pltpu.VMEM((tokens, features), BF16),
            pltpu.VMEM((n - 1, tokens, width), BF16),
            pltpu.VMEM((tokens, features), BF16),
            pltpu.VMEM((n - 1, tokens, width), BF16),
            pltpu.VMEM((chunks, 16, CHUNK), F32),
            pltpu.VMEM((n - 1, chunks, 16, CHUNK), F32),
            dma(3, 2),
            pltpu.SemaphoreType.DMA,
        ]
        + pair()
        + pair()
        + pair(),
        compiler_params=params(3, 60),
    )(
        queries, keys, values, seg_column, seg_row, cos_table, sin_table,
        w_output, w_query, w_key, w_value, w_down, scale1, grad_branch1, hidden, normed1,
    )

    grad_w_output = over_dp(attended, grad_branch1, 1)
    grad_w_query = over_dp(normed1, grad_query_lin, 0)
    grad_w_key = over_dp(normed1, grad_key_lin, 0)
    grad_w_value = over_dp(normed1, grad_value_lin, 0)

    rows = 128
    sum_count = 33
    plane_spec = pl.BlockSpec((stream_count, rows, width), lambda t: (0, t, 0))
    field_spec = pl.BlockSpec((rows, width), lambda t: (t, 0))
    stream_spec = pl.BlockSpec((rows, stream_count, width), lambda t: (t, 0, 0))
    new_streams, stream_grad, sums = pl.pallas_call(
        streams_kernel,
        name="streams",
        grid=(tokens // rows,),
        out_shape=[
            array(streams.shape, BF16),
            array(streams.shape, F32),
            array((sum_count, 8, 128), F32),
        ],
        in_specs=[smem, plane_spec, plane_spec] + [field_spec] * 4,
        out_specs=[
            stream_spec,
            stream_spec,
            pl.BlockSpec((sum_count, 8, 128), lambda t: (0, 0, 0)),
        ],
        compiler_params=pltpu.CompilerParams(vmem_limit_bytes=48 * MIB),
    )(coef, planes, cot_planes, branch1, branch2, grad_entry1, grad_entry2)
    sums = lax.psum(jnp.sum(sums, axis=(1, 2)), ("dp", "tensor"))
    s_c = sums[0:16].reshape(4, 4)
    s_e1, s_e2, c_b1, c_b2, b_e = sums[16:20], sums[20:24], sums[24:28], sums[28:32], sums[32]
    grad_mix_in1 = s_e1
    grad_mix_res1 = small("ik,jk->ij", s_c, mix_res2) + s_e2[:, None] * mix_in2[None, :]
    grad_mix_out1 = small("jk,k->j", mix_res2, c_b1) + mix_in2 * b_e
    grad_mix_in2 = small("ki,k->i", mix_res1, s_e2) + mix_out1 * b_e
    grad_mix_res2 = small("ki,kj->ij", mix_res1, s_c) + mix_out1[:, None] * c_b1[None, :]
    grad_mix_out2 = c_b2
    return (
        new_streams,
        stream_grad,
        grad_w_query,
        grad_w_key,
        grad_w_value,
        grad_w_output,
        grad_w_gate,
        grad_w_up,
        grad_w_down,
        grad_mix_in1,
        grad_mix_res1,
        grad_mix_out1,
        grad_mix_in2,
        grad_mix_res2,
        grad_mix_out2,
    )


def solution(mesh):
    return jax.shard_map(
        functools.partial(on_device, mesh.shape["tensor"]),
        mesh=mesh,
        in_specs=(
            P("dp", None, "tensor"),
            P("dp"),
            P("dp"),
            P(),
            P(),
            P(),
            P(),
            P(),
            P(),
            P(None, "tensor"),
            P(None, "tensor"),
            P(None, "tensor"),
            P("tensor", None),
            P(None, "tensor"),
            P(None, "tensor"),
            P("tensor", None),
            P("dp", None, "tensor"),
        ),
        out_specs=(
            P("dp", None, "tensor"),
            P("dp", None, "tensor"),
            P("dp", "tensor"),
            P("dp", "tensor"),
            P("dp", "tensor"),
            P("tensor", "dp"),
            P("dp", "tensor"),
            P("dp", "tensor"),
            P("tensor", "dp"),
            P(),
            P(),
            P(),
            P(),
            P(),
            P(),
        ),
        check_vma=False,
    )
```

time: 1720 us -> 899 us (0.52)
  waiting for transfers between devices: 1060 us -> 245 us
  Pallas kernels: 0 us -> 479 us
  matrix products: 512 us -> 72.6 us
  other arithmetic: 75.2 us -> 20 us
    pallas_call x0 -> x6, Pallas kernels: none -> 479 us  [the longest x1 113 us: on_device(): pl.pallas_call(functools.partial(units_back_kernel, n), name='units_back'...]
    dot_general x34 -> x7, matrix products: 439 us -> 6.05 us  [small(): return jnp.einsum(form, left, right, precision=PRECISE)]
    reduce_scatter x9 -> x7, waiting for transfers between devices: 669 us -> 245 us  [over_dp(): lax.psum_scatter(partial, 'dp', scatter_dimension=dimension, tiled=True)]
    all_gather x4 -> x0, waiting for transfers between devices: 216 us -> none  [the longest x1 85.3 us: on_device(): whole1 = lax.all_gather(entry1, 'tensor', axis=1, tiled=True)]
    psum x2 -> x0, waiting for transfers between devices: 172 us -> none  [the longest x1 172 us: on_device(): grad_normed2 = lax.psum(partial2, 'tensor')]
    reduce_sum x7 -> x1, other arithmetic: 38.9 us -> 0.32 us  [on_device(): sums = lax.psum(jnp.sum(sums, axis=(1, 2)), ('dp', 'tensor'))]
  transfers between devices with their start and end apart: 15 -> 7, of which waited for: 11 -> 3; matrix products, arithmetic and copies ran while one was open for 24% -> 9% of each run, Pallas kernels for 0% -> 15%
where the time goes in v1:
time: 899 us; the launch traced here: 890 us
  Pallas kernels  479 us (53%)
  waiting for transfers between devices  245 us (27%)
  matrix products  72.6 us (8%)
  blocking collectives  40.6 us (5%)
  other arithmetic  20 us (2%)
  local copies, waits for them, and re-layouts  17.3 us (2%)
  between operations  14.9 us (2%)
    reduce_scatter x7, waiting for transfers between devices, over_dp(): lax.psum_scatter(partial, 'dp', scatter_dimension=dimension, tiled=True)  245 us
    pallas_call x1, Pallas kernels, on_device(): pl.pallas_call(functools.partial(units_back_kernel, n), name='units_back'...  113 us
    pallas_call x1, Pallas kernels, on_device(): pl.pallas_call(functools.partial(attend_back_kernel, n), name='attend_bac...  109 us
    pallas_call x1, Pallas kernels, on_device(): pl.pallas_call(functools.partial(attend_kernel, n), name='attend', out_sh...  104 us
    pallas_call x1, Pallas kernels, on_device(): pl.pallas_call(functools.partial(project_kernel, n), name='project', out_...  98.4 us
    dot_general x7, matrix products, contract_rows(): lax.dot_general(left, right, (((0,), (0,)), ((), ())), preferred_element_...  66.5 us
    psum x1, blocking collectives, on_device(): sums = lax.psum(jnp.sum(sums, axis=(1, 2)), ('dp', 'tensor'))  40.6 us
    pallas_call x1, Pallas kernels, on_device(): pl.pallas_call(units_kernel, name='units', grid=(units // block,), out_sh...  34.6 us
  transfers between devices with their start and end apart: 7, of which 3 were waited for; matrix products, arithmetic and copies ran while one was open for 9% of the time, Pallas kernels for 15%

profile of v1, /device:TPU:0, one launch (start us, length us, event | category | flops | bytes accessed | tf_op | source)
XLA Modules:
  0.0 889.7 jit_solution(18338867799542463791)
XLA Ops:
  7.3 1.3 multiply_reduce_fusion
  8.5 0.8 convolution_bitcast_fusion.4
  9.3 0.8 convolution_bitcast_fusion.3
  10.2 0.8 fusion.11
  11.1 0.7 convert_element_type.45
  11.8 1.9 fusion.3
  13.7 7.6 copy_bitcast_fusion
  21.3 0.3 pad_maximum_fusion
  21.7 1.4 concatenate.9.coef
  23.1 98.4 %project.1 = (bf16[1024,2048]{1,0:T(8,128)(2,1)}, bf16[1024,512]{1,0:T(8,128)(2,1)S(1)}, bf16[1024,512]{1,0:T(8,128)(2,1)S(1)}, bf16[1024,512]{1,0:T(8,128)(2,1)...) custom-call(f32[34]{0:T(128)S(1)} %concatenate.9.coef, f32[1024,128]{1,0:T(8,128)S(1)} %get-tuple-element.83.cos_ref, ...), custom_call_target="tpu_custom_call" | custom-call | tf_op jit(solution)/shard_map/project/pallas_call | solution.py:726
  121.6 0.8 copy-done.10
  122.4 0.2 broadcast_in_dim.10.segc_ref
  122.6 103.8 %attend.1 = (bf16[1024,512]{1,0:T(8,128)(2,1)S(1)}, f32[1024,512]{1,0:T(8,128)}, bf16[1024,2048]{1,0:T(8,128)(2,1)}, f32[1024,128]{1,0:T(8,128)S(1)}) custom-call(f32[34]{0:T(128)S(1)} %concatenate.9.coef, bf16[1024,512]{1,0:T(8,128)(2,1)S(1)} %get-tuple-element.38.q_ref, bf16[1024,512]{1,0:T(8,128)(2,1)S(1)} %get-tuple-element.39.k_ref, ...), custom_call_target="tpu_custom_call" | custom-call | tf_op jit(solution)/shard_map/attend/pallas_call | solution.py:756
  226.5 34.6 %units.1 = (bf16[1024,2048]{1,0:T(8,128)(2,1)S(1)}, bf16[1024,2048]{1,0:T(8,128)(2,1)}, bf16[1024,2048]{1,0:T(8,128)(2,1)}) custom-call(bf16[1024,2048]{1,0:T(8,128)(2,1)} %get-tuple-element.43.normed_ref, bf16[1024,2048]{1,0:T(8,128)(2,1)} %get-tuple-element.44.grad_ref, bf16[2048,2048]{1,0:T(8,128)(2,1)} %wg_ref.3, bf16[2048,2048]{1,0:T(8,128)(2,1)} %wu_ref.3, ...), custom_call_target="tpu_custom_call" | custom-call | tf_op jit(solution)/shard_map/units/pallas_call | solution.py:783
  261.1 1.9 copy-done.4
  263.0 112.9 %units_back.1 = (f32[1024,512]{1,0:T(8,128)}, bf16[1024,2048]{1,0:T(8,128)(2,1)}) custom-call(f32[34]{0:T(128)} %copy-done.13, bf16[1024,2048]{1,0:T(8,128)(2,1)} %get-tuple-element.45.gate_ref, bf16[1024,2048]{1,0:T(8,128)(2,1)} %get-tuple-element.46.up_ref, bf16[2048,2048]{1,0:T(8,128)(2,1)} %wg_ref.3, bf16[2048,2048]{1,0:T(8,128)(2,1)} %wu_ref.3, ...), custom_call_target="tpu_custom_call" | custom-call | tf_op jit(solution)/shard_map/units_back/pallas_call | solution.py:809
  376.0 6.0 convolution_convert_fusion.3
  382.0 108.5 %attend_back.1 = (bf16[1024,512]{1,0:T(8,128)(2,1)}, bf16[1024,512]{1,0:T(8,128)(2,1)}, bf16[1024,512]{1,0:T(8,128)(2,1)}, f32[1024,512]{1,0:T(8,128)}, f32[1024,512]{1,0:T(8,128)}) custom-call(bf16[1024,512]{1,0:T(8,128)(2,1)} %copy-done.5, bf16[1024,512]{1,0:T(8,128)(2,1)} %copy-done.6, bf16[1024,512]{1,0:T(8,128)(2,1)} %copy-done.7, ...), custom_call_target="tpu_custom_call" | custom-call | tf_op jit(solution)/shard_map/attend_back/pallas_call | solution.py:834
  490.6 6.3 convolution_convert_fusion.6
  496.9 0.3 reduce-scatter.10.cloned.1.call-start
  497.1 6.0 convolution_convert_fusion.5
  503.2 6.0 convolution_convert_fusion.4
  509.3 14.1 %convolution_convert_fusion = bf16[2048,2048]{1,0:T(8,128)(2,1)} fusion(bf16[1024,2048]{1,0:T(8,128)(2,1)} %copy-done.4, bf16[1024,2048]{1,0:T(8,128)(2,1)} %get-tuple-element.44.grad_ref), kind=kOutput, calls=%fused_computation | convolution fusion | flops 8594128896 | bytes 16777216 | tf_op jit(solution)/shard_map/dot_general | solution.py:27
  523.4 0.3 reduce-scatter.18.cloned.1.call-start
  523.7 14.1 %convolution_convert_fusion.1 = bf16[2048,2048]{1,0:T(8,128)(2,1)} fusion(bf16[1024,2048]{1,0:T(8,128)(2,1)} %get-tuple-element.43.normed_ref, bf16[1024,2048]{1,0:T(8,128)(2,1)} %get-tuple-element.46.up_ref), kind=kOutput, calls=%fused_computation.1 | convolution fusion | flops 8594128896 | bytes 16777216 | tf_op jit(solution)/shard_map/dot_general | solution.py:27
  538.0 14.1 %convolution_convert_fusion.2 = bf16[2048,2048]{1,0:T(8,128)(2,1)} fusion(bf16[1024,2048]{1,0:T(8,128)(2,1)} %get-tuple-element.43.normed_ref, bf16[1024,2048]{1,0:T(8,128)(2,1)} %get-tuple-element.45.gate_ref), kind=kOutput, calls=%fused_computation.2 | convolution fusion | flops 8594128896 | bytes 16777216 | tf_op jit(solution)/shard_map/dot_general | solution.py:27
  552.0 1.6 copy-done.8
  553.6 1.6 copy-done.9
  555.2 20.6 %streams.1 = (bf16[1024,4,512]{2,1,0:T(4,128)(2,1)}, f32[1024,4,512]{2,1,0:T(4,128)}, f32[33,8,128]{2,1,0:T(8,128)S(1)}) custom-call(f32[34]{0:T(128)S(1)} %copy-done.14, bf16[4,1024,512]{2,1,0:T(8,128)(2,1)} %get-tuple-element.86.s_hbm.s_ref, bf16[4,1024,512]{2,1,0:T(8,128)(2,1)} %get-tuple-element.85.c_hbm.c_ref, f32[1024,512]{1,0:T(8,128)S(1)} %copy-done.8, ...), custom_call_target="tpu_custom_call" | custom-call | tf_op jit(solution)/shard_map/streams/pallas_call | solution.py:879
  575.8 0.3 reduce_sum.9
  576.1 40.6 %psum.7 = f32[33]{0:T(128)S(1)} all-reduce(f32[33]{0:T(128)S(1)} %reduce_sum.9), channel_id=1, replica_groups=mesh['dp'=8,'tensor'=4] {'dp','tensor'}, use_global_device_ids=true, to_apply=%region_8.0 | all-reduce | flops 33 | bytes 264 | tf_op jit(solution)/shard_map/psum | solution.py:896
  616.7 0.6 slice.22
  617.4 0.6 fusion.10
  618.0 0.2 fusion
  618.1 0.7 copy.34
  618.8 1.4 fusion.2
  620.2 1.4 fusion.1
  621.5 0.7 convolution_add_fusion
  622.3 1.8 convert_element_type.53
  624.0 1.8 convert_element_type.47
  625.8 1.8 convert_element_type.49
  627.7 1.8 convert_element_type.51
  629.5 69.7 %reduce-scatter.20.cloned.1.call-done = bf16[2048,256]{1,0:T(8,128)(2,1)} async-done(((bf16[2048,2048]{1,0:T(8,128)(2,1)}), bf16[2048,256]{1,0:T(8,128)(2,1)}) %reduce-scatter.20.cloned.1.call-update) | async-done | bytes 1048592 | tf_op jit(solution)/shard_map/reduce_scatter | solution.py:801
  699.2 2.7 convert_element_type.59
  701.9 87.4 %reduce-scatter.18.cloned.1.call-done = bf16[256,2048]{1,0:T(8,128)(2,1)} async-done(((bf16[2048,2048]{1,0:T(8,128)(2,1)}), bf16[256,2048]{1,0:T(8,128)(2,1)}) %reduce-scatter.18.cloned.1.call-update) | async-done | bytes 1048592 | tf_op jit(solution)/shard_map/reduce_scatter | solution.py:801
  789.3 2.8 convert_element_type.57
  792.1 87.5 %reduce-scatter.16.cloned.1.call-done = bf16[256,2048]{1,0:T(8,128)(2,1)} async-done(((bf16[2048,2048]{1,0:T(8,128)(2,1)}), bf16[256,2048]{1,0:T(8,128)(2,1)}) %reduce-scatter.16.cloned.1.call-update) | async-done | bytes 1048592 | tf_op jit(solution)/shard_map/reduce_scatter | solution.py:801
  879.6 2.8 convert_element_type.55
  (62 shorter events, 0.6 us)
Async XLA Ops:
  7.2 1.4 copy-start
  7.2 615.1 %reduce-scatter.14.cloned.1.call-start = ((), (), s32[]{:S(2)}) async-start(), calls=%async_computation.10 | async-start | bytes 2359296 | tf_op jit(solution)/shard_map/reduce_scatter | solution.py:801
  13.7 8.0 copy-start.17
  13.7 8.0 copy-start.18
  21.7 99.9 %copy-start.1 = (f32[1024,128]{1,0:T(8,128)}, f32[1024,128]{1,0:T(8,128)S(1)}, u32[]{:S(2)}) copy-start(f32[1024,128]{1,0:T(8,128)S(1)} %get-tuple-element.83.cos_ref) | copy-start | bytes 1572868
  21.7 99.9 %copy-start.2 = (f32[1024,128]{1,0:T(8,128)}, f32[1024,128]{1,0:T(8,128)S(1)}, u32[]{:S(2)}) copy-start(f32[1024,128]{1,0:T(8,128)S(1)} %get-tuple-element.84.sin_ref) | copy-start | bytes 1572868
  23.1 99.5 %copy-start.13 = (f32[34]{0:T(128)}, f32[34]{0:T(128)S(1)}, u32[]{:S(2)}) copy-start(f32[34]{0:T(128)S(1)} %concatenate.9.coef) | copy-start | bytes 412
  23.1 99.2 %copy-start.15 = (s32[1024]{0:T(1024)S(1)}, s32[1024]{0:T(1024)}, u32[]{:S(2)}) copy-start(s32[1024]{0:T(1024)} %param.18) | copy-start | bytes 12292
  121.6 0.8 copy-start.10
  122.4 104.1 %copy-start.5 = (bf16[1024,512]{1,0:T(8,128)(2,1)}, bf16[1024,512]{1,0:T(8,128)(2,1)S(1)}, u32[]{:S(2)}) copy-start(bf16[1024,512]{1,0:T(8,128)(2,1)S(1)} %get-tuple-element.38.q_ref) | copy-start | bytes 3145732
  122.4 104.1 %copy-start.6 = (bf16[1024,512]{1,0:T(8,128)(2,1)}, bf16[1024,512]{1,0:T(8,128)(2,1)S(1)}, u32[]{:S(2)}) copy-start(bf16[1024,512]{1,0:T(8,128)(2,1)S(1)} %get-tuple-element.39.k_ref) | copy-start | bytes 3145732
  122.4 104.1 %copy-start.7 = (bf16[1024,512]{1,0:T(8,128)(2,1)}, bf16[1024,512]{1,0:T(8,128)(2,1)S(1)}, u32[]{:S(2)}) copy-start(bf16[1024,512]{1,0:T(8,128)(2,1)S(1)} %get-tuple-element.40.v_ref) | copy-start | bytes 3145732
  122.4 104.1 %copy-start.12 = (s32[8,1024]{1,0:T(8,128)}, s32[8,1024]{1,0:T(8,128)S(1)}, u32[]{:S(2)}) copy-start(s32[8,1024]{1,0:T(8,128)S(1)} %broadcast_in_dim.11.segr_ref) | copy-start | bytes 98308
  122.6 103.9 %copy-start.3 = (s32[1024,128]{1,0:T(8,128)}, s32[1024,128]{1,0:T(8,128)S(1)}, u32[]{:S(2)}) copy-start(s32[1024,128]{1,0:T(8,128)S(1)} %broadcast_in_dim.10.segc_ref) | copy-start | bytes 1572868
  226.5 34.6 %copy-start.11 = (f32[1024,128]{1,0:T(8,128)}, f32[1024,128]{1,0:T(8,128)S(1)}, u32[]{:S(2)}) copy-start(f32[1024,128]{1,0:T(8,128)S(1)} %get-tuple-element.47.scale_ref) | copy-start | bytes 1572868
  261.1 1.9 copy-start.4
  382.0 242.1 %reduce-scatter.8.cloned.1.call-start = ((), (), s32[]{:S(2)}) async-start(), calls=%async_computation.7 | async-start | bytes 2359296 | tf_op jit(solution)/shard_map/reduce_scatter | solution.py:801
  490.5 6.6 copy-start.20
  496.9 129.0 %reduce-scatter.10.cloned.1.call-start = ((), (), s32[]{:S(2)}) async-start(), calls=%async_computation.8 | async-start | bytes 2359296 | tf_op jit(solution)/shard_map/reduce_scatter | solution.py:801
  497.1 6.1 copy-start.19
  503.2 124.5 %reduce-scatter.12.cloned.1.call-start = ((), (), s32[]{:S(2)}) async-start(), calls=%async_computation.9 | async-start | bytes 2359296 | tf_op jit(solution)/shard_map/reduce_scatter | solution.py:801
  509.2 190.0 %reduce-scatter.20.cloned.1.call-start = ((), (), s32[]{:S(2)}) async-start(), calls=%async_computation.13 | async-start | bytes 9437184 | tf_op jit(solution)/shard_map/reduce_scatter | solution.py:801
  523.4 265.9 %reduce-scatter.18.cloned.1.call-start = ((), (), s32[]{:S(2)}) async-start(), calls=%async_computation.12 | async-start | bytes 9437184 | tf_op jit(solution)/shard_map/reduce_scatter | solution.py:801
  537.9 341.7 %reduce-scatter.16.cloned.1.call-start = ((), (), s32[]{:S(2)}) async-start(), calls=%async_computation.11 | async-start | bytes 9437184 | tf_op jit(solution)/shard_map/reduce_scatter | solution.py:801
  552.0 1.6 copy-start.8
  552.0 1.6 copy-start.14
  553.6 1.6 copy-start.9
  555.2 62.7 %copy-start.21 = (f32[4]{0:T(128)S(1)}, f32[4]{0:T(128)}, u32[]{:S(2)}) copy-start(f32[4]{0:T(128)} %param.22) | copy-start | bytes 52
  555.2 65.0 %copy-start.16 = (f32[4,4]{1,0:T(4,128)S(1)}, f32[4,4]{1,0:T(4,128)}, u32[]{:S(2)}) copy-start(f32[4,4]{1,0:T(4,128)} %param.24) | copy-start | bytes 196
  555.2 65.0 %copy-start.22 = (f32[4]{0:T(128)S(1)}, f32[4]{0:T(128)}, u32[]{:S(2)}) copy-start(f32[4]{0:T(128)} %param.23) | copy-start | bytes 52
Sparse Core Ops, SparseCore 0:
  382.1 35.3 reduce-scatter.13
  497.0 36.6 reduce-scatter.7
  536.5 34.5 reduce-scatter.9
  573.9 34.4 reduce-scatter.11
  610.5 88.6 reduce-scatter.19
  701.3 87.9 reduce-scatter.17
  791.6 87.9 reduce-scatter.15

commit v2 on v1

--- a/solution.py
+++ b/solution.py
@@ -77,6 +77,10 @@
     return pl.ds(pl.multiple_of(c * CHUNK, CHUNK), CHUNK)
 
 
+def half_rows(c, half):
+    return pl.ds(pl.multiple_of(c * CHUNK + half * (CHUNK // 2), CHUNK // 2), CHUNK // 2)
+
+
 class Gather:
     def __init__(self, n, buf, width, send_sem, recv_sem):
         self.n, self.buf, self.width = n, buf, width
@@ -86,20 +90,58 @@
     def own(self):
         return columns(self.me, self.width)
 
+    def copy(self, rows, owner, k, c, target):
+        view = self.buf.at[rows, columns(owner, self.width)]
+        return remote(view, view, self.send_sem.at[k, c], self.recv_sem.at[k, c], target)
+
+    def direct(self):
+        return 2 if self.n == 4 else self.n - 1
+
+    def handed(self, c):
+        side, up, _ = self.to
+        return (
+            self.copy(half_rows(c, 0), side, 2, c, up),
+            self.copy(half_rows(c, 1), up, 3, c, side),
+        )
+
     def start(self, c):
-        view = self.buf.at[chunk_rows(c), self.own()]
-        for k in range(self.n - 1):
-            remote(view, view, self.send_sem.at[k, c], self.recv_sem.at[k, c], self.to[k]).start()
+        for k in range(self.direct()):
+            self.copy(chunk_rows(c), self.me, k, c, self.to[k]).start()
+
+    def relay(self, c):
+        if self.n == 4:
+            for k, copy in enumerate(self.handed(c)):
+                self.copy(chunk_rows(c), self.source[k], k, c, self.to[k]).wait_recv()
+                copy.start()
 
     def arrive(self, c):
-        for k in range(self.n - 1):
-            view = self.buf.at[chunk_rows(c), columns(self.source[k], self.width)]
-            remote(view, view, self.send_sem.at[k, c], self.recv_sem.at[k, c], self.to[k]).wait_recv()
+        if self.n == 4:
+            side, up, across = self.to
+            self.copy(half_rows(c, 0), across, 2, c, up).wait_recv()
+            self.copy(half_rows(c, 1), across, 3, c, side).wait_recv()
+        else:
+            for k in range(self.n - 1):
+                self.copy(chunk_rows(c), self.source[k], k, c, self.to[k]).wait_recv()
 
     def finish(self, c):
-        view = self.buf.at[chunk_rows(c), self.own()]
-        for k in range(self.n - 1):
-            remote(view, view, self.send_sem.at[k, c], self.recv_sem.at[k, c], self.to[k]).wait_send()
+        for k in range(self.direct()):
+            self.copy(chunk_rows(c), self.me, k, c, self.to[k]).wait_send()
+        if self.n == 4:
+            for copy in self.handed(c):
+                copy.wait_send()
+
+    def take(self, count, work):
+        self.relay(0)
+
+        def body(c):
+            @pl.when(c + 1 < count)
+            def _():
+                self.relay(c + 1)
+
+            self.arrive(c)
+            work(c)
+
+        loop(count, body)
 
 
 class Scatter:
@@ -108,30 +150,71 @@
         self.me, self.to, self.source = partners(n)
         self.send_sem, self.recv_sem = send_sem, recv_sem
 
-    def copy(self, c, k):
+    def copy(self, rows, owner, slot, k, c, target):
         return remote(
-            self.part.at[chunk_rows(c), columns(self.to[k], self.width)],
-            self.came.at[k, chunk_rows(c)],
+            self.part.at[rows, columns(owner, self.width)],
+            self.came.at[slot, rows],
             self.send_sem.at[k, c],
             self.recv_sem.at[k, c],
-            self.to[k],
+            target,
+        )
+
+    def first(self, c):
+        if self.n != 4:
+            return tuple(
+                (chunk_rows(c), self.to[k], k, k, c, self.to[k]) for k in range(self.n - 1)
+            )
+        side, up, across = self.to
+        return (
+            (half_rows(c, 0), across, 2, 0, c, side),
+            (half_rows(c, 1), across, 2, 1, c, up),
+            (half_rows(c, 0), side, 0, 2, c, side),
+            (half_rows(c, 1), up, 1, 3, c, up),
+        )
+
+    def second(self, c):
+        if self.n != 4:
+            return ()
+        side, up, _ = self.to
+        return (
+            (half_rows(c, 0), up, 1, 4, c, up),
+            (half_rows(c, 1), side, 0, 5, c, side),
         )
 
     def start(self, c):
-        for k in range(self.n - 1):
-            self.copy(c, k).start()
+        for place in self.first(c):
+            self.copy(*place).start()
+
+    def relay(self, c):
+        second = self.second(c)
+        first = self.first(c)
+        for half in range(len(second)):
+            self.copy(*first[half]).wait_recv()
+            owner = columns(self.to[1 - half], self.width)
+            base = c * CHUNK + half * (CHUNK // 2)
+
+            def add(r):
+                rows = pl.ds(pl.multiple_of(base + r * ROWS, ROWS), ROWS)
+                total = self.part[rows, owner].astype(F32) + self.came[2, rows].astype(F32)
+                self.part[rows, owner] = total.astype(BF16)
+
+            loop(CHUNK // 2 // ROWS, add)
+            self.copy(*second[half]).start()
 
     def arrive(self, c):
-        for k in range(self.n - 1):
-            self.copy(c, k).wait_recv()
+        places = self.first(c)
+        if self.n == 4:
+            places = places[2:] + self.second(c)
+        for place in places:
+            self.copy(*place).wait_recv()
 
     def finish(self, c):
-        for k in range(self.n - 1):
-            self.copy(c, k).wait_send()
+        for place in self.first(c) + self.second(c):
+            self.copy(*place).wait_send()
 
     def total(self, rows):
         total = self.part[rows, columns(self.me, self.width)].astype(F32)
-        for k in range(self.n - 1):
+        for k in range(2 if self.n == 4 else self.n - 1):
             total += self.came[k, rows].astype(F32)
         return total
 
@@ -147,7 +230,17 @@
             self.mine.at[c], self.came.at[k, c], self.send_sem.at[k, c], self.recv_sem.at[k, c], self.to[k]
         )
 
-    start, arrive, finish = Scatter.start, Scatter.arrive, Scatter.finish
+    def start(self, c):
+        for k in range(self.n - 1):
+            self.copy(c, k).start()
+
+    def arrive(self, c):
+        for k in range(self.n - 1):
+            self.copy(c, k).wait_recv()
+
+    def finish(self, c):
+        for k in range(self.n - 1):
+            self.copy(c, k).wait_send()
 
     def put(self, c, first, second):
         ones = jnp.ones((8, 128), F32)
@@ -155,6 +248,21 @@
             self.mine[c, place : place + 8] = lax.dot_general(
                 ones, field, (((1,), (1,)), ((), ())), precision=PRECISE, preferred_element_type=F32
             )
+
+    def moments(self, c, width):
+        pieces = [self.mine[c]] + [self.came[k, c] for k in range(self.n - 1)]
+        count = float(self.n * width)
+        mean = sum(piece[0:8] for piece in pieces) * (1.0 / count)
+        squares = sum(
+            piece[8:16] + width * (piece[0:8] * (1.0 / width) - mean) ** 2 for piece in pieces
+        )
+        share = jnp.full((8, 128), 0.125, F32)
+        return tuple(
+            lax.dot_general(
+                row, share, (((0,), (0,)), ((), ())), precision=PRECISE, preferred_element_type=F32
+            )
+            for row in (mean, lax.rsqrt(squares * (1.0 / count) + EPS))
+        )
 
     def means(self, c, features):
         total = self.mine[c]
@@ -185,17 +293,6 @@
     return pl.ds(pl.multiple_of(c * CHUNK + r * ROWS, ROWS), ROWS)
 
 
-def normalize_rows(source, rows, target, target_rows, scale_ref):
-    field = source[rows, :].astype(F32)
-    features = field.shape[1]
-    average = jnp.sum(field, axis=1, keepdims=True) * (1.0 / features)
-    centered = field - average
-    variance = jnp.sum(centered * centered, axis=1, keepdims=True) * (1.0 / features)
-    scaling = lax.rsqrt(variance + EPS)
-    target[target_rows, :] = (centered * scaling).astype(BF16)
-    scale_ref[rows, :] = jnp.broadcast_to(scaling, (field.shape[0], 128))
-
-
 def repeat_lanes(field, width):
     return jnp.concatenate([field] * (width // 128), axis=1)
 
@@ -207,6 +304,35 @@
     return total
 
 
+def local_rows(r):
+    return pl.ds(pl.multiple_of(r * ROWS, ROWS), ROWS)
+
+
+def fold_entry(entry, first, second, rows):
+    first[rows, :] = fold_lanes(entry)
+    centered = entry - jnp.sum(entry, axis=1, keepdims=True) * (1.0 / entry.shape[1])
+    second[rows, :] = fold_lanes(centered * centered)
+
+
+def standardize(c, stats, gather, first, second, stand_ref, scale_ref):
+    width = stand_ref.shape[1]
+    stats.arrive(c)
+    first[...], second[...] = stats.moments(c, width)
+
+    def piece(r):
+        rows, local = sub_rows(c, r), local_rows(r)
+        scaling = second[local, :]
+        stand = (stand_ref[rows, :] - repeat_lanes(first[local, :], width)) * repeat_lanes(
+            scaling, width
+        )
+        stand_ref[rows, :] = stand
+        scale_ref[rows, :] = scaling
+        gather.buf[rows, gather.own()] = stand.astype(BF16)
+
+    loop(CHUNK // ROWS, piece)
+    gather.start(c)
+
+
 def rotate(field, cos_rows, sin_rows, sign):
     turned = pltpu.roll(field, HEAD // 2, 1)
     return field * cos_rows + (sign * turned) * sin_rows
@@ -214,9 +340,9 @@
 
 def project_kernel(
     n, coef, cos_ref, sin_ref, s_hbm, c_hbm, wq_hbm, wk_hbm, wv_hbm,
-    normed_hbm, q_ref, k_ref, v_ref, scale_ref, gb2_hbm,
-    s_buf, c_buf, w_buf, all1, all2, normed, in_sem, w_sem, out_sem,
-    send1, recv1, send2, recv2,
+    normed_hbm, q_ref, k_ref, v_ref, stand_ref, scale_ref, gb2_hbm,
+    s_buf, c_buf, w_buf, all1, all2, first, second, mine, others, in_sem, w_sem, out_sem,
+    send1, recv1, send2, recv2, send3, recv3,
 ):
     _, tokens, width = s_buf.shape
     count = tokens // CHUNK
@@ -238,7 +364,7 @@
 
     def normed_out(c):
         return pltpu.make_async_copy(
-            normed.at[chunk_rows(c)], normed_hbm.at[chunk_rows(c)], out_sem.at[0, c]
+            all1.at[chunk_rows(c)], normed_hbm.at[chunk_rows(c)], out_sem.at[0, c]
         )
 
     def gb2_out(c):
@@ -250,40 +376,55 @@
     for j in range(3):
         w_in(j).start()
     loop(count, lambda c: c_in(c).start())
-    first = Gather(n, all1, width, send1, recv1)
-    second = Gather(n, all2, width, send2, recv2)
-    enter(n, first.to)
-
-    def mix(buf, base, target, gather, c):
-        def part(r):
-            rows = sub_rows(c, r)
-            total = coef[base] * buf[0, rows].astype(F32)
-            for i in range(1, buf.shape[0]):
-                total += coef[base + i] * buf[i, rows].astype(F32)
-            target[rows, gather.own()] = total.astype(BF16)
-
-        loop(CHUNK // ROWS, part)
-        gather.start(c)
-
-    def send_first(c):
+    gather = Gather(n, all1, width, send1, recv1)
+    incoming = Gather(n, all2, width, send2, recv2)
+    stats = Stats(n, mine, others, send3, recv3)
+    enter(n, gather.to)
+
+    def mix(buf, base, rows):
+        total = coef[base] * buf[0, rows].astype(F32)
+        for i in range(1, buf.shape[0]):
+            total += coef[base + i] * buf[i, rows].astype(F32)
+        return total
+
+    def entry(c):
         s_in(c).wait()
-        mix(s_buf, IN1, all1, first, c)
-
-    loop(count, send_first)
+
+        def piece(r):
+            field = mix(s_buf, IN1, sub_rows(c, r))
+            stand_ref[sub_rows(c, r), :] = field
+            fold_entry(field, first, second, local_rows(r))
+
+        loop(CHUNK // ROWS, piece)
+        stats.put(c, first[...], second[...])
+        stats.start(c)
+
+    def send(c):
+        standardize(c, stats, gather, first, second, stand_ref, scale_ref)
+
+    entry(0)
+
+    def ahead(c):
+        entry(c + 1)
+        send(c)
+
+    loop(count - 1, ahead)
+    send(count - 1)
     for j in range(3):
         w_in(j).wait()
 
     def work(c):
         c_in(c).wait()
-        mix(c_buf, OUT2, all2, second, c)
-        first.arrive(c)
-        loop(
-            CHUNK // ROWS,
-            lambda r: normalize_rows(all1, sub_rows(c, r), normed, sub_rows(c, r), scale_ref),
-        )
+
+        def piece(r):
+            rows = sub_rows(c, r)
+            all2[rows, incoming.own()] = mix(c_buf, OUT2, rows).astype(BF16)
+
+        loop(CHUNK // ROWS, piece)
+        incoming.start(c)
         normed_out(c).start()
         rows = chunk_rows(c)
-        block = normed[rows, :]
+        block = all1[rows, :]
         cos_rows, sin_rows = cos_ref[rows, :], sin_ref[rows, :]
         for j, target in ((0, q_ref), (1, k_ref)):
             lin = dot_nn(block, w_buf[j])
@@ -292,19 +433,15 @@
                 target[rows, place] = rotate(lin[:, place], cos_rows, sin_rows, 1.0).astype(BF16)
         v_ref[rows, :] = dot_nn(block, w_buf[2]).astype(BF16)
 
-    loop(count, work)
-
-    def end(c):
-        second.arrive(c)
-        gb2_out(c).start()
-
-    loop(count, end)
+    gather.take(count, work)
+    incoming.take(count, lambda c: gb2_out(c).start())
 
     def drain(c):
         gb2_out(c).wait()
         normed_out(c).wait()
-        first.finish(c)
-        second.finish(c)
+        stats.finish(c)
+        gather.finish(c)
+        incoming.finish(c)
 
     loop(count, drain)
 
@@ -328,8 +465,9 @@
 
 def attend_kernel(
     n, coef, q_ref, k_ref, v_ref, segc_ref, segr_ref, wo_ref, s_hbm,
-    attended_ref, branch_ref, normed_hbm, scale_ref,
-    s_buf, part, came, all2, normed, bias, in_sem, out_sem, send1, recv1, send2, recv2,
+    attended_ref, branch_ref, normed_hbm, stand_ref, scale_ref,
+    s_buf, part, came, all2, first, second, mine, others, bias, in_sem, out_sem,
+    send1, recv1, send2, recv2, send3, recv3,
 ):
     tokens, width = q_ref.shape
     count = tokens // CHUNK
@@ -338,6 +476,7 @@
     s_in.start()
     scatter = Scatter(n, part, came, width, send1, recv1)
     gather = Gather(n, all2, width, send2, recv2)
+    stats = Stats(n, mine, others, send3, recv3)
     enter(n, gather.to)
 
     def attend(c):
@@ -355,7 +494,12 @@
         part[rows, :] = dot_nn(attended_ref[rows, :], wo_ref[...]).astype(BF16)
         scatter.start(c)
 
+        @pl.when(c >= 1)
+        def _():
+            scatter.relay(c - 1)
+
     loop(count, attend)
+    scatter.relay(count - 1)
     s_in.wait()
 
     def middle(c):
@@ -368,37 +512,61 @@
             entry = coef[ENTRY_B] * branch
             for i in range(s_buf.shape[0]):
                 entry += coef[ENTRY + i] * s_buf[i, rows].astype(F32)
-            all2[rows, gather.own()] = entry.astype(BF16)
+            stand_ref[rows, :] = entry
+            fold_entry(entry, first, second, local_rows(r))
 
         loop(CHUNK // ROWS, piece)
-        gather.start(c)
-
-    loop(count, middle)
+        stats.put(c, first[...], second[...])
+        stats.start(c)
+
+    def send(c):
+        standardize(c, stats, gather, first, second, stand_ref, scale_ref)
+
+    middle(0)
+
+    def ahead(c):
+        middle(c + 1)
+        send(c)
+
+    loop(count - 1, ahead)
+    send(count - 1)
 
     def normed_out(c):
         return pltpu.make_async_copy(
-            normed.at[chunk_rows(c)], normed_hbm.at[chunk_rows(c)], out_sem.at[c]
-        )
-
-    def last(c):
-        gather.arrive(c)
-        loop(
-            CHUNK // ROWS,
-            lambda r: normalize_rows(all2, sub_rows(c, r), normed, sub_rows(c, r), scale_ref),
-        )
-        normed_out(c).start()
-
-    loop(count, last)
+            all2.at[chunk_rows(c)], normed_hbm.at[chunk_rows(c)], out_sem.at[c]
+        )
+
+    gather.take(count, lambda c: normed_out(c).start())
 
     def drain(c):
         normed_out(c).wait()
         scatter.finish(c)
+        stats.finish(c)
         gather.finish(c)
 
     loop(count, drain)
 
 
-def units_kernel(normed_ref, grad_ref, wg_ref, wu_ref, wd_ref, hidden_ref, gate_ref, up_ref):
+def units_kernel(
+    normed_ref, grad_ref, wg_ref, wu_ref, wd_ref, hidden_ref, acts_hbm, buf, sem
+):
+    step, steps = pl.program_id(0), pl.num_programs(0)
+    slot = lax.rem(step, 2)
+    width = buf.shape[3]
+
+    def out(at, part):
+        place = (part * steps + at) * width
+        return pltpu.make_async_copy(
+            buf.at[lax.rem(at, 2), part],
+            acts_hbm.at[:, pl.ds(pl.multiple_of(place, width), width)],
+            sem.at[lax.rem(at, 2), part],
+        )
+
+    @pl.when(step >= 2)
+    def _():
+        out(step - 2, 0).wait()
+        out(step - 2, 1).wait()
+
     block = normed_ref[...]
     gate = dot_nn(block, wg_ref[...])
     up = dot_nn(block, wu_ref[...])
@@ -406,8 +574,20 @@
     sig = jax.nn.sigmoid(gate)
     act = gate * sig
     hidden_ref[...] = (act * up).astype(BF16)
-    gate_ref[...] = (grad * up * sig * (1.0 + gate * (1.0 - sig))).astype(BF16)
-    up_ref[...] = (grad * act).astype(BF16)
+    buf[slot, 0] = (grad * up * sig * (1.0 + gate * (1.0 - sig))).astype(BF16)
+    buf[slot, 1] = (grad * act).astype(BF16)
+    out(step, 0).start()
+    out(step, 1).start()
+
+    @pl.when(step == steps - 1)
+    def _():
+        @pl.when(step >= 1)
+        def _():
+            out(step - 1, 0).wait()
+            out(step - 1, 1).wait()
+
+        out(step, 0).wait()
+        out(step, 1).wait()
 
 
 def stats_part(part32, normed, normed_rows, part, c, first, second):
@@ -422,7 +602,7 @@
 
 
 def units_back_kernel(
-    n, coef, gate_ref, up_ref, wg_ref, wu_ref, normed_ref, scale_ref, c_hbm,
+    n, coef, acts_ref, wg_ref, wu_ref, normed_ref, stand_ref, scale_ref, c_hbm, _down, _gate_up,
     entry_ref, gb1_hbm,
     c_buf, part32, first, second, part, came, mine, others, all1, in_sem, out_sem,
     send1, recv1, send2, recv2, send3, recv3,
@@ -439,14 +619,20 @@
 
     def work(c):
         rows = chunk_rows(c)
-        part32[...] = dot_nt(gate_ref[rows, :], wg_ref[...])
-        part32[...] += dot_nt(up_ref[rows, :], wu_ref[...])
+        units = wg_ref.shape[1]
+        part32[...] = dot_nt(acts_ref[rows, 0:units], wg_ref[...])
+        part32[...] += dot_nt(acts_ref[rows, units : 2 * units], wu_ref[...])
         stats_part(part32, normed_ref, lambda r: sub_rows(c, r), part, c, first, second)
         stats.put(c, first[...], second[...])
         stats.start(c)
         scatter.start(c)
 
+        @pl.when(c >= 1)
+        def _():
+            scatter.relay(c - 1)
+
     loop(count, work)
+    scatter.relay(count - 1)
     c_in.wait()
 
     def middle(c):
@@ -457,7 +643,7 @@
         def piece(r):
             rows = sub_rows(c, r)
             local = pl.ds(pl.multiple_of(r * ROWS, ROWS), ROWS)
-            standard = normed_ref[rows, gather.own()].astype(F32)
+            standard = stand_ref[rows, :]
             entry = repeat_lanes(scale_ref[rows, :], width) * (
                 scatter.total(rows)
                 - repeat_lanes(first[local, :], width)
@@ -479,11 +665,7 @@
             all1.at[chunk_rows(c)], gb1_hbm.at[chunk_rows(c)], out_sem.at[c]
         )
 
-    def last(c):
-        gather.arrive(c)
-        gb1_out(c).start()
-
-    loop(count, last)
+    gather.take(count, lambda c: gb1_out(c).start())
 
     def drain(c):
         gb1_out(c).wait()
@@ -496,10 +678,10 @@
 
 def attend_back_kernel(
     n, q_ref, k_ref, v_ref, segc_ref, segr_ref, cos_ref, sin_ref, wo_ref, wq_ref, wk_ref, wv_ref,
-    wd_ref, scale_ref, gb1_hbm, hidden_hbm, normed_hbm,
-    dq_ref, dk_ref, dv_ref, branch_ref, entry_ref,
-    gb1_buf, hidden_buf, normed_buf, own_buf, bias, dk_t, dv_t, part32, first, second,
-    part1, came1, part2, came2, mine, others, in_sem, own_sem,
+    wd_ref, stand_ref, scale_ref, gb1_hbm, hidden_hbm, normed_hbm, _output, _down,
+    lin_ref, branch_ref, entry_ref,
+    gb1_buf, hidden_buf, normed_buf, bias, dk_t, dv_t, part32, first, second,
+    part1, came1, part2, came2, mine, others, in_sem,
     send1, recv1, send2, recv2, send3, recv3,
 ):
     tokens, width = q_ref.shape
@@ -519,8 +701,6 @@
             )
         )
 
-    own_in = pltpu.make_async_copy(normed_hbm.at[:, columns(down.me, width)], own_buf, own_sem)
-    own_in.start()
     for copy in inputs(count - 1, 0):
         copy.start()
     dk_t[...] = jnp.zeros_like(dk_t)
@@ -559,13 +739,13 @@
             dv_t[place, keys] += dot_nn(jnp.transpose(grad_h), probs.astype(BF16))
             dk_t[place, keys] += dot_nn(jnp.transpose(query), grad_scores)
             dq = dot_nn(grad_scores, k_ref[keys, place]) * factor
-            dq_ref[rows, place] = rotate(dq, cos_rows, sin_rows, -1.0).astype(BF16)
+            lin_ref[rows, place] = rotate(dq, cos_rows, sin_rows, -1.0).astype(BF16)
             dk = jnp.transpose(dk_t[place, rows]) * factor
-            dk_ref[rows, place] = rotate(dk, cos_rows, sin_rows, -1.0).astype(BF16)
-            dv_ref[rows, place] = jnp.transpose(dv_t[place, rows]).astype(BF16)
-        part32[...] = dot_nt(dq_ref[rows, :], wq_ref[...])
-        part32[...] += dot_nt(dk_ref[rows, :], wk_ref[...])
-        part32[...] += dot_nt(dv_ref[rows, :], wv_ref[...])
+            lin_ref[rows, slice(width + HEAD * h, width + HEAD * (h + 1))] = rotate(dk, cos_rows, sin_rows, -1.0).astype(BF16)
+            lin_ref[rows, slice(2 * width + HEAD * h, 2 * width + HEAD * (h + 1))] = jnp.transpose(dv_t[place, rows]).astype(BF16)
+        part32[...] = dot_nt(lin_ref[rows, 0:width], wq_ref[...])
+        part32[...] += dot_nt(lin_ref[rows, width : 2 * width], wk_ref[...])
+        part32[...] += dot_nt(lin_ref[rows, 2 * width : 3 * width], wv_ref[...])
         stats_part(
             part32,
             normed_buf.at[slot],
@@ -578,9 +758,14 @@
         stats.put(c, first[...], second[...])
         stats.start(c)
         scatter.start(c)
+        down.relay(c)
+
+        @pl.when(i >= 1)
+        def _():
+            scatter.relay(c + 1)
 
     loop(count, work)
-    own_in.wait()
+    scatter.relay(0)
 
     def last(i):
         c = count - 1 - i
@@ -600,7 +785,7 @@
             entry_ref[rows, :] = repeat_lanes(scale_ref[rows, :], width) * (
                 scatter.total(rows)
                 - repeat_lanes(first[local, :], width)
-                - own_buf[rows, :].astype(F32) * repeat_lanes(second[local, :], width)
+                - stand_ref[rows, :] * repeat_lanes(second[local, :], width)
             )
 
         loop(CHUNK // ROWS, piece)
@@ -616,7 +801,7 @@
 
 
 def streams_kernel(
-    coef, s_ref, c_ref, b1_ref, b2_ref, e1_ref, e2_ref, new_ref, grad_ref, sums_ref
+    coef, s_ref, c_ref, b1_ref, b2_ref, e1_ref, e2_ref, _gate_up, new_ref, grad_ref, sums_ref
 ):
     @pl.when(pl.program_id(0) == 0)
     def _():
@@ -689,8 +874,17 @@
     def dma(*shape):
         return pltpu.SemaphoreType.DMA(shape)
 
-    def pair():
-        return [dma(n - 1, chunks), dma(n - 1, chunks)]
+    def pair(lanes):
+        return [dma(lanes, chunks), dma(lanes, chunks)]
+
+    gather_sems = pair(4 if n == 4 else n - 1)
+    scatter_sems = pair(6 if n == 4 else n - 1)
+    stats_sems = pair(n - 1)
+
+    def lasts(micros):
+        return pl.CostEstimate(
+            flops=int(micros * 1.0e9), bytes_accessed=int(micros * 3.6e6), transcendentals=0
+        )
 
     def params(identity, mib):
         return pltpu.CompilerParams(
@@ -723,68 +917,79 @@
     planes = jnp.transpose(streams, (1, 0, 2))
     cot_planes = jnp.transpose(cotangent, (1, 0, 2))
 
-    normed1, queries, keys, values, scale1, grad_branch2 = pl.pallas_call(
+    def stats_scratch():
+        return [
+            pltpu.VMEM((CHUNK, 128), F32),
+            pltpu.VMEM((CHUNK, 128), F32),
+            pltpu.VMEM((chunks, 16, CHUNK), F32),
+            pltpu.VMEM((n - 1, chunks, 16, CHUNK), F32),
+        ]
+
+    normed1, queries, keys, values, stand1, scale1, grad_branch2 = pl.pallas_call(
         functools.partial(project_kernel, n),
         name="project",
+        cost_estimate=lasts(100),
         out_shape=[
             array((tokens, features), BF16),
             array((tokens, width), BF16),
             array((tokens, width), BF16),
             array((tokens, width), BF16),
+            array((tokens, width), F32),
             array((tokens, 128), F32),
             array((tokens, features), BF16),
         ],
         in_specs=[smem, vmem, vmem] + [any_spec] * 5,
-        out_specs=[any_spec, vmem, vmem, vmem, vmem, any_spec],
+        out_specs=[any_spec, vmem, vmem, vmem, vmem, vmem, any_spec],
         scratch_shapes=[
             pltpu.VMEM((stream_count, tokens, width), BF16),
             pltpu.VMEM((stream_count, tokens, width), BF16),
             pltpu.VMEM((3, features, width), BF16),
             pltpu.VMEM((tokens, features), BF16),
             pltpu.VMEM((tokens, features), BF16),
-            pltpu.VMEM((tokens, features), BF16),
-            dma(2, chunks),
-            dma(3),
-            dma(2, chunks),
         ]
-        + pair()
-        + pair(),
+        + stats_scratch()
+        + [dma(2, chunks), dma(3), dma(2, chunks)]
+        + gather_sems
+        + gather_sems
+        + stats_sems,
         compiler_params=params(0, 48),
     )(coef, cos_table, sin_table, planes, cot_planes, w_query, w_key, w_value)
 
     extent = window(0, tokens)[1]
-    attended, branch1, normed2, scale2 = pl.pallas_call(
+    attended, branch1, normed2, stand2, scale2 = pl.pallas_call(
         functools.partial(attend_kernel, n),
         name="attend",
+        cost_estimate=lasts(100),
         out_shape=[
             array((tokens, width), BF16),
             array((tokens, width), F32),
             array((tokens, features), BF16),
+            array((tokens, width), F32),
             array((tokens, 128), F32),
         ],
         in_specs=[smem] + [vmem] * 6 + [any_spec],
-        out_specs=[vmem, vmem, any_spec, vmem],
+        out_specs=[vmem, vmem, any_spec, vmem, vmem],
         scratch_shapes=[
             pltpu.VMEM((stream_count, tokens, width), BF16),
             pltpu.VMEM((tokens, features), BF16),
             pltpu.VMEM((n - 1, tokens, width), BF16),
             pltpu.VMEM((tokens, features), BF16),
-            pltpu.VMEM((tokens, features), BF16),
-            pltpu.VMEM((CHUNK, extent), F32),
-            pltpu.SemaphoreType.DMA,
-            dma(chunks),
         ]
-        + pair()
-        + pair(),
+        + stats_scratch()
+        + [pltpu.VMEM((CHUNK, extent), F32), pltpu.SemaphoreType.DMA, dma(chunks)]
+        + scatter_sems
+        + gather_sems
+        + stats_sems,
         compiler_params=params(1, 48),
     )(coef, queries, keys, values, seg_column, seg_row, w_output, planes)
 
     block = min(256, units)
-    hidden, grad_gate_act, grad_up_act = pl.pallas_call(
+    hidden, grad_acts = pl.pallas_call(
         units_kernel,
         name="units",
+        cost_estimate=lasts(35),
         grid=(units // block,),
-        out_shape=[array((tokens, units), BF16)] * 3,
+        out_shape=[array((tokens, units), BF16), array((tokens, 2 * units), BF16)],
         in_specs=[
             pl.BlockSpec((tokens, features), lambda f: (0, 0)),
             pl.BlockSpec((tokens, features), lambda f: (0, 0)),
@@ -792,25 +997,28 @@
             pl.BlockSpec((features, block), lambda f: (0, f)),
             pl.BlockSpec((block, features), lambda f: (f, 0)),
         ],
-        out_specs=[pl.BlockSpec((tokens, block), lambda f: (0, f))] * 3,
+        out_specs=[pl.BlockSpec((tokens, block), lambda f: (0, f)), any_spec],
+        scratch_shapes=[pltpu.VMEM((2, 2, tokens, block), BF16), dma(2, 2)],
         compiler_params=pltpu.CompilerParams(vmem_limit_bytes=48 * MIB),
     )(normed2, grad_branch2, w_gate, w_up, w_down)
 
-    def over_dp(left, right, dimension):
-        partial = contract_rows(left, right).astype(BF16)
-        return lax.psum_scatter(
-            partial, "dp", scatter_dimension=dimension, tiled=True
-        ).astype(F32)
-
-    grad_w_down = over_dp(hidden, grad_branch2, 1)
-    grad_w_gate = over_dp(normed2, grad_gate_act, 0)
-    grad_w_up = over_dp(normed2, grad_up_act, 0)
+    def over_dp(partial, dimension):
+        return lax.psum_scatter(partial, "dp", scatter_dimension=dimension, tiled=True)
+
+    part_down = contract_rows(hidden, grad_branch2).astype(BF16)
+    part_gate_up = contract_rows(normed2, grad_acts).astype(BF16)
+    grad_down = over_dp(part_down, 1)
+    grad_gate_up = over_dp(part_gate_up, 0)
+    grad_w_down = grad_down.astype(F32)
+    grad_w_gate = grad_gate_up[:, :units].astype(F32)
+    grad_w_up = grad_gate_up[:, units:].astype(F32)
 
     grad_entry2, grad_branch1 = pl.pallas_call(
         functools.partial(units_back_kernel, n),
         name="units_back",
+        cost_estimate=lasts(400),
         out_shape=[array((tokens, width), F32), array((tokens, features), BF16)],
-        in_specs=[smem] + [vmem] * 6 + [any_spec],
+        in_specs=[smem] + [vmem] * 6 + [any_spec] * 3,
         out_specs=[vmem, any_spec],
         scratch_shapes=[
             pltpu.VMEM((stream_count, tokens, width), BF16),
@@ -825,23 +1033,28 @@
             pltpu.SemaphoreType.DMA,
             dma(chunks),
         ]
-        + pair()
-        + pair()
-        + pair(),
-        compiler_params=params(2, 58),
-    )(coef, grad_gate_act, grad_up_act, w_gate, w_up, normed2, scale2, cot_planes)
-
-    grad_query_lin, grad_key_lin, grad_value_lin, branch2, grad_entry1 = pl.pallas_call(
+        + scatter_sems
+        + stats_sems
+        + gather_sems,
+        compiler_params=params(2, 60),
+    )(
+        coef, grad_acts, w_gate, w_up, normed2, stand2, scale2, cot_planes,
+        part_down, part_gate_up,
+    )
+
+    part_output = contract_rows(grad_branch1, attended).astype(BF16)
+
+    grad_lin, branch2, grad_entry1 = pl.pallas_call(
         functools.partial(attend_back_kernel, n),
         name="attend_back",
-        out_shape=[array((tokens, width), BF16)] * 3 + [array((tokens, width), F32)] * 2,
-        in_specs=[vmem] * 13 + [any_spec] * 3,
-        out_specs=[vmem] * 5,
+        cost_estimate=lasts(2),
+        out_shape=[array((tokens, 3 * width), BF16)] + [array((tokens, width), F32)] * 2,
+        in_specs=[vmem] * 14 + [any_spec] * 5,
+        out_specs=[vmem] * 3,
         scratch_shapes=[
             pltpu.VMEM((2, CHUNK, features), BF16),
             pltpu.VMEM((2, CHUNK, units), BF16),
             pltpu.VMEM((2, CHUNK, features), BF16),
-            pltpu.VMEM((tokens, width), BF16),
             pltpu.VMEM((CHUNK, extent), F32),
             pltpu.VMEM((width, tokens), F32),
             pltpu.VMEM((width, tokens), F32),
@@ -855,21 +1068,23 @@
             pltpu.VMEM((chunks, 16, CHUNK), F32),
             pltpu.VMEM((n - 1, chunks, 16, CHUNK), F32),
             dma(3, 2),
-            pltpu.SemaphoreType.DMA,
         ]
-        + pair()
-        + pair()
-        + pair(),
+        + scatter_sems
+        + scatter_sems
+        + stats_sems,
         compiler_params=params(3, 60),
     )(
         queries, keys, values, seg_column, seg_row, cos_table, sin_table,
-        w_output, w_query, w_key, w_value, w_down, scale1, grad_branch1, hidden, normed1,
+        w_output, w_query, w_key, w_value, w_down, stand1, scale1,
+        grad_branch1, hidden, normed1, part_output, grad_down,
     )
 
-    grad_w_output = over_dp(attended, grad_branch1, 1)
-    grad_w_query = over_dp(normed1, grad_query_lin, 0)
-    grad_w_key = over_dp(normed1, grad_key_lin, 0)
-    grad_w_value = over_dp(normed1, grad_value_lin, 0)
+    part_lin = contract_rows(normed1, grad_lin).astype(BF16)
+    grad_lin_w = over_dp(jnp.concatenate([part_lin, part_output], axis=1), 0)
+    grad_w_output = jnp.transpose(grad_lin_w[:, 3 * width :]).astype(F32)
+    grad_w_query, grad_w_key, grad_w_value = (
+        grad_lin_w[:, width * j : width * (j + 1)].astype(F32) for j in range(3)
+    )
 
     rows = 128
     sum_count = 33
@@ -879,20 +1094,21 @@
     new_streams, stream_grad, sums = pl.pallas_call(
         streams_kernel,
         name="streams",
+        cost_estimate=lasts(2),
         grid=(tokens // rows,),
         out_shape=[
             array(streams.shape, BF16),
             array(streams.shape, F32),
             array((sum_count, 8, 128), F32),
         ],
-        in_specs=[smem, plane_spec, plane_spec] + [field_spec] * 4,
+        in_specs=[smem, plane_spec, plane_spec] + [field_spec] * 4 + [any_spec],
         out_specs=[
             stream_spec,
             stream_spec,
             pl.BlockSpec((sum_count, 8, 128), lambda t: (0, 0, 0)),
         ],
         compiler_params=pltpu.CompilerParams(vmem_limit_bytes=48 * MIB),
-    )(coef, planes, cot_planes, branch1, branch2, grad_entry1, grad_entry2)
+    )(coef, planes, cot_planes, branch1, branch2, grad_entry1, grad_entry2, grad_gate_up)
     sums = lax.psum(jnp.sum(sums, axis=(1, 2)), ("dp", "tensor"))
     s_c = sums[0:16].reshape(4, 4)
     s_e1, s_e2, c_b1, c_b2, b_e = sums[16:20], sums[20:24], sums[24:28], sums[28:32], sums[32]

time: 899 us -> 608 us (0.68)
  waiting for transfers between devices: 245 us -> 50.5 us
  Pallas kernels: 479 us -> 400 us
  matrix products: 72.6 us -> 58.6 us
    reduce_scatter x7 -> x3, waiting for transfers between devices: 245 us -> 50.5 us  [over_dp(): lax.psum_scatter(partial, 'dp', scatter_dimension=dimension, tiled=True)]
    pallas_call x4, Pallas kernels: 257 us -> 221 us  [the longest x1 83.1 us: on_device(): pl.pallas_call(functools.partial(project_kernel, n), name='project', cost...]
    pallas_call x1, Pallas kernels: 113 us -> 91.7 us  [on_device(): pl.pallas_call(functools.partial(units_back_kernel, n), name='units_back'...]
    pallas_call x1, Pallas kernels: 109 us -> 87.4 us  [on_device(): pl.pallas_call(functools.partial(attend_back_kernel, n), name='attend_bac...]
    dot_general x7 -> x4, matrix products: 66.5 us -> 52.6 us  [contract_rows(): lax.dot_general(left, right, (((0,), (0,)), ((), ())), preferred_element_...]
    convert_element_type x7 -> x3, other arithmetic: 15.5 us -> 6.35 us  [the longest x1 2.54 us: on_device(): grad_w_up = grad_gate_up[:, units:].astype(F32)]
  transfers between devices with their start and end apart: 7 -> 3, of which waited for: 3 -> 2; matrix products, arithmetic and copies ran while one was open for 9% -> 10% of each run, Pallas kernels for 15% -> 33%
where the time goes in v2:
time: 608 us; the launch traced here: 605 us
  Pallas kernels  400 us (66%)
  matrix products  58.6 us (10%)
  waiting for transfers between devices  50.5 us (8%)
  blocking collectives  39.5 us (6%)
  local copies, waits for them, and re-layouts  23.3 us (4%)
  other arithmetic  18.8 us (3%)
  between operations  14.3 us (2%)
    pallas_call x1, Pallas kernels, on_device(): pl.pallas_call(functools.partial(units_back_kernel, n), name='units_back'...  91.7 us
    pallas_call x1, Pallas kernels, on_device(): pl.pallas_call(functools.partial(attend_back_kernel, n), name='attend_bac...  87.4 us
    pallas_call x1, Pallas kernels, on_device(): pl.pallas_call(functools.partial(project_kernel, n), name='project', cost...  83.1 us
    pallas_call x1, Pallas kernels, on_device(): pl.pallas_call(functools.partial(attend_kernel, n), name='attend', cost_e...  82.2 us
    dot_general x4, matrix products, contract_rows(): lax.dot_general(left, right, (((0,), (0,)), ((), ())), preferred_element_...  52.6 us
    reduce_scatter x3, waiting for transfers between devices, over_dp(): lax.psum_scatter(partial, 'dp', scatter_dimension=dimension, tiled=True)  50.5 us
    psum x1, blocking collectives, on_device(): sums = lax.psum(jnp.sum(sums, axis=(1, 2)), ('dp', 'tensor'))  39.5 us
    pallas_call x1, Pallas kernels, on_device(): pl.pallas_call(units_kernel, name='units', cost_estimate=lasts(35), grid=...  34.9 us
  transfers between devices with their start and end apart: 3, of which 2 were waited for; matrix products, arithmetic and copies ran while one was open for 10% of the time, Pallas kernels for 33%

profile of v2, /device:TPU:0, one launch (start us, length us, event | category | flops | bytes accessed | tf_op | source)
XLA Modules:
  0.0 605.2 jit_solution(3501693330913539671)
XLA Ops:
  7.2 0.0 reduce-scatter.4.cloned.1.call-start
  7.3 0.6 copy-done
  7.9 0.8 fusion.11
  8.7 0.8 convolution_bitcast_fusion.3
  9.5 1.3 multiply_reduce_fusion
  10.8 0.8 convolution_bitcast_fusion.4
  11.6 0.7 convert_element_type.39
  12.3 0.1 reshape.49
  12.4 1.9 fusion.3
  14.3 7.9 %copy_bitcast_fusion = (bf16[4,1024,512]{2,1,0:T(8,128)(2,1)}, bf16[4,1024,512]{2,1,0:T(8,128)(2,1)}) fusion(bf16[1024,4,512]{2,1,0:T(4,128)(2,1)} %param.33, bf16[1024,4,512]{2,1,0:T(4,128)(2,1)} %param.17), kind=kLoop, calls=%fused_computation.4 | loop fusion | bytes 16777216 | tf_op jit(solution)/shard_map/transpose | solution.py:918
  22.2 0.3 pad_maximum_fusion.1
  22.6 1.4 concatenate.12.coef
  24.0 83.1 %project.1 = (bf16[1024,2048]{1,0:T(8,128)(2,1)}, bf16[1024,512]{1,0:T(8,128)(2,1)S(1)}, bf16[1024,512]{1,0:T(8,128)(2,1)S(1)}, bf16[1024,512]{1,0:T(8,128)(2,1)...) custom-call(f32[34]{0:T(128)S(1)} %concatenate.12.coef, ...), custom_call_target="tpu_custom_call" | custom-call | flops 99999997952 | bytes 360000000 | tf_op jit(solution)/shard_map/project/pallas_call | solution.py:928
  107.2 0.8 copy-done.10
  108.0 0.2 broadcast_in_dim.10.segc_ref
  108.2 82.2 %attend.1 = (bf16[1024,512]{1,0:T(8,128)(2,1)S(1)}, f32[1024,512]{1,0:T(8,128)}, bf16[1024,2048]{1,0:T(8,128)(2,1)}, f32[1024,512]{1,0:T(8,128)}, f32[1024,128]{1,0:T(8,128)S(1)}) custom-call(f32[34]{0:T(128)S(1)} %concatenate.12.coef, bf16[1024,512]{1,0:T(8,128)(2,1)S(1)} %get-tuple-element.37.q_ref, bf16[1024,512]{1,0:T(8,128)(2,1)S(1)} %get-tuple-element.38.k_ref, ...), custom_call_target="tpu_custom_call" | custom-call | flops 99999997952 | bytes 360000000 | tf_op jit(solution)/shard_map/attend/pallas_call | solution.py:959
  190.5 34.9 %units.1 = (bf16[1024,2048]{1,0:T(8,128)(2,1)S(1)}, bf16[1024,4096]{1,0:T(8,128)(2,1)}) custom-call(bf16[1024,2048]{1,0:T(8,128)(2,1)} %get-tuple-element.43.normed_ref, bf16[1024,2048]{1,0:T(8,128)(2,1)} %get-tuple-element.44.grad_ref, bf16[2048,2048]{1,0:T(8,128)(2,1)} %wg_ref.3, bf16[2048,2048]{1,0:T(8,128)(2,1)} %wu_ref.3, bf16[2048,2048]{1,0:T(8,128)(2,1)} %wd_ref.3), custom_call_target="tpu_custom_call" | custom-call | flops 35000000512 | bytes 126000000 | tf_op jit(solution)/shard_map/units/pallas_call | solution.py:987
  225.4 2.0 copy-done.1
  227.4 11.8 %convolution_convert_fusion.2._down = bf16[2048,2048]{1,0:T(8,128)(2,1)} fusion(bf16[1024,2048]{1,0:T(8,128)(2,1)S(1)} %get-tuple-element.48.hidden_hbm, bf16[1024,2048]{1,0:T(8,128)(2,1)S(1)} %copy-done.25), kind=kOutput, calls=%fused_computation.3 | convolution fusion | flops 8594128896 | bytes 16777216 | tf_op jit(solution)/shard_map/dot_general | solution.py:27
  239.2 0.0 reduce-scatter.6.cloned.1.call-start
  239.3 24.6 %convolution_convert_fusion._gate_up = bf16[2048,4096]{1,0:T(8,128)(2,1)} fusion(bf16[1024,2048]{1,0:T(8,128)(2,1)} %get-tuple-element.43.normed_ref, bf16[1024,4096]{1,0:T(8,128)(2,1)} %get-tuple-element.45.acts_ref), kind=kOutput, calls=%fused_computation | convolution fusion | flops 17188257792 | bytes 29360128 | tf_op jit(solution)/shard_map/dot_general | solution.py:27
  263.9 0.0 reduce-scatter.8.cloned.1.call-start
  263.9 91.7 %units_back.1 = (f32[1024,512]{1,0:T(8,128)}, bf16[1024,2048]{1,0:T(8,128)(2,1)}) custom-call(f32[34]{0:T(128)} %copy-done.12, bf16[1024,4096]{1,0:T(8,128)(2,1)} %get-tuple-element.45.acts_ref, bf16[2048,2048]{1,0:T(8,128)(2,1)} %wg_ref.3, bf16[2048,2048]{1,0:T(8,128)(2,1)} %wu_ref.3, bf16[1024,2048]{1,0:T(8,128)(2,1)} %get-tuple-element.43.normed_ref, ...), custom_call_target="tpu_custom_call" | custom-call | flops 399999991808 | bytes 1440000000 | tf_op jit(solution)/shard_map/units_back/pallas_call | solution.py:1016
  355.7 4.6 convolution_convert_fusion.3._output
  360.3 2.6 copy.35
  362.9 87.4 %attend_back.1 = (bf16[1024,1536]{1,0:T(8,128)(2,1)}, f32[1024,512]{1,0:T(8,128)}, f32[1024,512]{1,0:T(8,128)}) custom-call(bf16[1024,512]{1,0:T(8,128)(2,1)} %copy-done.7, bf16[1024,512]{1,0:T(8,128)(2,1)} %copy-done.8, bf16[1024,512]{1,0:T(8,128)(2,1)} %copy-done.9, s32[1024,128]{1,0:T(8,128)} %copy-done.4, s32[8,1024]{1,0:T(8,128)} %copy-done.11, ...), custom_call_target="tpu_custom_call" | custom-call | flops 2000000000 | bytes 7200000 | tf_op jit(solution)/shard_map/attend_back/pallas_call | solution.py:1047
  450.4 11.6 %convolution_convert_fusion.1 = bf16[2048,1536]{0,1:T(8,128)(2,1)} fusion(bf16[1024,2048]{1,0:T(8,128)(2,1)} %get-tuple-element.50.normed_hbm, bf16[1024,1536]{1,0:T(8,128)(2,1)} %get-tuple-element.57), kind=kOutput, calls=%fused_computation.2 | convolution fusion | flops 6445596672 | bytes 13631488 | tf_op jit(solution)/shard_map/dot_general | solution.py:27
  462.0 7.9 %pad_maximum_fusion = bf16[2048,2048]{0,1:T(8,128)(2,1)} fusion(bf16[2048,512]{0,1:T(8,128)(2,1)S(1)} %copy-done.17, bf16[2048,1536]{0,1:T(8,128)(2,1)} %convolution_convert_fusion.1), kind=kLoop, calls=%fused_computation.1 | loop fusion | flops 16777216 | bytes 16777216 | tf_op jit(solution)/shard_map/concatenate | solution.py:1083
  470.0 28.2 %reduce-scatter.6.cloned.1.call-done._gate_up = bf16[256,4096]{1,0:T(8,128)(2,1)} async-done(((bf16[2048,4096]{1,0:T(8,128)(2,1)}), bf16[256,4096]{1,0:T(8,128)(2,1)}) %reduce-scatter.6.cloned.1.call-update) | async-done | bytes 2097168 | tf_op jit(solution)/shard_map/reduce_scatter | solution.py:1006
  498.3 1.6 copy-done.6
  499.9 20.6 %streams.1 = (bf16[1024,4,512]{2,1,0:T(4,128)(2,1)}, f32[1024,4,512]{2,1,0:T(4,128)}, f32[33,8,128]{2,1,0:T(8,128)S(1)}) custom-call(f32[34]{0:T(128)S(1)} %copy-done.13, bf16[4,1024,512]{2,1,0:T(8,128)(2,1)} %get-tuple-element.90.s_hbm.s_ref, bf16[4,1024,512]{2,1,0:T(8,128)(2,1)} %get-tuple-element.89.c_hbm.c_ref, f32[1024,512]{1,0:T(8,128)S(1)} %copy-done.5, ...), custom_call_target="tpu_custom_call" | custom-call | flops 2000000000 | bytes 7200000 | tf_op jit(solution)/shard_map/streams/pallas_call | solution.py:1094
  520.5 0.3 reduce_sum.9
  520.8 1.5 convert_element_type.51
  522.3 39.5 %psum.7 = f32[33]{0:T(128)S(1)} all-reduce(f32[33]{0:T(128)S(1)} %reduce_sum.9), channel_id=1, replica_groups=mesh['dp'=8,'tensor'=4] {'dp','tensor'}, use_global_device_ids=true, to_apply=%region_4.0 | all-reduce | flops 33 | bytes 264 | tf_op jit(solution)/shard_map/psum | solution.py:1112
  561.8 0.6 slice.46
  562.4 0.1 reshape.50
  562.5 0.6 fusion.10
  563.1 0.2 fusion
  563.2 0.7 copy.39
  563.9 1.4 fusion.2
  565.3 1.4 fusion.1
  566.6 0.7 convolution_add_fusion
  567.4 22.2 %reduce-scatter.8.cloned.1.call-done = bf16[256,2048]{0,1:T(8,128)(2,1)} async-done(((bf16[2048,2048]{0,1:T(8,128)(2,1)}), bf16[256,2048]{0,1:T(8,128)(2,1)}) %reduce-scatter.8.cloned.1.call-update) | async-done | bytes 1048592 | tf_op jit(solution)/shard_map/reduce_scatter | solution.py:1006
  589.6 2.3 convert_bitcast_fusion
  591.9 2.0 copy.36
  593.9 1.0 copy.37
  594.9 1.0 copy.38
  595.9 2.5 slice_convert_fusion
  (54 shorter events, 0.2 us)
Async XLA Ops:
  7.2 0.7 copy-start
  7.2 355.7 %reduce-scatter.4.cloned.1.call-start = ((), (), s32[]{:S(2)}) async-start(), calls=%async_computation.3 | async-start | bytes 9437184 | tf_op jit(solution)/shard_map/reduce_scatter | solution.py:1006
  14.3 8.3 %copy-start.21 = (f32[4]{0:T(128)S(1)}, f32[4]{0:T(128)}, u32[]{:S(2)}) copy-start(f32[4]{0:T(128)} %param.20) | copy-start | bytes 52
  14.3 8.3 %copy-start.22 = (f32[4]{0:T(128)S(1)}, f32[4]{0:T(128)}, u32[]{:S(2)}) copy-start(f32[4]{0:T(128)} %param.25) | copy-start | bytes 52
  22.5 84.6 %copy-start.2 = (f32[1024,128]{1,0:T(8,128)}, f32[1024,128]{1,0:T(8,128)S(1)}, u32[]{:S(2)}) copy-start(f32[1024,128]{1,0:T(8,128)S(1)} %get-tuple-element.87.cos_ref) | copy-start | bytes 1572868
  22.5 84.6 %copy-start.3 = (f32[1024,128]{1,0:T(8,128)}, f32[1024,128]{1,0:T(8,128)S(1)}, u32[]{:S(2)}) copy-start(f32[1024,128]{1,0:T(8,128)S(1)} %get-tuple-element.88.sin_ref) | copy-start | bytes 1572868
  24.0 84.2 %copy-start.12 = (f32[34]{0:T(128)}, f32[34]{0:T(128)S(1)}, u32[]{:S(2)}) copy-start(f32[34]{0:T(128)S(1)} %concatenate.12.coef) | copy-start | bytes 412
  24.0 84.0 %copy-start.19 = (s32[1024]{0:T(1024)S(1)}, s32[1024]{0:T(1024)}, u32[]{:S(2)}) copy-start(s32[1024]{0:T(1024)} %param.18) | copy-start | bytes 12292
  107.1 0.8 copy-start.10
  107.9 82.5 %copy-start.7 = (bf16[1024,512]{1,0:T(8,128)(2,1)}, bf16[1024,512]{1,0:T(8,128)(2,1)S(1)}, u32[]{:S(2)}) copy-start(bf16[1024,512]{1,0:T(8,128)(2,1)S(1)} %get-tuple-element.37.q_ref) | copy-start | bytes 3145732
  107.9 82.5 %copy-start.8 = (bf16[1024,512]{1,0:T(8,128)(2,1)}, bf16[1024,512]{1,0:T(8,128)(2,1)S(1)}, u32[]{:S(2)}) copy-start(bf16[1024,512]{1,0:T(8,128)(2,1)S(1)} %get-tuple-element.38.k_ref) | copy-start | bytes 3145732
  107.9 82.5 %copy-start.9 = (bf16[1024,512]{1,0:T(8,128)(2,1)}, bf16[1024,512]{1,0:T(8,128)(2,1)S(1)}, u32[]{:S(2)}) copy-start(bf16[1024,512]{1,0:T(8,128)(2,1)S(1)} %get-tuple-element.39.v_ref) | copy-start | bytes 3145732
  108.2 82.3 %copy-start.4 = (s32[1024,128]{1,0:T(8,128)}, s32[1024,128]{1,0:T(8,128)S(1)}, u32[]{:S(2)}) copy-start(s32[1024,128]{1,0:T(8,128)S(1)} %broadcast_in_dim.10.segc_ref) | copy-start | bytes 1572868
  108.2 82.3 %copy-start.11 = (s32[8,1024]{1,0:T(8,128)}, s32[8,1024]{1,0:T(8,128)S(1)}, u32[]{:S(2)}) copy-start(s32[8,1024]{1,0:T(8,128)S(1)} %broadcast_in_dim.11.segr_ref) | copy-start | bytes 98308
  190.5 35.0 %copy-start.14 = (f32[1024,128]{1,0:T(8,128)}, f32[1024,128]{1,0:T(8,128)S(1)}, u32[]{:S(2)}) copy-start(f32[1024,128]{1,0:T(8,128)S(1)} %get-tuple-element.47.scale_ref) | copy-start | bytes 1572868
  190.5 37.0 %copy-start.25 = (bf16[1024,2048]{1,0:T(8,128)(2,1)S(1)}, bf16[1024,2048]{1,0:T(8,128)(2,1)}, u32[]{:S(2)}) copy-start(bf16[1024,2048]{1,0:T(8,128)(2,1)} %get-tuple-element.44.grad_ref) | copy-start | bytes 12582916
  225.4 2.0 copy-start.1
  239.2 259.0 %reduce-scatter.6.cloned.1.call-start = ((), (), s32[]{:S(2)}) async-start(), calls=%async_computation.4 | async-start | bytes 18874368 | tf_op jit(solution)/shard_map/reduce_scatter | solution.py:1006
  263.9 325.7 %reduce-scatter.8.cloned.1.call-start = ((), (), s32[]{:S(2)}) async-start(), calls=%async_computation.5 | async-start | bytes 9437184 | tf_op jit(solution)/shard_map/reduce_scatter | solution.py:1006
  360.3 2.6 copy-start.15
  450.4 11.7 %copy-start.17 = (bf16[2048,512]{0,1:T(8,128)(2,1)S(1)}, bf16[2048,512]{0,1:T(8,128)(2,1)}, u32[]{:S(2)}) copy-start(bf16[2048,512]{0,1:T(8,128)(2,1)} %copy.35) | copy-start | bytes 6291460
  470.0 28.3 %copy-start.5 = (f32[1024,512]{1,0:T(8,128)S(1)}, f32[1024,512]{1,0:T(8,128)}, u32[]{:S(2)}) copy-start(f32[1024,512]{1,0:T(8,128)} %get-tuple-element.40.b1_ref) | copy-start | bytes 6291460
  470.0 28.3 %copy-start.13 = (f32[34]{0:T(128)S(1)}, f32[34]{0:T(128)}, u32[]{:S(2)}) copy-start(f32[34]{0:T(128)} %copy-done.12) | copy-start | bytes 412
  498.3 1.6 copy-start.6
  499.8 20.9 %copy-start.18 = (bf16[2048,256]{1,0:T(8,128)(2,1)S(1)}, bf16[2048,256]{1,0:T(8,128)(2,1)}, u32[]{:S(2)}) copy-start(bf16[2048,256]{1,0:T(8,128)(2,1)} %reduce-scatter.4.cloned.1.call-done._down) | copy-start | bytes 3145732
  499.8 63.2 %copy-start.23 = (f32[4]{0:T(128)S(1)}, f32[4]{0:T(128)}, u32[]{:S(2)}) copy-start(f32[4]{0:T(128)} %param.22) | copy-start | bytes 52
  499.8 65.4 %copy-start.20 = (f32[4,4]{1,0:T(4,128)S(1)}, f32[4,4]{1,0:T(4,128)}, u32[]{:S(2)}) copy-start(f32[4,4]{1,0:T(4,128)} %param.24) | copy-start | bytes 196
  499.8 65.4 %copy-start.24 = (f32[4]{0:T(128)S(1)}, f32[4]{0:T(128)}, u32[]{:S(2)}) copy-start(f32[4]{0:T(128)} %param.23) | copy-start | bytes 52
  520.8 75.1 %copy-start.16 = (bf16[256,4096]{1,0:T(8,128)(2,1)S(1)}, bf16[256,4096]{1,0:T(8,128)(2,1)}, u32[]{:S(2)}) copy-start(bf16[256,4096]{1,0:T(8,128)(2,1)} %reduce-scatter.6.cloned.1.call-done._gate_up) | copy-start | bytes 6291460
Sparse Core Ops, SparseCore 0:
  239.3 89.8 reduce-scatter.3
  331.6 166.5 reduce-scatter.5
  500.5 88.9 reduce-scatter.7

commit v3 on v2

--- a/solution.py
+++ b/solution.py
@@ -1,4 +1,5 @@
 import functools
+import math
 
 import jax
 import jax.numpy as jnp
@@ -20,7 +21,27 @@
 ROWS = 32
 MIB = 1 << 20
 
-IN1, OUT2, ENTRY, ENTRY_B, BRANCH, BRANCH_E, MIXED = 0, 4, 8, 12, 13, 17, 18
+
+def inner(left, right):
+    total = left[0] * right[0]
+    for a, b in zip(left[1:], right[1:]):
+        total += a * b
+    return total
+
+
+class Mixing:
+    def __init__(self, refs):
+        vectors = [[ref[i] for i in range(4)] for ref in refs[:4]]
+        self.in1, self.out1, self.in2, self.out2 = vectors
+        self.res1, self.res2 = (
+            [[ref[i, j] for j in range(4)] for i in range(4)] for ref in refs[4:]
+        )
+        self.entry = [inner(row, self.in2) for row in self.res1]
+        self.branch = [inner(self.out1, column) for column in zip(*self.res2)]
+        self.across = inner(self.out1, self.in2)
+
+    def mixed(self, k, j):
+        return inner(self.res1[k], [row[j] for row in self.res2])
 
 
 def contract_rows(left, right):
@@ -338,60 +359,76 @@
     return field * cos_rows + (sign * turned) * sin_rows
 
 
+def spread(row):
+    share = jnp.full((8, 128), 0.125, F32)
+    return lax.dot_general(
+        jnp.broadcast_to(row, (8, 128)),
+        share,
+        (((0,), (0,)), ((), ())),
+        precision=PRECISE,
+        preferred_element_type=F32,
+    )
+
+
 def project_kernel(
-    n, coef, cos_ref, sin_ref, s_hbm, c_hbm, wq_hbm, wk_hbm, wv_hbm,
-    normed_hbm, q_ref, k_ref, v_ref, stand_ref, scale_ref, gb2_hbm,
-    s_buf, c_buf, w_buf, all1, all2, first, second, mine, others, in_sem, w_sem, out_sem,
-    send1, recv1, send2, recv2, send3, recv3,
+    n, in1, out2, positions_ref, segments_ref, s_hbm, c_hbm, wq_hbm, wk_hbm, wv_hbm,
+    normed_hbm, q_ref, k_ref, v_ref, stand_ref, scale_ref, gb2_hbm, planes_hbm, cot_hbm,
+    cos_ref, sin_ref, segc_ref, segr_ref,
+    s_buf, c_buf, planes, cot_planes, w_buf, all1, all2, first, second, mine, others,
+    in_sem, w_sem, out_sem, send1, recv1, send2, recv2, send3, recv3,
 ):
-    _, tokens, width = s_buf.shape
+    tokens, streams, width = s_buf.shape
     count = tokens // CHUNK
     heads = width // HEAD
     weights = (wq_hbm, wk_hbm, wv_hbm)
 
     def s_in(c):
         return pltpu.make_async_copy(
-            s_hbm.at[:, chunk_rows(c)], s_buf.at[:, chunk_rows(c)], in_sem.at[0, c]
+            s_hbm.at[chunk_rows(c)], s_buf.at[chunk_rows(c)], in_sem.at[0, c]
         )
 
     def c_in(c):
         return pltpu.make_async_copy(
-            c_hbm.at[:, chunk_rows(c)], c_buf.at[:, chunk_rows(c)], in_sem.at[1, c]
+            c_hbm.at[chunk_rows(c)], c_buf.at[chunk_rows(c)], in_sem.at[1, c]
         )
 
     def w_in(j):
         return pltpu.make_async_copy(weights[j], w_buf.at[j], w_sem.at[j])
 
-    def normed_out(c):
-        return pltpu.make_async_copy(
-            all1.at[chunk_rows(c)], normed_hbm.at[chunk_rows(c)], out_sem.at[0, c]
-        )
-
-    def gb2_out(c):
-        return pltpu.make_async_copy(
-            all2.at[chunk_rows(c)], gb2_hbm.at[chunk_rows(c)], out_sem.at[1, c]
-        )
-
+    def out(c, i):
+        rows = chunk_rows(c)
+        source, target = (
+            (all1.at[rows], normed_hbm.at[rows]),
+            (all2.at[rows], gb2_hbm.at[rows]),
+            (planes.at[:, rows], planes_hbm.at[:, rows]),
+            (cot_planes.at[:, rows], cot_hbm.at[:, rows]),
+        )[i]
+        return pltpu.make_async_copy(source, target, out_sem.at[i, c])
+
+    c_in(0).start()
     loop(count, lambda c: s_in(c).start())
+    loop(count - 1, lambda c: c_in(c + 1).start())
     for j in range(3):
         w_in(j).start()
-    loop(count, lambda c: c_in(c).start())
     gather = Gather(n, all1, width, send1, recv1)
     incoming = Gather(n, all2, width, send2, recv2)
     stats = Stats(n, mine, others, send3, recv3)
     enter(n, gather.to)
 
-    def mix(buf, base, rows):
-        total = coef[base] * buf[0, rows].astype(F32)
-        for i in range(1, buf.shape[0]):
-            total += coef[base + i] * buf[i, rows].astype(F32)
+    def mix(buf, weight, target, rows):
+        block = buf[rows].astype(F32)
+        total = None
+        for i in range(streams):
+            field = block[:, i, :]
+            target[i, rows] = field.astype(BF16)
+            total = weight[i] * field if total is None else total + weight[i] * field
         return total
 
     def entry(c):
         s_in(c).wait()
 
         def piece(r):
-            field = mix(s_buf, IN1, sub_rows(c, r))
+            field = mix(s_buf, in1, planes, sub_rows(c, r))
             stand_ref[sub_rows(c, r), :] = field
             fold_entry(field, first, second, local_rows(r))
 
@@ -402,6 +439,18 @@
     def send(c):
         standardize(c, stats, gather, first, second, stand_ref, scale_ref)
 
+    def grad(c):
+        c_in(c).wait()
+
+        def piece(r):
+            rows = sub_rows(c, r)
+            all2[rows, incoming.own()] = mix(c_buf, out2, cot_planes, rows).astype(BF16)
+
+        loop(CHUNK // ROWS, piece)
+        incoming.start(c)
+        out(c, 3).start()
+
+    grad(0)
     entry(0)
 
     def ahead(c):
@@ -409,20 +458,33 @@
         send(c)
 
     loop(count - 1, ahead)
+    grad(1)
     send(count - 1)
+    loop(count - 2, lambda c: grad(c + 2))
+
+    segr_ref[...] = jnp.concatenate(
+        [
+            jnp.broadcast_to(segments_ref[a : a + 1, :].astype(F32), (8, 128))
+            for a in range(tokens // 128)
+        ],
+        axis=1,
+    )
+    lane = lax.broadcasted_iota(jnp.int32, (128, 128), 1)
+    exponent = lax.rem(lane, HEAD // 2).astype(F32) * (-2.0 / HEAD * math.log(10000.0))
+    inverse = jnp.exp(exponent)
+    for a in range(tokens // 128):
+        rows = slice(128 * a, 128 * (a + 1))
+        segc_ref[rows, :] = spread(segments_ref[a : a + 1, :].astype(F32))
+        angles = spread(positions_ref[a : a + 1, :].astype(F32)) * inverse
+        cos_ref[rows, :] = jnp.cos(angles)
+        sine = jnp.sin(angles)
+        sin_ref[rows, :] = jnp.where(lane < HEAD // 2, -sine, sine)
     for j in range(3):
         w_in(j).wait()
 
     def work(c):
-        c_in(c).wait()
-
-        def piece(r):
-            rows = sub_rows(c, r)
-            all2[rows, incoming.own()] = mix(c_buf, OUT2, rows).astype(BF16)
-
-        loop(CHUNK // ROWS, piece)
-        incoming.start(c)
-        normed_out(c).start()
+        for i in (0, 2):
+            out(c, i).start()
         rows = chunk_rows(c)
         block = all1[rows, :]
         cos_rows, sin_rows = cos_ref[rows, :], sin_ref[rows, :]
@@ -432,13 +494,19 @@
                 place = slice(HEAD * h, HEAD * (h + 1))
                 target[rows, place] = rotate(lin[:, place], cos_rows, sin_rows, 1.0).astype(BF16)
         v_ref[rows, :] = dot_nn(block, w_buf[2]).astype(BF16)
+        incoming.relay(c)
 
     gather.take(count, work)
-    incoming.take(count, lambda c: gb2_out(c).start())
+
+    def end(c):
+        incoming.arrive(c)
+        out(c, 1).start()
+
+    loop(count, end)
 
     def drain(c):
-        gb2_out(c).wait()
-        normed_out(c).wait()
+        for i in range(4):
+            out(c, i).wait()
         stats.finish(c)
         gather.finish(c)
         incoming.finish(c)
@@ -464,16 +532,56 @@
 
 
 def attend_kernel(
-    n, coef, q_ref, k_ref, v_ref, segc_ref, segr_ref, wo_ref, s_hbm,
-    attended_ref, branch_ref, normed_hbm, stand_ref, scale_ref,
-    s_buf, part, came, all2, first, second, mine, others, bias, in_sem, out_sem,
-    send1, recv1, send2, recv2, send3, recv3,
+    n, in1, out1, in2, out2, res1, res2, q_ref, k_ref, v_ref, segc_ref, segr_ref, wo_ref,
+    s_hbm, gb2_hbm, wg_hbm, wu_hbm, wd_hbm,
+    attended_ref, branch_ref, normed_hbm, stand_ref, scale_ref, hidden_hbm, acts_hbm,
+    s_buf, gb2_buf, wg_buf, wu_buf, wd_buf, hidden_buf, gate_buf, up_buf,
+    part, came, all2, first, second, mine, others, bias,
+    s_sem, gb2_sem, w_sem, normed_sem, out_sem, send1, recv1, send2, recv2, send3, recv3,
 ):
     tokens, width = q_ref.shape
+    units = wg_buf.shape[1]
     count = tokens // CHUNK
     heads = width // HEAD
-    s_in = pltpu.make_async_copy(s_hbm, s_buf, in_sem)
-    s_in.start()
+    block = min(units, 512)
+    mixing = Mixing((in1, out1, in2, out2, res1, res2))
+
+    def s_in(c):
+        slot = lax.rem(c, 2)
+        return pltpu.make_async_copy(s_hbm.at[:, chunk_rows(c)], s_buf.at[slot], s_sem.at[slot])
+
+    def gb2_in(c):
+        slot = lax.rem(c, 2)
+        return pltpu.make_async_copy(gb2_hbm.at[chunk_rows(c)], gb2_buf.at[slot], gb2_sem.at[slot])
+
+    def normed_out(c):
+        return pltpu.make_async_copy(
+            all2.at[chunk_rows(c)], normed_hbm.at[chunk_rows(c)], normed_sem.at[c]
+        )
+
+    def outs(c):
+        slot, rows = lax.rem(c, 2), chunk_rows(c)
+        return tuple(
+            pltpu.make_async_copy(buf.at[slot], target, out_sem.at[i, slot])
+            for i, (buf, target) in enumerate(
+                (
+                    (hidden_buf, hidden_hbm.at[rows]),
+                    (gate_buf, acts_hbm.at[rows, 0:units]),
+                    (up_buf, acts_hbm.at[rows, units : 2 * units]),
+                )
+            )
+        )
+
+    weights = tuple(
+        pltpu.make_async_copy(source, target, w_sem.at[i])
+        for i, (source, target) in enumerate(
+            ((wg_hbm, wg_buf), (wu_hbm, wu_buf), (wd_hbm, wd_buf))
+        )
+    )
+    s_in(0).start()
+    gb2_in(0).start()
+    for copy in weights:
+        copy.start()
     scatter = Scatter(n, part, came, width, send1, recv1)
     gather = Gather(n, all2, width, send2, recv2)
     stats = Stats(n, mine, others, send3, recv3)
@@ -492,26 +600,23 @@
             probs = (raised * inverse).astype(BF16)
             attended_ref[rows, place] = dot_nn(probs, v_ref[pl.ds(start, extent), place]).astype(BF16)
         part[rows, :] = dot_nn(attended_ref[rows, :], wo_ref[...]).astype(BF16)
-        scatter.start(c)
-
-        @pl.when(c >= 1)
+
+    def middle(c):
+        @pl.when(c + 1 < count)
         def _():
-            scatter.relay(c - 1)
-
-    loop(count, attend)
-    scatter.relay(count - 1)
-    s_in.wait()
-
-    def middle(c):
+            s_in(c + 1).start()
+
+        s_in(c).wait()
+        slot = lax.rem(c, 2)
         scatter.arrive(c)
 
         def piece(r):
             rows = sub_rows(c, r)
             branch = scatter.total(rows)
             branch_ref[rows, :] = branch
-            entry = coef[ENTRY_B] * branch
-            for i in range(s_buf.shape[0]):
-                entry += coef[ENTRY + i] * s_buf[i, rows].astype(F32)
+            entry = mixing.across * branch
+            for i in range(s_buf.shape[1]):
+                entry += mixing.entry[i] * s_buf[slot, i, local_rows(r)].astype(F32)
             stand_ref[rows, :] = entry
             fold_entry(entry, first, second, local_rows(r))
 
@@ -522,21 +627,81 @@
     def send(c):
         standardize(c, stats, gather, first, second, stand_ref, scale_ref)
 
+    def work(c):
+        normed_out(c).start()
+        slot = lax.rem(c, 2)
+
+        @pl.when(c + 1 < count)
+        def _():
+            gb2_in(c + 1).start()
+
+        @pl.when(c >= 2)
+        def _():
+            for copy in outs(c - 2):
+                copy.wait()
+
+        gb2_in(c).wait()
+
+        def piece(f):
+            place = columns(f, block)
+            gate = dot_nn(all2[chunk_rows(c), :], wg_buf[:, place])
+            up = dot_nn(all2[chunk_rows(c), :], wu_buf[:, place])
+            grad = dot_nt(gb2_buf[slot], wd_buf[place, :])
+            sig = jax.nn.sigmoid(gate)
+            act = gate * sig
+            hidden_buf[slot, :, place] = (act * up).astype(BF16)
+            gate_buf[slot, :, place] = (grad * up * sig * (1.0 + gate * (1.0 - sig))).astype(BF16)
+            up_buf[slot, :, place] = (grad * act).astype(BF16)
+
+        loop(units // block, piece)
+        for copy in outs(c):
+            copy.start()
+
+    def attend_send(c):
+        attend(c)
+        scatter.start(c)
+
+        @pl.when(c >= 1)
+        def _():
+            scatter.relay(c - 1)
+
+    end = count - 1
+    loop(end, attend_send)
     middle(0)
+    attend(end)
+    send(0)
+    scatter.start(end)
+    scatter.relay(end - 1)
 
     def ahead(c):
-        middle(c + 1)
+        middle(c)
         send(c)
 
-    loop(count - 1, ahead)
-    send(count - 1)
-
-    def normed_out(c):
-        return pltpu.make_async_copy(
-            all2.at[chunk_rows(c)], normed_hbm.at[chunk_rows(c)], out_sem.at[c]
-        )
-
-    gather.take(count, lambda c: normed_out(c).start())
+    loop(end - 2, lambda c: ahead(c + 1))
+    scatter.relay(end)
+    middle(end - 1)
+    gather.relay(0)
+    send(end - 1)
+    for copy in weights:
+        copy.wait()
+    gather.arrive(0)
+    work(0)
+    middle(end)
+    gather.relay(1)
+    send(end)
+
+    def rest(c):
+        gather.arrive(c)
+        work(c)
+
+        @pl.when(c + 1 < count)
+        def _():
+            gather.relay(c + 1)
+
+    loop(end, lambda c: rest(c + 1))
+    for c in range(max(count - 2, 0), count):
+        for copy in outs(c):
+            copy.wait()
 
     def drain(c):
         normed_out(c).wait()
@@ -545,49 +710,6 @@
         gather.finish(c)
 
     loop(count, drain)
-
-
-def units_kernel(
-    normed_ref, grad_ref, wg_ref, wu_ref, wd_ref, hidden_ref, acts_hbm, buf, sem
-):
-    step, steps = pl.program_id(0), pl.num_programs(0)
-    slot = lax.rem(step, 2)
-    width = buf.shape[3]
-
-    def out(at, part):
-        place = (part * steps + at) * width
-        return pltpu.make_async_copy(
-            buf.at[lax.rem(at, 2), part],
-            acts_hbm.at[:, pl.ds(pl.multiple_of(place, width), width)],
-            sem.at[lax.rem(at, 2), part],
-        )
-
-    @pl.when(step >= 2)
-    def _():
-        out(step - 2, 0).wait()
-        out(step - 2, 1).wait()
-
-    block = normed_ref[...]
-    gate = dot_nn(block, wg_ref[...])
-    up = dot_nn(block, wu_ref[...])
-    grad = dot_nt(grad_ref[...], wd_ref[...])
-    sig = jax.nn.sigmoid(gate)
-    act = gate * sig
-    hidden_ref[...] = (act * up).astype(BF16)
-    buf[slot, 0] = (grad * up * sig * (1.0 + gate * (1.0 - sig))).astype(BF16)
-    buf[slot, 1] = (grad * act).astype(BF16)
-    out(step, 0).start()
-    out(step, 1).start()
-
-    @pl.when(step == steps - 1)
-    def _():
-        @pl.when(step >= 1)
-        def _():
-            out(step - 1, 0).wait()
-            out(step - 1, 1).wait()
-
-        out(step, 0).wait()
-        out(step, 1).wait()
 
 
 def stats_part(part32, normed, normed_rows, part, c, first, second):
@@ -602,7 +724,7 @@
 
 
 def units_back_kernel(
-    n, coef, acts_ref, wg_ref, wu_ref, normed_ref, stand_ref, scale_ref, c_hbm, _down, _gate_up,
+    n, in1, out1, in2, out2, res1, res2, acts_ref, wg_ref, wu_ref, normed_ref, stand_ref, scale_ref, c_hbm, _down, _gate_up,
     entry_ref, gb1_hbm,
     c_buf, part32, first, second, part, came, mine, others, all1, in_sem, out_sem,
     send1, recv1, send2, recv2, send3, recv3,
@@ -610,6 +732,7 @@
     tokens, features = normed_ref.shape
     width = entry_ref.shape[1]
     count = tokens // CHUNK
+    mixing = Mixing((in1, out1, in2, out2, res1, res2))
     c_in = pltpu.make_async_copy(c_hbm, c_buf, in_sem)
     c_in.start()
     scatter = Scatter(n, part, came, width, send1, recv1)
@@ -650,9 +773,9 @@
                 - standard * repeat_lanes(second[local, :], width)
             )
             entry_ref[rows, :] = entry
-            grad = coef[BRANCH_E] * entry
+            grad = mixing.across * entry
             for i in range(c_buf.shape[0]):
-                grad += coef[BRANCH + i] * c_buf[i, rows].astype(F32)
+                grad += mixing.branch[i] * c_buf[i, rows].astype(F32)
             all1[rows, gather.own()] = grad.astype(BF16)
 
         loop(CHUNK // ROWS, piece)
@@ -801,13 +924,15 @@
 
 
 def streams_kernel(
-    coef, s_ref, c_ref, b1_ref, b2_ref, e1_ref, e2_ref, _gate_up, new_ref, grad_ref, sums_ref
+    in1, out1, in2, out2, res1, res2, s_ref, c_ref, b1_ref, b2_ref, e1_ref, e2_ref, new_ref, grad_ref, sums_ref
 ):
     @pl.when(pl.program_id(0) == 0)
     def _():
         sums_ref[...] = jnp.zeros_like(sums_ref)
 
     count = s_ref.shape[0]
+    mixing = Mixing((in1, out1, in2, out2, res1, res2))
+    mixed = [[mixing.mixed(k, j) for j in range(count)] for k in range(count)]
 
     def fold(field):
         field = fold_lanes(field)
@@ -822,11 +947,11 @@
         c = [c_ref[i, rows].astype(F32) for i in range(count)]
         b1, b2, e1, e2 = b1_ref[rows, :], b2_ref[rows, :], e1_ref[rows, :], e2_ref[rows, :]
         for j in range(count):
-            new = coef[BRANCH + j] * b1 + coef[OUT2 + j] * b2
-            grad = coef[ENTRY + j] * e2 + coef[IN1 + j] * e1
+            new = mixing.branch[j] * b1 + mixing.out2[j] * b2
+            grad = mixing.entry[j] * e2 + mixing.in1[j] * e1
             for k in range(count):
-                new += coef[MIXED + count * k + j] * s[k]
-                grad += coef[MIXED + count * j + k] * c[k]
+                new += mixed[k][j] * s[k]
+                grad += mixed[j][k] * c[k]
             new_ref[rows, j, :] = new.astype(BF16)
             grad_ref[rows, j, :] = grad
         pairs = [(s[i], c[j]) for i in range(count) for j in range(count)]
@@ -839,8 +964,208 @@
     loop(s_ref.shape[1] // 16, piece)
 
 
+PLANES = 4
+CORES = 2
+SUMS = 33
+SUM_ROWS = 40
+
+
+def finish_kernel(
+    n, first_hbm, last_hbm, sums_ref,
+    q_out, k_out, v_out, o_out, sums_out,
+    own, core, right, left, by_core, by_plane, by_tensor,
+    own_sem, core_send, core_recv, right_send, right_recv, left_send, left_recv, sum_send, sum_recv,
+):
+    _, pieces, height, width = own.shape
+    me = lax.axis_index("dp")
+    plane, mine = lax.div(me, CORES), lax.rem(me, CORES)
+    partner = me + 1 - 2 * mine
+    here, peers, peer_source = partners(n)
+    planes_to = [lax.rem(plane + k, PLANES) for k in range(1, PLANES)]
+    planes_from = [lax.rem(plane + PLANES - k, PLANES) for k in range(1, PLANES)]
+
+    def dp_at(position):
+        return position * CORES + mine
+
+    def rows_of(position, half):
+        return pl.ds(pl.multiple_of((position * CORES + half) * height, height), height)
+
+    def block(position, half, p):
+        if p < pieces - 1:
+            return first_hbm.at[rows_of(position, half), p * width : (p + 1) * width]
+        return last_hbm.at[rows_of(position, half)]
+
+    def over_dp(source, target, send_sem, recv_sem, device):
+        return pltpu.make_async_remote_copy(
+            src_ref=source, dst_ref=target, send_sem=send_sem, recv_sem=recv_sem,
+            device_id={"dp": device}, device_id_type=MESH,
+        )
+
+    def own_in(position, p):
+        return pltpu.make_async_copy(
+            block(position, mine, p), own.at[position, p], own_sem.at[position, p]
+        )
+
+    def core_in(position, p):
+        return over_dp(
+            block(position, 1 - mine, p), core.at[position, p],
+            core_send.at[position, p], core_recv.at[position, p], partner,
+        )
+
+    def rightward(step, p):
+        return over_dp(
+            own.at[lax.rem(plane + PLANES - step, PLANES), p], right.at[step - 1, p],
+            right_send.at[step - 1, p], right_recv.at[step - 1, p], lax.rem(me + CORES, PLANES * CORES),
+        )
+
+    def leftward(step, p):
+        return over_dp(
+            own.at[lax.rem(plane + step, PLANES), p], left.at[step - 1, p],
+            left_send.at[step - 1, p], left_recv.at[step - 1, p],
+            lax.rem(me + (PLANES - 1) * CORES, PLANES * CORES),
+        )
+
+    order = (3, 0, 2, 1)
+    for position in order:
+        for p in range(pieces):
+            own_in(position, p).start()
+
+    barrier = pltpu.get_barrier_semaphore()
+    pl.semaphore_signal(barrier, inc=1, device_id={"dp": partner}, device_id_type=MESH)
+    for k in range(PLANES - 1):
+        pl.semaphore_signal(
+            barrier, inc=1, device_id={"dp": dp_at(planes_to[k])}, device_id_type=MESH
+        )
+    for k in range(n - 1):
+        pl.semaphore_signal(barrier, inc=1, device_id={"tensor": peers[k]}, device_id_type=MESH)
+    pl.semaphore_wait(barrier, 1 + PLANES - 1 + n - 1)
+
+    by_core[mine] = jnp.zeros((SUM_ROWS, 128), F32)
+    by_core[mine, 0:SUMS] = jnp.sum(sums_ref[...], axis=1)
+    over_dp(
+        by_core.at[mine], by_core.at[mine], sum_send.at[0], sum_recv.at[0], partner
+    ).start()
+    for position in order:
+        for p in range(pieces):
+            core_in(position, p).start()
+    over_dp(
+        by_core.at[1 - mine], by_core.at[1 - mine], sum_send.at[0], sum_recv.at[0], partner
+    ).wait_recv()
+    by_plane[plane] = by_core[0] + by_core[1]
+
+    def plane_sums(k, at):
+        return over_dp(
+            by_plane.at[at], by_plane.at[at], sum_send.at[1 + k], sum_recv.at[1 + k],
+            dp_at(planes_to[k]),
+        )
+
+    def tensor_sums(k, at):
+        at = by_tensor.at[at]
+        return remote(at, at, sum_send.at[PLANES + k], sum_recv.at[PLANES + k], peers[k])
+
+    for k in range(PLANES - 1):
+        plane_sums(k, plane).start()
+
+    def gather_pair(position):
+        def piece(p):
+            pltpu.make_async_copy(
+                own.at[position, p], own.at[position, p], own_sem.at[position, p]
+            ).wait()
+            over_dp(
+                core.at[position, p], core.at[position, p],
+                core_send.at[position, p], core_recv.at[position, p], partner,
+            ).wait_recv()
+            add(own.at[position, p], core.at[position, p])
+
+        loop(pieces, piece)
+
+    def add(target, source):
+        def part(r):
+            rows = local_rows(r)
+            target[rows, :] = (target[rows, :].astype(F32) + source[rows, :].astype(F32)).astype(BF16)
+
+        loop(height // ROWS, part)
+
+    def send_step(step):
+        def piece(p):
+            @pl.when(plane <= step - 1)
+            def _():
+                if step >= 2:
+
+                    @pl.when(plane >= 1)
+                    def _():
+                        rightward(step - 1, p).wait_recv()
+                        add(own.at[lax.rem(plane + PLANES - step, PLANES), p], right.at[step - 2, p])
+
+                rightward(step, p).start()
+
+            @pl.when(plane >= PLANES - step)
+            def _():
+                if step >= 2:
+
+                    @pl.when(plane <= PLANES - 2)
+                    def _():
+                        leftward(step - 1, p).wait_recv()
+                        add(own.at[lax.rem(plane + step, PLANES), p], left.at[step - 2, p])
+
+                leftward(step, p).start()
+
+        loop(pieces, piece)
+
+    gather_pair(3)
+    gather_pair(0)
+    send_step(1)
+    gather_pair(2)
+    gather_pair(1)
+    for k in range(PLANES - 1):
+        plane_sums(k, planes_from[k]).wait_recv()
+    by_tensor[here] = sum((by_plane[i] for i in range(1, PLANES)), by_plane[0])
+    for k in range(n - 1):
+        tensor_sums(k, here).start()
+    for step in range(2, PLANES):
+        send_step(step)
+    for k in range(n - 1):
+        tensor_sums(k, peer_source[k]).wait_recv()
+    sums_out[...] = sum((by_tensor[i] for i in range(1, n)), by_tensor[0])
+
+    for p, target in enumerate((q_out, k_out, v_out, o_out)):
+        steps = PLANES - 2
+
+        @pl.when(plane >= 1)
+        def _():
+            rightward(PLANES - 1, p).wait_recv()
+
+        @pl.when(plane <= PLANES - 2)
+        def _():
+            leftward(PLANES - 1, p).wait_recv()
+
+        total = own[plane, p].astype(F32)
+        total += jnp.where(plane >= 1, right[steps, p].astype(F32), 0.0)
+        total += jnp.where(plane <= PLANES - 2, left[steps, p].astype(F32), 0.0)
+        target[...] = total if p < pieces - 1 else jnp.transpose(total)
+
+    over_dp(by_core.at[mine], by_core.at[mine], sum_send.at[0], sum_recv.at[0], partner).wait_send()
+    for k in range(PLANES - 1):
+        plane_sums(k, plane).wait_send()
+    for k in range(n - 1):
+        tensor_sums(k, here).wait_send()
+    for p in range(pieces):
+        for position in range(PLANES):
+            core_in(position, p).wait_send()
+        for step in range(1, PLANES):
+
+            @pl.when(plane <= step - 1)
+            def _():
+                rightward(step, p).wait_send()
+
+            @pl.when(plane >= PLANES - step)
+            def _():
+                leftward(step, p).wait_send()
+
+
 def on_device(
     n,
+    replicas,
     streams,
     segments,
     positions,
@@ -891,31 +1216,10 @@
             collective_id=identity, has_side_effects=True, vmem_limit_bytes=mib * MIB
         )
 
-    half = HEAD // 2
-    inverse = 1.0 / 10000.0 ** (jnp.arange(half, dtype=F32) * 2.0 / HEAD)
-    angles = positions.astype(F32)[:, None] * inverse[None, :]
-    cosine, sine = jnp.cos(angles), jnp.sin(angles)
-    cos_table = jnp.concatenate([cosine, cosine], axis=-1)
-    sin_table = jnp.concatenate([-sine, sine], axis=-1)
-    seg_column = jnp.broadcast_to(segments[:, None], (tokens, 128))
-    seg_row = jnp.broadcast_to(segments[None, :], (8, tokens))
-
     def small(form, left, right):
         return jnp.einsum(form, left, right, precision=PRECISE)
 
-    coef = jnp.concatenate(
-        [
-            mix_in1,
-            mix_out2,
-            small("ij,j->i", mix_res1, mix_in2),
-            small("j,j->", mix_in2, mix_out1)[None],
-            small("i,ij->j", mix_out1, mix_res2),
-            small("i,i->", mix_out1, mix_in2)[None],
-            small("ki,ij->kj", mix_res1, mix_res2).reshape(-1),
-        ]
-    )
-    planes = jnp.transpose(streams, (1, 0, 2))
-    cot_planes = jnp.transpose(cotangent, (1, 0, 2))
+    mixes = (mix_in1, mix_out1, mix_in2, mix_out2, mix_res1, mix_res2)
 
     def stats_scratch():
         return [
@@ -925,7 +1229,10 @@
             pltpu.VMEM((n - 1, chunks, 16, CHUNK), F32),
         ]
 
-    normed1, queries, keys, values, stand1, scale1, grad_branch2 = pl.pallas_call(
+    (
+        normed1, queries, keys, values, stand1, scale1, grad_branch2, planes, cot_planes,
+        cos_table, sin_table, seg_column, seg_row,
+    ) = pl.pallas_call(
         functools.partial(project_kernel, n),
         name="project",
         cost_estimate=lasts(100),
@@ -937,10 +1244,18 @@
             array((tokens, width), F32),
             array((tokens, 128), F32),
             array((tokens, features), BF16),
+            array((stream_count, tokens, width), BF16),
+            array((stream_count, tokens, width), BF16),
+            array((tokens, HEAD), F32),
+            array((tokens, HEAD), F32),
+            array((tokens, 128), F32),
+            array((8, tokens), F32),
         ],
-        in_specs=[smem, vmem, vmem] + [any_spec] * 5,
-        out_specs=[any_spec, vmem, vmem, vmem, vmem, vmem, any_spec],
+        in_specs=[smem, smem, vmem, vmem] + [any_spec] * 5,
+        out_specs=[any_spec] + [vmem] * 5 + [any_spec] * 3 + [vmem] * 4,
         scratch_shapes=[
+            pltpu.VMEM((tokens, stream_count, width), BF16),
+            pltpu.VMEM((tokens, stream_count, width), BF16),
             pltpu.VMEM((stream_count, tokens, width), BF16),
             pltpu.VMEM((stream_count, tokens, width), BF16),
             pltpu.VMEM((3, features, width), BF16),
@@ -948,15 +1263,19 @@
             pltpu.VMEM((tokens, features), BF16),
         ]
         + stats_scratch()
-        + [dma(2, chunks), dma(3), dma(2, chunks)]
+        + [dma(2, chunks), dma(3), dma(4, chunks)]
         + gather_sems
         + gather_sems
         + stats_sems,
-        compiler_params=params(0, 48),
-    )(coef, cos_table, sin_table, planes, cot_planes, w_query, w_key, w_value)
+        compiler_params=params(0, 56),
+    )(
+        mix_in1, mix_out2,
+        positions.reshape(tokens // 128, 128), segments.reshape(tokens // 128, 128),
+        streams, cotangent, w_query, w_key, w_value,
+    )
 
     extent = window(0, tokens)[1]
-    attended, branch1, normed2, stand2, scale2 = pl.pallas_call(
+    attended, branch1, normed2, stand2, scale2, hidden, grad_acts = pl.pallas_call(
         functools.partial(attend_kernel, n),
         name="attend",
         cost_estimate=lasts(100),
@@ -966,41 +1285,34 @@
             array((tokens, features), BF16),
             array((tokens, width), F32),
             array((tokens, 128), F32),
+            array((tokens, units), BF16),
+            array((tokens, 2 * units), BF16),
         ],
-        in_specs=[smem] + [vmem] * 6 + [any_spec],
-        out_specs=[vmem, vmem, any_spec, vmem, vmem],
+        in_specs=[smem] * 6 + [vmem] * 6 + [any_spec] * 5,
+        out_specs=[vmem, vmem, any_spec, vmem, vmem, any_spec, any_spec],
         scratch_shapes=[
-            pltpu.VMEM((stream_count, tokens, width), BF16),
+            pltpu.VMEM((2, stream_count, CHUNK, width), BF16),
+            pltpu.VMEM((2, CHUNK, features), BF16),
+            pltpu.VMEM((features, units), BF16),
+            pltpu.VMEM((features, units), BF16),
+            pltpu.VMEM((units, features), BF16),
+            pltpu.VMEM((2, CHUNK, units), BF16),
+            pltpu.VMEM((2, CHUNK, units), BF16),
+            pltpu.VMEM((2, CHUNK, units), BF16),
             pltpu.VMEM((tokens, features), BF16),
             pltpu.VMEM((n - 1, tokens, width), BF16),
             pltpu.VMEM((tokens, features), BF16),
         ]
         + stats_scratch()
-        + [pltpu.VMEM((CHUNK, extent), F32), pltpu.SemaphoreType.DMA, dma(chunks)]
+        + [pltpu.VMEM((CHUNK, extent), F32), dma(2), dma(2), dma(3), dma(chunks), dma(3, 2)]
         + scatter_sems
         + gather_sems
         + stats_sems,
-        compiler_params=params(1, 48),
-    )(coef, queries, keys, values, seg_column, seg_row, w_output, planes)
-
-    block = min(256, units)
-    hidden, grad_acts = pl.pallas_call(
-        units_kernel,
-        name="units",
-        cost_estimate=lasts(35),
-        grid=(units // block,),
-        out_shape=[array((tokens, units), BF16), array((tokens, 2 * units), BF16)],
-        in_specs=[
-            pl.BlockSpec((tokens, features), lambda f: (0, 0)),
-            pl.BlockSpec((tokens, features), lambda f: (0, 0)),
-            pl.BlockSpec((features, block), lambda f: (0, f)),
-            pl.BlockSpec((features, block), lambda f: (0, f)),
-            pl.BlockSpec((block, features), lambda f: (f, 0)),
-        ],
-        out_specs=[pl.BlockSpec((tokens, block), lambda f: (0, f)), any_spec],
-        scratch_shapes=[pltpu.VMEM((2, 2, tokens, block), BF16), dma(2, 2)],
-        compiler_params=pltpu.CompilerParams(vmem_limit_bytes=48 * MIB),
-    )(normed2, grad_branch2, w_gate, w_up, w_down)
+        compiler_params=params(1, 62),
+    )(
+        *mixes, queries, keys, values, seg_column, seg_row, w_output, planes,
+        grad_branch2, w_gate, w_up, w_down,
+    )
 
     def over_dp(partial, dimension):
         return lax.psum_scatter(partial, "dp", scatter_dimension=dimension, tiled=True)
@@ -1018,7 +1330,7 @@
         name="units_back",
         cost_estimate=lasts(400),
         out_shape=[array((tokens, width), F32), array((tokens, features), BF16)],
-        in_specs=[smem] + [vmem] * 6 + [any_spec] * 3,
+        in_specs=[smem] * 6 + [vmem] * 6 + [any_spec] * 3,
         out_specs=[vmem, any_spec],
         scratch_shapes=[
             pltpu.VMEM((stream_count, tokens, width), BF16),
@@ -1038,7 +1350,7 @@
         + gather_sems,
         compiler_params=params(2, 60),
     )(
-        coef, grad_acts, w_gate, w_up, normed2, stand2, scale2, cot_planes,
+        *mixes, grad_acts, w_gate, w_up, normed2, stand2, scale2, cot_planes,
         part_down, part_gate_up,
     )
 
@@ -1080,14 +1392,8 @@
     )
 
     part_lin = contract_rows(normed1, grad_lin).astype(BF16)
-    grad_lin_w = over_dp(jnp.concatenate([part_lin, part_output], axis=1), 0)
-    grad_w_output = jnp.transpose(grad_lin_w[:, 3 * width :]).astype(F32)
-    grad_w_query, grad_w_key, grad_w_value = (
-        grad_lin_w[:, width * j : width * (j + 1)].astype(F32) for j in range(3)
-    )
 
     rows = 128
-    sum_count = 33
     plane_spec = pl.BlockSpec((stream_count, rows, width), lambda t: (0, t, 0))
     field_spec = pl.BlockSpec((rows, width), lambda t: (t, 0))
     stream_spec = pl.BlockSpec((rows, stream_count, width), lambda t: (t, 0, 0))
@@ -1099,17 +1405,54 @@
         out_shape=[
             array(streams.shape, BF16),
             array(streams.shape, F32),
-            array((sum_count, 8, 128), F32),
+            array((SUMS, 8, 128), F32),
         ],
-        in_specs=[smem, plane_spec, plane_spec] + [field_spec] * 4 + [any_spec],
+        in_specs=[smem] * 6 + [plane_spec, plane_spec] + [field_spec] * 4,
         out_specs=[
             stream_spec,
             stream_spec,
-            pl.BlockSpec((sum_count, 8, 128), lambda t: (0, 0, 0)),
+            pl.BlockSpec((SUMS, 8, 128), lambda t: (0, 0, 0)),
         ],
         compiler_params=pltpu.CompilerParams(vmem_limit_bytes=48 * MIB),
-    )(coef, planes, cot_planes, branch1, branch2, grad_entry1, grad_entry2, grad_gate_up)
-    sums = lax.psum(jnp.sum(sums, axis=(1, 2)), ("dp", "tensor"))
+    )(*mixes, planes, cot_planes, branch1, branch2, grad_entry1, grad_entry2)
+    height = features // replicas
+    if replicas == PLANES * CORES and stream_count == 4:
+        steps = PLANES - 1
+        grad_w_query, grad_w_key, grad_w_value, grad_w_output, sums = pl.pallas_call(
+            functools.partial(finish_kernel, n),
+            name="finish",
+            cost_estimate=lasts(2),
+            out_shape=[array((height, width), F32)] * 3
+            + [array((width, height), F32), array((SUM_ROWS, 128), F32)],
+            in_specs=[any_spec, any_spec, vmem],
+            out_specs=[vmem] * 5,
+            scratch_shapes=[
+                pltpu.VMEM((PLANES, 4, height, width), BF16),
+                pltpu.VMEM((PLANES, 4, height, width), BF16),
+                pltpu.VMEM((steps, 4, height, width), BF16),
+                pltpu.VMEM((steps, 4, height, width), BF16),
+                pltpu.VMEM((CORES, SUM_ROWS, 128), F32),
+                pltpu.VMEM((PLANES, SUM_ROWS, 128), F32),
+                pltpu.VMEM((n, SUM_ROWS, 128), F32),
+                dma(PLANES, 4),
+                dma(PLANES, 4),
+                dma(PLANES, 4),
+                dma(steps, 4),
+                dma(steps, 4),
+                dma(steps, 4),
+                dma(steps, 4),
+                dma(PLANES + n - 1),
+                dma(PLANES + n - 1),
+            ],
+            compiler_params=params(4, 48),
+        )(part_lin, part_output, sums)
+        sums = jnp.sum(sums[:SUMS], axis=1)
+    else:
+        grad_w_query, grad_w_key, grad_w_value = (
+            over_dp(part_lin[:, width * j : width * (j + 1)], 0).astype(F32) for j in range(3)
+        )
+        grad_w_output = jnp.transpose(over_dp(part_output, 0)).astype(F32)
+        sums = lax.psum(jnp.sum(sums, axis=(1, 2)), ("dp", "tensor"))
     s_c = sums[0:16].reshape(4, 4)
     s_e1, s_e2, c_b1, c_b2, b_e = sums[16:20], sums[20:24], sums[24:28], sums[28:32], sums[32]
     grad_mix_in1 = s_e1
@@ -1139,7 +1482,7 @@
 
 def solution(mesh):
     return jax.shard_map(
-        functools.partial(on_device, mesh.shape["tensor"]),
+        functools.partial(on_device, mesh.shape["tensor"], mesh.shape["dp"]),
         mesh=mesh,
         in_specs=(
             P("dp", None, "tensor"),

time: 608 us -> 578 us (0.951); the launches traced: 605 us -> 566 us
  Pallas kernels: 400 us -> 471 us
  waiting for transfers between devices: 50.5 us -> 0.04 us
  blocking collectives: 39.5 us -> 0 us
  local copies, waits for them, and re-layouts: 23.3 us -> 6.77 us
  other arithmetic: 18.8 us -> 5.66 us
  matrix products: 58.6 us -> 68.6 us
    reduce_scatter x3 -> x2, waiting for transfers between devices: 50.5 us -> 0.01 us  [over_dp(): lax.psum_scatter(partial, 'dp', scatter_dimension=dimension, tiled=True)]
    psum x1 -> x0, blocking collectives: 39.5 us -> none  [on_device(): sums = lax.psum(jnp.sum(sums, axis=(1, 2)), ('dp', 'tensor'))]
    pallas_call x1, Pallas kernels: 34.9 us -> 72.1 us  [on_device(): pl.pallas_call(functools.partial(finish_kernel, n), name='finish', cost_e...]
    pallas_call x1, Pallas kernels: 82.2 us -> 109 us  [on_device(): pl.pallas_call(functools.partial(attend_kernel, n), name='attend', cost_e...]
    dot_general x4, matrix products: 52.6 us -> 64.9 us  [contract_rows(): lax.dot_general(left, right, (((0,), (0,)), ((), ())), preferred_element_...]
    concatenate x2 -> x0, other arithmetic: 8.26 us -> none  [the longest x1 7.93 us: on_device(): grad_lin_w = over_dp(jnp.concatenate([part_lin, part_output], axis=1), 0)]
    transpose x1 -> x0, local copies, waits for them, and re-layouts: 7.88 us -> none  [on_device(): cot_planes = jnp.transpose(cotangent, (1, 0, 2))]
    pallas_call x1, Pallas kernels: 83.1 us -> 90.2 us  [on_device(): pl.pallas_call(functools.partial(project_kernel, n), name='project', cost...]
  transfers between devices with their start and end apart: 3 -> 2, of which waited for: 2 -> 0; matrix products, arithmetic and copies ran while one was open for 10% -> 10% of each run, Pallas kernels for 33% -> 48%
where the time goes in v3:
time: 578 us; the launch traced here: 566 us
  Pallas kernels  471 us (81%)
  matrix products  68.6 us (12%)
  between operations  14.6 us (3%)
  local copies, waits for them, and re-layouts  6.77 us (1%)
    pallas_call x1, Pallas kernels, on_device(): pl.pallas_call(functools.partial(attend_kernel, n), name='attend', cost_e...  109 us
    pallas_call x1, Pallas kernels, on_device(): pl.pallas_call(functools.partial(project_kernel, n), name='project', cost...  90.2 us
    pallas_call x1, Pallas kernels, on_device(): pl.pallas_call(functools.partial(units_back_kernel, n), name='units_back'...  89.3 us
    pallas_call x1, Pallas kernels, on_device(): pl.pallas_call(functools.partial(attend_back_kernel, n), name='attend_bac...  87.9 us
    pallas_call x1, Pallas kernels, on_device(): pl.pallas_call(functools.partial(finish_kernel, n), name='finish', cost_e...  72.1 us
    dot_general x4, matrix products, contract_rows(): lax.dot_general(left, right, (((0,), (0,)), ((), ())), preferred_element_...  64.9 us
    pallas_call x1, Pallas kernels, on_device(): pl.pallas_call(streams_kernel, name='streams', cost_estimate=lasts(2), gr...  21.8 us
  transfers between devices with their start and end apart: 2, of which 0 were waited for; matrix products, arithmetic and copies ran while one was open for 10% of the time, Pallas kernels for 48%

profile of v3, /device:TPU:0, one launch (start us, length us, event | category | flops | bytes accessed | tf_op | source)
XLA Modules:
  0.0 566.4 jit_solution(6109294478593521088)
XLA Ops:
  7.2 0.0 reduce-scatter.3.cloned.1.call-start
  7.2 90.2 %project.1 = (bf16[1024,2048]{1,0:T(8,128)(2,1)}, bf16[1024,512]{1,0:T(8,128)(2,1)}, bf16[1024,512]{1,0:T(8,128)(2,1)}, bf16[1024,512]{1,0:T(8,128)(2,1)}, f32[1...) custom-call(f32[4]{0:T(128)} %in1.7, f32[4]{0:T(128)} %out2.7, ...), custom_call_target="tpu_custom_call" | custom-call | flops 99999997952 | bytes 360000000 | tf_op jit(solution)/shard_map/project/pallas_call | solution.py:1235
  97.4 109.3 %attend.1 = (bf16[1024,512]{1,0:T(8,128)(2,1)}, f32[1024,512]{1,0:T(8,128)}, bf16[1024,2048]{1,0:T(8,128)(2,1)}, f32[1024,512]{1,0:T(8,128)}, f32[1024,128]{1,0:...) custom-call(f32[4]{0:T(128)} %in1.7, f32[4]{0:T(128)} %out1.5, f32[4]{0:T(128)} %in2.5, f32[4]{0:T(128)} %out2.7, ...), custom_call_target="tpu_custom_call" | custom-call | flops 99999997952 | bytes 360000000 | tf_op jit(solution)/shard_map/attend/pallas_call | solution.py:1278
  206.8 14.0 %convolution_convert_fusion.2._down = bf16[2048,2048]{1,0:T(8,128)(2,1)} fusion(bf16[1024,2048]{1,0:T(8,128)(2,1)} %get-tuple-element.65.hidden_hbm, bf16[1024,2048]{1,0:T(8,128)(2,1)} %get-tuple-element.55.gb2_hbm), kind=kOutput, calls=%fused_computation.2 | convolution fusion | flops 8594128896 | bytes 16777216 | tf_op jit(solution)/shard_map/dot_general | solution.py:48
  220.8 0.0 reduce-scatter.3.cloned.1.call-update
  220.8 0.0 reduce-scatter.5.cloned.1.call-start
  220.9 36.1 %convolution_convert_fusion._gate_up = bf16[2048,4096]{1,0:T(8,128)(2,1)} fusion(bf16[1024,2048]{1,0:T(8,128)(2,1)} %get-tuple-element.62.normed_ref, bf16[1024,4096]{1,0:T(8,128)(2,1)} %get-tuple-element.61.acts_ref), kind=kOutput, calls=%fused_computation | convolution fusion | flops 17188257792 | bytes 29360128 | tf_op jit(solution)/shard_map/dot_general | solution.py:48
  257.0 0.0 reduce-scatter.5.cloned.1.call-update
  257.0 0.0 copy-start.12
  257.0 89.3 %units_back.1 = (f32[1024,512]{1,0:T(8,128)}, bf16[1024,2048]{1,0:T(8,128)(2,1)}) custom-call(f32[4]{0:T(128)} %in1.7, f32[4]{0:T(128)} %out1.5, f32[4]{0:T(128)} %in2.5, f32[4]{0:T(128)} %out2.7, f32[4,4]{1,0:T(4,128)} %res1.5, f32[4,4]{1,0:T(4,128)} %res2.5, bf16[1024,4096]{1,0:T(8,128)(2,1)} %get-tuple-element.61.acts_ref, bf16[2048,2048]{1,0:T(8,128)(2,1)} %wg_ref.1, ...), custom_call_target="tpu_custom_call" | custom-call | flops 399999991808 | bytes 1440000000 | tf_op jit(solution)/shard_map/units_back/pallas_call | solution.py:1328
  346.4 0.0 copy-done.12
  346.4 6.0 %convolution_convert_fusion.3._output.last_hbm = bf16[2048,512]{1,0:T(8,128)(2,1)} fusion(bf16[1024,2048]{1,0:T(8,128)(2,1)} %get-tuple-element.66.gb1_hbm, bf16[1024,512]{1,0:T(8,128)(2,1)S(1)} %copy-done.12), kind=kOutput, calls=%fused_computation.3 | convolution fusion | flops 2148532224 | bytes 7340032 | tf_op jit(solution)/shard_map/dot_general | solution.py:48
  352.3 0.0 copy-start.5
  352.4 0.0 copy-start.6
  352.4 0.0 copy-start.7
  352.4 0.0 copy-start.8
  352.4 87.9 %attend_back.1 = (bf16[1024,1536]{1,0:T(8,128)(2,1)}, f32[1024,512]{1,0:T(8,128)}, f32[1024,512]{1,0:T(8,128)}) custom-call(bf16[1024,512]{1,0:T(8,128)(2,1)} %get-tuple-element.50.q_ref, bf16[1024,512]{1,0:T(8,128)(2,1)} %get-tuple-element.51.k_ref, bf16[1024,512]{1,0:T(8,128)(2,1)} %get-tuple-element.52.v_ref, f32[1024,128]{1,0:T(8,128)} %get-tuple-element.53.segc_ref, ...), custom_call_target="tpu_custom_call" | custom-call | flops 2000000000 | bytes 7200000 | tf_op jit(solution)/shard_map/attend_back/pallas_call | solution.py:1359
  440.3 0.0 copy-done.1
  440.3 0.0 copy-done.3
  440.3 0.0 copy-done.4
  440.4 0.0 copy-done.5
  440.4 0.0 copy-done.6
  440.4 0.0 copy-done.7
  440.4 0.0 copy-done.8
  440.4 0.0 copy-start.2
  440.4 1.6 copy-done.2
  442.0 21.8 %streams.1 = (bf16[1024,4,512]{2,1,0:T(4,128)(2,1)}, f32[1024,4,512]{2,1,0:T(4,128)}, f32[33,8,128]{2,1,0:T(8,128)S(1)}) custom-call(f32[4]{0:T(128)S(1)} %copy-done.5, f32[4]{0:T(128)S(1)} %copy-done.7, f32[4]{0:T(128)S(1)} %copy-done.8, f32[4]{0:T(128)S(1)} %copy-done.6, f32[4,4]{1,0:T(4,128)S(1)} %copy-done.3, f32[4,4]{1,0:T(4,128)S(1)} %copy-done.4, ...), custom_call_target="tpu_custom_call" | custom-call | flops 2000000000 | bytes 7200000 | tf_op jit(solution)/shard_map/streams/pallas_call | solution.py:1400
  463.8 0.0 copy-done.10
  463.8 0.0 copy-done.11
  463.8 0.0 copy-start
  463.8 8.8 %convolution_convert_fusion.1.first_hbm = bf16[2048,1536]{1,0:T(8,128)(2,1)} fusion(bf16[1024,2048]{1,0:T(8,128)(2,1)S(1)} %copy-done.10, bf16[1024,1536]{1,0:T(8,128)(2,1)S(1)} %copy-done.11), kind=kOutput, calls=%fused_computation.1 | convolution fusion | flops 6445596672 | bytes 13631488 | tf_op jit(solution)/shard_map/dot_general | solution.py:48
  472.6 0.0 copy-done
  472.6 72.1 %finish.1 = (f32[256,512]{1,0:T(8,128)S(1)}, f32[256,512]{1,0:T(8,128)S(1)}, f32[256,512]{1,0:T(8,128)S(1)}, f32[512,256]{1,0:T(8,128)S(1)}, f32[40,128]{1,0:T(8,128)S(1)}) custom-call(bf16[2048,1536]{1,0:T(8,128)(2,1)} %convolution_convert_fusion.1.first_hbm, bf16[2048,512]{1,0:T(8,128)(2,1)S(1)} %copy-done, f32[33,8,128]{2,1,0:T(8,128)S(1)} %get-tuple-element.75.sums_ref), custom_call_target="tpu_custom_call" | custom-call | flops 2000000000 | bytes 7200000 | tf_op jit(solution)/shard_map/finish/pallas_call | solution.py:1421
  544.7 0.1 slice_reduce_fusion
  544.8 0.6 slice.34
  545.4 0.1 reshape.45
  545.5 0.6 fusion.7
  546.1 0.2 fusion
  546.3 0.7 copy.32
  547.0 1.5 convert_element_type.27
  548.5 1.4 fusion.2
  549.8 1.4 fusion.1
  551.2 0.7 convolution_add_fusion
  551.9 4.1 slice_convert_fusion
  556.0 0.8 copy.37
  556.8 0.8 copy.38
  557.6 0.8 copy.39
  558.3 0.8 copy.40
  (9 shorter events, 0.0 us)
Async XLA Ops:
  7.2 345.1 %reduce-scatter.3.cloned.1.call-start = ((), (), s32[]{:S(2)}) async-start(), calls=%async_computation.2 | async-start | bytes 9437184 | tf_op jit(solution)/shard_map/reduce_scatter | solution.py:1318
  220.8 331.1 %reduce-scatter.5.cloned.1.call-start = ((), (), s32[]{:S(2)}) async-start(), calls=%async_computation.3 | async-start | bytes 18874368 | tf_op jit(solution)/shard_map/reduce_scatter | solution.py:1318
  257.0 89.3 %copy-start.12 = (bf16[1024,512]{1,0:T(8,128)(2,1)S(1)}, bf16[1024,512]{1,0:T(8,128)(2,1)}, u32[]{:S(2)}) copy-start(bf16[1024,512]{1,0:T(8,128)(2,1)} %get-tuple-element.68) | copy-start | bytes 3145732
  352.3 88.0 %copy-start.1 = (f32[1024,512]{1,0:T(8,128)S(1)}, f32[1024,512]{1,0:T(8,128)}, u32[]{:S(2)}) copy-start(f32[1024,512]{1,0:T(8,128)} %get-tuple-element.56.b1_ref) | copy-start | bytes 6291460
  352.3 88.0 %copy-start.3 = (f32[4,4]{1,0:T(4,128)S(1)}, f32[4,4]{1,0:T(4,128)}, u32[]{:S(2)}) copy-start(f32[4,4]{1,0:T(4,128)} %res1.5) | copy-start | bytes 196
  352.3 88.0 %copy-start.4 = (f32[4,4]{1,0:T(4,128)S(1)}, f32[4,4]{1,0:T(4,128)}, u32[]{:S(2)}) copy-start(f32[4,4]{1,0:T(4,128)} %res2.5) | copy-start | bytes 196
  352.3 88.0 %copy-start.5 = (f32[4]{0:T(128)S(1)}, f32[4]{0:T(128)}, u32[]{:S(2)}) copy-start(f32[4]{0:T(128)} %in1.7) | copy-start | bytes 52
  352.4 88.0 %copy-start.6 = (f32[4]{0:T(128)S(1)}, f32[4]{0:T(128)}, u32[]{:S(2)}) copy-start(f32[4]{0:T(128)} %out2.7) | copy-start | bytes 52
  352.4 88.0 %copy-start.7 = (f32[4]{0:T(128)S(1)}, f32[4]{0:T(128)}, u32[]{:S(2)}) copy-start(f32[4]{0:T(128)} %out1.5) | copy-start | bytes 52
  352.4 88.0 %copy-start.8 = (f32[4]{0:T(128)S(1)}, f32[4]{0:T(128)}, u32[]{:S(2)}) copy-start(f32[4]{0:T(128)} %in2.5) | copy-start | bytes 52
  440.4 1.6 copy-start.2
  442.0 21.8 %copy-start.10 = (bf16[1024,2048]{1,0:T(8,128)(2,1)S(1)}, bf16[1024,2048]{1,0:T(8,128)(2,1)}, u32[]{:S(2)}) copy-start(bf16[1024,2048]{1,0:T(8,128)(2,1)} %get-tuple-element.67.normed_hbm) | copy-start | bytes 12582916
  442.0 21.8 %copy-start.11 = (bf16[1024,1536]{1,0:T(8,128)(2,1)S(1)}, bf16[1024,1536]{1,0:T(8,128)(2,1)}, u32[]{:S(2)}) copy-start(bf16[1024,1536]{1,0:T(8,128)(2,1)} %get-tuple-element.74) | copy-start | bytes 9437188
  463.8 8.9 %copy-start = (bf16[2048,512]{1,0:T(8,128)(2,1)S(1)}, bf16[2048,512]{1,0:T(8,128)(2,1)}, u32[]{:S(2)}) copy-start(bf16[2048,512]{1,0:T(8,128)(2,1)} %convolution_convert_fusion.3._output.last_hbm) | copy-start | bytes 6291460
  472.6 74.3 %copy-start.9 = (bf16[2048,256]{1,0:T(8,128)(2,1)S(1)}, bf16[2048,256]{1,0:T(8,128)(2,1)}, u32[]{:S(2)}) copy-start(bf16[2048,256]{1,0:T(8,128)(2,1)} %reduce-scatter.3.cloned.1.call-done._down) | copy-start | bytes 3145732
Sparse Core Ops, SparseCore 0:
  220.9 89.8 reduce-scatter.2
  313.2 166.5 reduce-scatter.4

commit v4 on v3

--- a/solution.py
+++ b/solution.py
@@ -150,19 +150,6 @@
         if self.n == 4:
             for copy in self.handed(c):
                 copy.wait_send()
-
-    def take(self, count, work):
-        self.relay(0)
-
-        def body(c):
-            @pl.when(c + 1 < count)
-            def _():
-                self.relay(c + 1)
-
-            self.arrive(c)
-            work(c)
-
-        loop(count, body)
 
 
 class Scatter:
@@ -372,19 +359,19 @@
 
 def project_kernel(
     n, in1, out2, positions_ref, segments_ref, s_hbm, c_hbm, wq_hbm, wk_hbm, wv_hbm,
-    normed_hbm, q_ref, k_ref, v_ref, stand_ref, scale_ref, gb2_hbm, planes_hbm, cot_hbm,
+    normed_hbm, q_ref, k_ref, v_ref, stand_ref, scale_ref, gb2_hbm, cot_hbm,
     cos_ref, sin_ref, segc_ref, segr_ref,
-    s_buf, c_buf, planes, cot_planes, w_buf, all1, all2, first, second, mine, others,
+    s_buf, c_buf, cot_planes, w_buf, all1, all2, first, second, mine, others,
     in_sem, w_sem, out_sem, send1, recv1, send2, recv2, send3, recv3,
 ):
-    tokens, streams, width = s_buf.shape
+    streams, tokens, width = s_buf.shape
     count = tokens // CHUNK
     heads = width // HEAD
     weights = (wq_hbm, wk_hbm, wv_hbm)
 
     def s_in(c):
         return pltpu.make_async_copy(
-            s_hbm.at[chunk_rows(c)], s_buf.at[chunk_rows(c)], in_sem.at[0, c]
+            s_hbm.at[:, chunk_rows(c)], s_buf.at[:, chunk_rows(c)], in_sem.at[0, c]
         )
 
     def c_in(c):
@@ -400,14 +387,12 @@
         source, target = (
             (all1.at[rows], normed_hbm.at[rows]),
             (all2.at[rows], gb2_hbm.at[rows]),
-            (planes.at[:, rows], planes_hbm.at[:, rows]),
             (cot_planes.at[:, rows], cot_hbm.at[:, rows]),
         )[i]
         return pltpu.make_async_copy(source, target, out_sem.at[i, c])
 
-    c_in(0).start()
     loop(count, lambda c: s_in(c).start())
-    loop(count - 1, lambda c: c_in(c + 1).start())
+    loop(count, lambda c: c_in(c).start())
     for j in range(3):
         w_in(j).start()
     gather = Gather(n, all1, width, send1, recv1)
@@ -415,20 +400,14 @@
     stats = Stats(n, mine, others, send3, recv3)
     enter(n, gather.to)
 
-    def mix(buf, weight, target, rows):
-        block = buf[rows].astype(F32)
-        total = None
-        for i in range(streams):
-            field = block[:, i, :]
-            target[i, rows] = field.astype(BF16)
-            total = weight[i] * field if total is None else total + weight[i] * field
-        return total
-
     def entry(c):
         s_in(c).wait()
 
         def piece(r):
-            field = mix(s_buf, in1, planes, sub_rows(c, r))
+            rows = sub_rows(c, r)
+            field = in1[0] * s_buf[0, rows].astype(F32)
+            for i in range(1, streams):
+                field += in1[i] * s_buf[i, rows].astype(F32)
             stand_ref[sub_rows(c, r), :] = field
             fold_entry(field, first, second, local_rows(r))
 
@@ -444,13 +423,18 @@
 
         def piece(r):
             rows = sub_rows(c, r)
-            all2[rows, incoming.own()] = mix(c_buf, out2, cot_planes, rows).astype(BF16)
+            block = c_buf[rows].astype(F32)
+            total = None
+            for i in range(streams):
+                field = block[:, i, :]
+                cot_planes[i, rows] = field.astype(BF16)
+                total = out2[i] * field if total is None else total + out2[i] * field
+            all2[rows, incoming.own()] = total.astype(BF16)
 
         loop(CHUNK // ROWS, piece)
         incoming.start(c)
-        out(c, 3).start()
-
-    grad(0)
+        out(c, 2).start()
+
     entry(0)
 
     def ahead(c):
@@ -458,9 +442,12 @@
         send(c)
 
     loop(count - 1, ahead)
+    send(count - 1)
+    grad(0)
+    gather.relay(0)
     grad(1)
-    send(count - 1)
-    loop(count - 2, lambda c: grad(c + 2))
+    gather.relay(1)
+    incoming.relay(0)
 
     segr_ref[...] = jnp.concatenate(
         [
@@ -479,12 +466,17 @@
         cos_ref[rows, :] = jnp.cos(angles)
         sine = jnp.sin(angles)
         sin_ref[rows, :] = jnp.where(lane < HEAD // 2, -sine, sine)
+    grad(2)
+    gather.relay(2)
+    grad(3)
+    gather.relay(3)
+    incoming.relay(1)
     for j in range(3):
         w_in(j).wait()
 
     def work(c):
-        for i in (0, 2):
-            out(c, i).start()
+        gather.arrive(c)
+        out(c, 0).start()
         rows = chunk_rows(c)
         block = all1[rows, :]
         cos_rows, sin_rows = cos_ref[rows, :], sin_ref[rows, :]
@@ -494,9 +486,12 @@
                 place = slice(HEAD * h, HEAD * (h + 1))
                 target[rows, place] = rotate(lin[:, place], cos_rows, sin_rows, 1.0).astype(BF16)
         v_ref[rows, :] = dot_nn(block, w_buf[2]).astype(BF16)
-        incoming.relay(c)
-
-    gather.take(count, work)
+
+        @pl.when(c + 2 < count)
+        def _():
+            incoming.relay(c + 2)
+
+    loop(count, work)
 
     def end(c):
         incoming.arrive(c)
@@ -505,7 +500,7 @@
     loop(count, end)
 
     def drain(c):
-        for i in range(4):
+        for i in range(3):
             out(c, i).wait()
         stats.finish(c)
         gather.finish(c)
@@ -534,10 +529,10 @@
 def attend_kernel(
     n, in1, out1, in2, out2, res1, res2, q_ref, k_ref, v_ref, segc_ref, segr_ref, wo_ref,
     s_hbm, gb2_hbm, wg_hbm, wu_hbm, wd_hbm,
-    attended_ref, branch_ref, normed_hbm, stand_ref, scale_ref, hidden_hbm, acts_hbm,
+    attended_ref, branch_ref, normed_hbm, stand_ref, scale_ref, hidden_hbm, acts_hbm, grads_hbm,
     s_buf, gb2_buf, wg_buf, wu_buf, wd_buf, hidden_buf, gate_buf, up_buf,
     part, came, all2, first, second, mine, others, bias,
-    s_sem, gb2_sem, w_sem, normed_sem, out_sem, send1, recv1, send2, recv2, send3, recv3,
+    s_sem, gb2_sem, grad_sem, w_sem, normed_sem, out_sem, send1, recv1, send2, recv2, send3, recv3,
 ):
     tokens, width = q_ref.shape
     units = wg_buf.shape[1]
@@ -553,6 +548,18 @@
     def gb2_in(c):
         slot = lax.rem(c, 2)
         return pltpu.make_async_copy(gb2_hbm.at[chunk_rows(c)], gb2_buf.at[slot], gb2_sem.at[slot])
+
+    def grads_out(c):
+        slot = lax.rem(c, 2)
+        return pltpu.make_async_copy(
+            gate_buf.at[slot], grads_hbm.at[chunk_rows(c)], grad_sem.at[0, slot]
+        )
+
+    def grads_in(c):
+        slot = lax.rem(c, 2)
+        return pltpu.make_async_copy(
+            grads_hbm.at[chunk_rows(c)], gb2_buf.at[slot, :, 0:units], grad_sem.at[1, slot]
+        )
 
     def normed_out(c):
         return pltpu.make_async_copy(
@@ -575,11 +582,12 @@
     weights = tuple(
         pltpu.make_async_copy(source, target, w_sem.at[i])
         for i, (source, target) in enumerate(
-            ((wg_hbm, wg_buf), (wu_hbm, wu_buf), (wd_hbm, wd_buf))
+            ((wd_hbm, wd_buf), (wg_hbm, wg_buf), (wu_hbm, wu_buf))
         )
     )
     s_in(0).start()
     gb2_in(0).start()
+    gb2_in(1).start()
     for copy in weights:
         copy.start()
     scatter = Scatter(n, part, came, width, send1, recv1)
@@ -628,25 +636,22 @@
         standardize(c, stats, gather, first, second, stand_ref, scale_ref)
 
     def work(c):
+        gather.arrive(c)
         normed_out(c).start()
         slot = lax.rem(c, 2)
-
-        @pl.when(c + 1 < count)
-        def _():
-            gb2_in(c + 1).start()
 
         @pl.when(c >= 2)
         def _():
             for copy in outs(c - 2):
                 copy.wait()
 
-        gb2_in(c).wait()
+        grads_in(c).wait()
 
         def piece(f):
             place = columns(f, block)
             gate = dot_nn(all2[chunk_rows(c), :], wg_buf[:, place])
             up = dot_nn(all2[chunk_rows(c), :], wu_buf[:, place])
-            grad = dot_nt(gb2_buf[slot], wd_buf[place, :])
+            grad = gb2_buf[slot, :, place].astype(F32)
             sig = jax.nn.sigmoid(gate)
             act = gate * sig
             hidden_buf[slot, :, place] = (act * up).astype(BF16)
@@ -657,6 +662,26 @@
         for copy in outs(c):
             copy.start()
 
+        @pl.when(c + 2 < count)
+        def _():
+            grads_in(c + 2).start()
+            gather.relay(c + 2)
+
+    def grads(c):
+        slot = lax.rem(c, 2)
+        if c >= 2:
+            grads_out(c - 2).wait()
+        gb2_in(c).wait()
+
+        def piece(f):
+            place = columns(f, block)
+            gate_buf[slot, :, place] = dot_nt(gb2_buf[slot], wd_buf[place, :]).astype(BF16)
+
+        loop(units // block, piece)
+        grads_out(c).start()
+        if c + 2 < count:
+            gb2_in(c + 2).start()
+
     def attend_send(c):
         attend(c)
         scatter.start(c)
@@ -665,40 +690,30 @@
         def _():
             scatter.relay(c - 1)
 
-    end = count - 1
-    loop(end, attend_send)
+    loop(count, attend_send)
     middle(0)
-    attend(end)
+    weights[0].wait()
+    grads(0)
+    scatter.relay(3)
+    middle(1)
     send(0)
-    scatter.start(end)
-    scatter.relay(end - 1)
-
-    def ahead(c):
-        middle(c)
-        send(c)
-
-    loop(end - 2, lambda c: ahead(c + 1))
-    scatter.relay(end)
-    middle(end - 1)
+    grads(1)
+    middle(2)
+    send(1)
+    grads(2)
+    middle(3)
+    grads(3)
     gather.relay(0)
-    send(end - 1)
-    for copy in weights:
-        copy.wait()
-    gather.arrive(0)
-    work(0)
-    middle(end)
+    send(2)
     gather.relay(1)
-    send(end)
-
-    def rest(c):
-        gather.arrive(c)
-        work(c)
-
-        @pl.when(c + 1 < count)
-        def _():
-            gather.relay(c + 1)
-
-    loop(end, lambda c: rest(c + 1))
+    send(3)
+    grads_out(2).wait()
+    grads_out(3).wait()
+    grads_in(0).start()
+    grads_in(1).start()
+    weights[1].wait()
+    weights[2].wait()
+    loop(count, work)
     for c in range(max(count - 2, 0), count):
         for copy in outs(c):
             copy.wait()
@@ -754,10 +769,6 @@
         def _():
             scatter.relay(c - 1)
 
-    loop(count, work)
-    scatter.relay(count - 1)
-    c_in.wait()
-
     def middle(c):
         scatter.arrive(c)
         stats.arrive(c)
@@ -781,14 +792,33 @@
         loop(CHUNK // ROWS, piece)
         gather.start(c)
 
-    loop(count, middle)
+    c_in.wait()
+
+    def ahead(c):
+        work(c)
+
+        @pl.when(c >= 2)
+        def _():
+            middle(c - 2)
+
+    loop(count, ahead)
+    scatter.relay(count - 1)
+    middle(count - 2)
+    gather.relay(0)
+    middle(count - 1)
+    for c in range(1, count):
+        gather.relay(c)
 
     def gb1_out(c):
         return pltpu.make_async_copy(
             all1.at[chunk_rows(c)], gb1_hbm.at[chunk_rows(c)], out_sem.at[c]
         )
 
-    gather.take(count, lambda c: gb1_out(c).start())
+    def last(c):
+        gather.arrive(c)
+        gb1_out(c).start()
+
+    loop(count, last)
 
     def drain(c):
         gb1_out(c).wait()
@@ -1188,7 +1218,7 @@
     features = w_query.shape[0]
     units = w_gate.shape[1]
     chunks = tokens // CHUNK
-    assert tokens == LENGTH and stream_count == 4
+    assert tokens == LENGTH == 4 * CHUNK and stream_count == 4
     any_spec = pl.BlockSpec(memory_space=pl.ANY)
     vmem = pl.BlockSpec(memory_space=pltpu.VMEM)
     smem = pl.BlockSpec(memory_space=pltpu.SMEM)
@@ -1219,6 +1249,7 @@
     def small(form, left, right):
         return jnp.einsum(form, left, right, precision=PRECISE)
 
+    planes = jnp.transpose(streams, (1, 0, 2))
     mixes = (mix_in1, mix_out1, mix_in2, mix_out2, mix_res1, mix_res2)
 
     def stats_scratch():
@@ -1230,7 +1261,7 @@
         ]
 
     (
-        normed1, queries, keys, values, stand1, scale1, grad_branch2, planes, cot_planes,
+        normed1, queries, keys, values, stand1, scale1, grad_branch2, cot_planes,
         cos_table, sin_table, seg_column, seg_row,
     ) = pl.pallas_call(
         functools.partial(project_kernel, n),
@@ -1245,25 +1276,23 @@
             array((tokens, 128), F32),
             array((tokens, features), BF16),
             array((stream_count, tokens, width), BF16),
-            array((stream_count, tokens, width), BF16),
             array((tokens, HEAD), F32),
             array((tokens, HEAD), F32),
             array((tokens, 128), F32),
             array((8, tokens), F32),
         ],
         in_specs=[smem, smem, vmem, vmem] + [any_spec] * 5,
-        out_specs=[any_spec] + [vmem] * 5 + [any_spec] * 3 + [vmem] * 4,
+        out_specs=[any_spec] + [vmem] * 5 + [any_spec] * 2 + [vmem] * 4,
         scratch_shapes=[
+            pltpu.VMEM((stream_count, tokens, width), BF16),
             pltpu.VMEM((tokens, stream_count, width), BF16),
-            pltpu.VMEM((tokens, stream_count, width), BF16),
-            pltpu.VMEM((stream_count, tokens, width), BF16),
             pltpu.VMEM((stream_count, tokens, width), BF16),
             pltpu.VMEM((3, features, width), BF16),
             pltpu.VMEM((tokens, features), BF16),
             pltpu.VMEM((tokens, features), BF16),
         ]
         + stats_scratch()
-        + [dma(2, chunks), dma(3), dma(4, chunks)]
+        + [dma(2, chunks), dma(3), dma(3, chunks)]
         + gather_sems
         + gather_sems
         + stats_sems,
@@ -1271,11 +1300,11 @@
     )(
         mix_in1, mix_out2,
         positions.reshape(tokens // 128, 128), segments.reshape(tokens // 128, 128),
-        streams, cotangent, w_query, w_key, w_value,
+        planes, cotangent, w_query, w_key, w_value,
     )
 
     extent = window(0, tokens)[1]
-    attended, branch1, normed2, stand2, scale2, hidden, grad_acts = pl.pallas_call(
+    attended, branch1, normed2, stand2, scale2, hidden, grad_acts, _ = pl.pallas_call(
         functools.partial(attend_kernel, n),
         name="attend",
         cost_estimate=lasts(100),
@@ -1287,9 +1316,10 @@
             array((tokens, 128), F32),
             array((tokens, units), BF16),
             array((tokens, 2 * units), BF16),
+            array((tokens, units), BF16),
         ],
         in_specs=[smem] * 6 + [vmem] * 6 + [any_spec] * 5,
-        out_specs=[vmem, vmem, any_spec, vmem, vmem, any_spec, any_spec],
+        out_specs=[vmem, vmem, any_spec, vmem, vmem, any_spec, any_spec, any_spec],
         scratch_shapes=[
             pltpu.VMEM((2, stream_count, CHUNK, width), BF16),
             pltpu.VMEM((2, CHUNK, features), BF16),
@@ -1304,7 +1334,8 @@
             pltpu.VMEM((tokens, features), BF16),
         ]
         + stats_scratch()
-        + [pltpu.VMEM((CHUNK, extent), F32), dma(2), dma(2), dma(3), dma(chunks), dma(3, 2)]
+        + [pltpu.VMEM((CHUNK, extent), F32), dma(2), dma(2), dma(2, 2)]
+        + [dma(3), dma(chunks), dma(3, 2)]
         + scatter_sems
         + gather_sems
         + stats_sems,

time: 578 us -> 559 us (0.967)
  Pallas kernels: 471 us -> 459 us
  matrix products: 68.6 us -> 57.3 us
    pallas_call x1, Pallas kernels: 109 us -> 93.2 us  [on_device(): pl.pallas_call(functools.partial(attend_kernel, n), name='attend', cost_e...]
    dot_general x4, matrix products: 64.9 us -> 53.7 us  [contract_rows(): lax.dot_general(left, right, (((0,), (0,)), ((), ())), preferred_element_...]
    pallas_call x1, Pallas kernels: 72.1 us -> 79.2 us  [on_device(): pl.pallas_call(functools.partial(finish_kernel, n), name='finish', cost_e...]
    pallas_call x1, Pallas kernels: 90.2 us -> 84 us  [on_device(): pl.pallas_call(functools.partial(project_kernel, n), name='project', cost...]
  transfers between devices with their start and end apart: 2 -> 2, of which waited for: 0 -> 0; matrix products, arithmetic and copies ran while one was open for 10% -> 9% of each run, Pallas kernels for 48% -> 51%
where the time goes in v4:
time: 559 us; the launch traced here: 548 us
  Pallas kernels  459 us (82%)
  matrix products  57.3 us (10%)
  between operations  14.7 us (3%)
  local copies, waits for them, and re-layouts  11.7 us (2%)
  other arithmetic  5.66 us (1%)
    pallas_call x1, Pallas kernels, on_device(): pl.pallas_call(functools.partial(attend_kernel, n), name='attend', cost_e...  93.2 us
    pallas_call x1, Pallas kernels, on_device(): pl.pallas_call(functools.partial(units_back_kernel, n), name='units_back'...  90.6 us
    pallas_call x1, Pallas kernels, on_device(): pl.pallas_call(functools.partial(attend_back_kernel, n), name='attend_bac...  89.8 us
    pallas_call x1, Pallas kernels, on_device(): pl.pallas_call(functools.partial(project_kernel, n), name='project', cost...  84 us
    pallas_call x1, Pallas kernels, on_device(): pl.pallas_call(functools.partial(finish_kernel, n), name='finish', cost_e...  79.2 us
    dot_general x4, matrix products, contract_rows(): lax.dot_general(left, right, (((0,), (0,)), ((), ())), preferred_element_...  53.7 us
    pallas_call x1, Pallas kernels, on_device(): pl.pallas_call(streams_kernel, name='streams', cost_estimate=lasts(2), gr...  21.8 us
  transfers between devices with their start and end apart: 2, of which 0 were waited for; matrix products, arithmetic and copies ran while one was open for 9% of the time, Pallas kernels for 51%

profile of v4, /device:TPU:0, one launch (start us, length us, event | category | flops | bytes accessed | tf_op | source)
XLA Modules:
  0.0 548.1 jit_solution(11089933317790081359)
XLA Ops:
  7.2 0.0 reduce-scatter.3.cloned.1.call-start
  7.2 5.0 copy.35
  12.2 84.0 %project.1 = (bf16[1024,2048]{1,0:T(8,128)(2,1)}, bf16[1024,512]{1,0:T(8,128)(2,1)}, bf16[1024,512]{1,0:T(8,128)(2,1)}, bf16[1024,512]{1,0:T(8,128)(2,1)}, f32[1...) custom-call(f32[4]{0:T(128)} %in1.7, f32[4]{0:T(128)} %out2.7, ...), custom_call_target="tpu_custom_call" | custom-call | flops 99999997952 | bytes 360000000 | tf_op jit(solution)/shard_map/project/pallas_call | solution.py:1266
  96.2 93.2 %attend.1 = (bf16[1024,512]{1,0:T(8,128)(2,1)}, f32[1024,512]{1,0:T(8,128)}, bf16[1024,2048]{1,0:T(8,128)(2,1)}, f32[1024,512]{1,0:T(8,128)}, f32[1024,128]{1,0:...) custom-call(f32[4]{0:T(128)} %in1.7, f32[4]{0:T(128)} %out1.5, ...), custom_call_target="tpu_custom_call" | custom-call | flops 99999997952 | bytes 360000000 | tf_op jit(solution)/shard_map/attend/pallas_call | solution.py:1307
  189.4 14.0 %convolution_convert_fusion.2._down = bf16[2048,2048]{1,0:T(8,128)(2,1)} fusion(bf16[1024,2048]{1,0:T(8,128)(2,1)} %get-tuple-element.63.hidden_hbm, bf16[1024,2048]{1,0:T(8,128)(2,1)} %get-tuple-element.53.gb2_hbm), kind=kOutput, calls=%fused_computation.2 | convolution fusion | flops 8594128896 | bytes 16777216 | tf_op jit(solution)/shard_map/dot_general | solution.py:48
  203.4 0.0 reduce-scatter.3.cloned.1.call-update
  203.5 0.0 reduce-scatter.5.cloned.1.call-start
  203.5 24.9 %convolution_convert_fusion._gate_up = bf16[2048,4096]{1,0:T(8,128)(2,1)} fusion(bf16[1024,2048]{1,0:T(8,128)(2,1)} %get-tuple-element.60.normed_ref, bf16[1024,4096]{1,0:T(8,128)(2,1)} %get-tuple-element.59.acts_ref), kind=kOutput, calls=%fused_computation | convolution fusion | flops 17188257792 | bytes 29360128 | tf_op jit(solution)/shard_map/dot_general | solution.py:48
  228.4 0.0 reduce-scatter.5.cloned.1.call-update
  228.4 0.0 copy-start.12
  228.4 90.6 %units_back.1 = (f32[1024,512]{1,0:T(8,128)}, bf16[1024,2048]{1,0:T(8,128)(2,1)}) custom-call(f32[4]{0:T(128)} %in1.7, f32[4]{0:T(128)} %out1.5, f32[4]{0:T(128)} %in2.5, f32[4]{0:T(128)} %out2.7, f32[4,4]{1,0:T(4,128)} %res1.5, f32[4,4]{1,0:T(4,128)} %res2.5, bf16[1024,4096]{1,0:T(8,128)(2,1)} %get-tuple-element.59.acts_ref, bf16[2048,2048]{1,0:T(8,128)(2,1)} %wg_ref.1, ...), custom_call_target="tpu_custom_call" | custom-call | flops 399999991808 | bytes 1440000000 | tf_op jit(solution)/shard_map/units_back/pallas_call | solution.py:1359
  319.1 0.0 copy-done.12
  319.1 5.9 %convolution_convert_fusion.3._output.last_hbm = bf16[2048,512]{1,0:T(8,128)(2,1)} fusion(bf16[1024,2048]{1,0:T(8,128)(2,1)} %get-tuple-element.64.gb1_hbm, bf16[1024,512]{1,0:T(8,128)(2,1)S(1)} %copy-done.12), kind=kOutput, calls=%fused_computation.4 | convolution fusion | flops 2148532224 | bytes 7340032 | tf_op jit(solution)/shard_map/dot_general | solution.py:48
  325.0 0.0 copy-start.5
  325.0 0.0 copy-start.6
  325.0 0.0 copy-start.7
  325.0 0.0 copy-start.8
  325.1 89.8 %attend_back.1 = (bf16[1024,1536]{1,0:T(8,128)(2,1)}, f32[1024,512]{1,0:T(8,128)}, f32[1024,512]{1,0:T(8,128)}) custom-call(bf16[1024,512]{1,0:T(8,128)(2,1)} %get-tuple-element.48.q_ref, bf16[1024,512]{1,0:T(8,128)(2,1)} %get-tuple-element.49.k_ref, bf16[1024,512]{1,0:T(8,128)(2,1)} %get-tuple-element.50.v_ref, f32[1024,128]{1,0:T(8,128)} %get-tuple-element.51.segc_ref, ...), custom_call_target="tpu_custom_call" | custom-call | flops 2000000000 | bytes 7200000 | tf_op jit(solution)/shard_map/attend_back/pallas_call | solution.py:1390
  414.8 0.0 copy-done.1
  414.8 0.0 copy-done.3
  414.9 0.0 copy-done.4
  414.9 0.0 copy-done.5
  414.9 0.0 copy-done.6
  414.9 0.0 copy-done.7
  414.9 0.0 copy-done.8
  414.9 0.0 copy-start.2
  414.9 1.6 copy-done.2
  416.5 21.8 %streams.1 = (bf16[1024,4,512]{2,1,0:T(4,128)(2,1)}, f32[1024,4,512]{2,1,0:T(4,128)}, f32[33,8,128]{2,1,0:T(8,128)S(1)}) custom-call(f32[4]{0:T(128)S(1)} %copy-done.5, f32[4]{0:T(128)S(1)} %copy-done.7, f32[4]{0:T(128)S(1)} %copy-done.8, f32[4]{0:T(128)S(1)} %copy-done.6, f32[4,4]{1,0:T(4,128)S(1)} %copy-done.3, f32[4,4]{1,0:T(4,128)S(1)} %copy-done.4, ...), custom_call_target="tpu_custom_call" | custom-call | flops 2000000000 | bytes 7200000 | tf_op jit(solution)/shard_map/streams/pallas_call | solution.py:1431
  438.3 0.0 copy-done.11
  438.3 0.0 copy-start
  438.3 8.8 %convolution_convert_fusion.1.first_hbm = bf16[2048,1536]{1,0:T(8,128)(2,1)} fusion(bf16[1024,2048]{1,0:T(8,128)(2,1)S(1)} %copy-done.10, bf16[1024,1536]{1,0:T(8,128)(2,1)S(1)} %copy-done.11), kind=kOutput, calls=%fused_computation.1 | convolution fusion | flops 6445596672 | bytes 13631488 | tf_op jit(solution)/shard_map/dot_general | solution.py:48
  447.2 0.0 copy-done
  447.2 79.2 %finish.1 = (f32[256,512]{1,0:T(8,128)S(1)}, f32[256,512]{1,0:T(8,128)S(1)}, f32[256,512]{1,0:T(8,128)S(1)}, f32[512,256]{1,0:T(8,128)S(1)}, f32[40,128]{1,0:T(8,128)S(1)}) custom-call(bf16[2048,1536]{1,0:T(8,128)(2,1)} %convolution_convert_fusion.1.first_hbm, bf16[2048,512]{1,0:T(8,128)(2,1)S(1)} %copy-done, f32[33,8,128]{2,1,0:T(8,128)S(1)} %get-tuple-element.73.sums_ref), custom_call_target="tpu_custom_call" | custom-call | flops 2000000000 | bytes 7200000 | tf_op jit(solution)/shard_map/finish/pallas_call | solution.py:1452
  526.4 0.1 slice_reduce_fusion
  526.5 0.6 slice.34
  527.1 0.1 reshape.45
  527.2 0.6 fusion.7
  527.7 0.2 fusion
  527.9 0.7 copy.33
  528.6 1.5 convert_element_type.27
  530.1 1.4 fusion.2
  531.5 1.4 fusion.1
  532.8 0.7 convolution_add_fusion
  533.5 4.1 slice_convert_fusion
  537.6 0.8 copy.40
  538.4 0.8 copy.41
  539.2 0.8 copy.42
  540.0 0.8 copy.43
  (10 shorter events, 0.0 us)
Async XLA Ops:
  7.2 317.8 %reduce-scatter.3.cloned.1.call-start = ((), (), s32[]{:S(2)}) async-start(), calls=%async_computation.2 | async-start | bytes 9437184 | tf_op jit(solution)/shard_map/reduce_scatter | solution.py:1349
  203.5 330.1 %reduce-scatter.5.cloned.1.call-start = ((), (), s32[]{:S(2)}) async-start(), calls=%async_computation.3 | async-start | bytes 18874368 | tf_op jit(solution)/shard_map/reduce_scatter | solution.py:1349
  228.4 90.7 %copy-start.12 = (bf16[1024,512]{1,0:T(8,128)(2,1)S(1)}, bf16[1024,512]{1,0:T(8,128)(2,1)}, u32[]{:S(2)}) copy-start(bf16[1024,512]{1,0:T(8,128)(2,1)} %get-tuple-element.66) | copy-start | bytes 3145732
  325.0 89.8 %copy-start.1 = (f32[1024,512]{1,0:T(8,128)S(1)}, f32[1024,512]{1,0:T(8,128)}, u32[]{:S(2)}) copy-start(f32[1024,512]{1,0:T(8,128)} %get-tuple-element.54.b1_ref) | copy-start | bytes 6291460
  325.0 89.9 %copy-start.3 = (f32[4,4]{1,0:T(4,128)S(1)}, f32[4,4]{1,0:T(4,128)}, u32[]{:S(2)}) copy-start(f32[4,4]{1,0:T(4,128)} %res1.5) | copy-start | bytes 196
  325.0 89.9 %copy-start.4 = (f32[4,4]{1,0:T(4,128)S(1)}, f32[4,4]{1,0:T(4,128)}, u32[]{:S(2)}) copy-start(f32[4,4]{1,0:T(4,128)} %res2.5) | copy-start | bytes 196
  325.0 89.9 %copy-start.5 = (f32[4]{0:T(128)S(1)}, f32[4]{0:T(128)}, u32[]{:S(2)}) copy-start(f32[4]{0:T(128)} %in1.7) | copy-start | bytes 52
  325.0 89.9 %copy-start.6 = (f32[4]{0:T(128)S(1)}, f32[4]{0:T(128)}, u32[]{:S(2)}) copy-start(f32[4]{0:T(128)} %out2.7) | copy-start | bytes 52
  325.0 89.9 %copy-start.7 = (f32[4]{0:T(128)S(1)}, f32[4]{0:T(128)}, u32[]{:S(2)}) copy-start(f32[4]{0:T(128)} %out1.5) | copy-start | bytes 52
  325.0 89.9 %copy-start.8 = (f32[4]{0:T(128)S(1)}, f32[4]{0:T(128)}, u32[]{:S(2)}) copy-start(f32[4]{0:T(128)} %in2.5) | copy-start | bytes 52
  414.9 1.6 copy-start.2
  416.5 21.8 %copy-start.10 = (bf16[1024,2048]{1,0:T(8,128)(2,1)S(1)}, bf16[1024,2048]{1,0:T(8,128)(2,1)}, u32[]{:S(2)}) copy-start(bf16[1024,2048]{1,0:T(8,128)(2,1)} %get-tuple-element.65.normed_hbm) | copy-start | bytes 12582916
  416.5 21.8 %copy-start.11 = (bf16[1024,1536]{1,0:T(8,128)(2,1)S(1)}, bf16[1024,1536]{1,0:T(8,128)(2,1)}, u32[]{:S(2)}) copy-start(bf16[1024,1536]{1,0:T(8,128)(2,1)} %get-tuple-element.72) | copy-start | bytes 9437188
  438.3 8.9 %copy-start = (bf16[2048,512]{1,0:T(8,128)(2,1)S(1)}, bf16[2048,512]{1,0:T(8,128)(2,1)}, u32[]{:S(2)}) copy-start(bf16[2048,512]{1,0:T(8,128)(2,1)} %convolution_convert_fusion.3._output.last_hbm) | copy-start | bytes 6291460
  447.2 81.5 %copy-start.9 = (bf16[2048,256]{1,0:T(8,128)(2,1)S(1)}, bf16[2048,256]{1,0:T(8,128)(2,1)}, u32[]{:S(2)}) copy-start(bf16[2048,256]{1,0:T(8,128)(2,1)} %reduce-scatter.3.cloned.1.call-done._down) | copy-start | bytes 3145732
Sparse Core Ops, SparseCore 0:
  203.6 89.8 reduce-scatter.2
  295.8 172.2 reduce-scatter.4

commit v5 on v4

--- a/solution.py
+++ b/solution.py
@@ -998,6 +998,100 @@
 CORES = 2
 SUMS = 33
 SUM_ROWS = 40
+
+
+def pair_kernel(
+    left_hbm, right_hbm, out_hbm, left, right, turned, sent, came, mine_buf,
+    left_sem, right_sem, out_sem, send_sem, recv_sem,
+):
+    steps, height, width = came.shape
+    block = height // 2
+    piece = right_sem.shape[0]
+    across = width // piece
+    me = lax.axis_index("dp")
+    mine = lax.rem(me, CORES)
+    partner = me + 1 - 2 * mine
+
+    def left_in(step, half, part):
+        index = (2 * step + part) * CORES + half
+        return pltpu.make_async_copy(
+            left_hbm.at[:, columns(index, block)],
+            left.at[2 * step + part, half],
+            left_sem.at[2 * step + part, half],
+        )
+
+    def right_in(f):
+        return pltpu.make_async_copy(
+            right_hbm.at[:, columns(f, across)], right.at[:, columns(f, across)], right_sem.at[f]
+        )
+
+    def swap(step):
+        return pltpu.make_async_remote_copy(
+            src_ref=sent.at[step],
+            dst_ref=came.at[step],
+            send_sem=send_sem.at[step],
+            recv_sem=recv_sem.at[step],
+            device_id={"dp": partner},
+            device_id_type=MESH,
+        )
+
+    def out(step):
+        rows = pl.ds(pl.multiple_of(step * height, height), height)
+        return pltpu.make_async_copy(mine_buf.at[step], out_hbm.at[rows], out_sem.at[step])
+
+    for part in range(2):
+        left_in(0, 1 - mine, part).start()
+    for f in range(piece):
+        right_in(f).start()
+    for half in (1 - mine, mine):
+        for step in range(steps):
+            for part in range(2):
+                if half is mine or step > 0:
+                    left_in(step, half, part).start()
+    barrier = pltpu.get_barrier_semaphore()
+    pl.semaphore_signal(barrier, inc=1, device_id={"dp": partner}, device_id_type=MESH)
+    pl.semaphore_wait(barrier, 1)
+
+    def turn(step, half):
+        for part in range(2):
+            left_in(step, half, part).wait()
+            turned[part * block : (part + 1) * block, :] = jnp.transpose(left[2 * step + part, half])
+
+    def other(step):
+        turn(step, 1 - mine)
+
+        def part(f):
+            @pl.when(step == 0)
+            def _():
+                right_in(f).wait()
+
+            place = columns(f, across)
+            sent[step, :, place] = dot_nn(turned[...], right[:, place]).astype(BF16)
+
+        loop(piece, part)
+        swap(step).start()
+
+    loop(steps, other)
+
+    def own(step):
+        turn(step, mine)
+        swap(step).wait_recv()
+
+        def part(f):
+            place = columns(f, across)
+            total = dot_nn(turned[...], right[:, place]) + came[step, :, place].astype(F32)
+            mine_buf[step, :, place] = total.astype(BF16)
+
+        loop(piece, part)
+        out(step).start()
+
+    loop(steps, own)
+
+    def drain(step):
+        swap(step).wait_send()
+        out(step).wait()
+
+    loop(steps, drain)
 
 
 def finish_kernel(
@@ -1348,11 +1442,46 @@
     def over_dp(partial, dimension):
         return lax.psum_scatter(partial, "dp", scatter_dimension=dimension, tiled=True)
 
-    part_down = contract_rows(hidden, grad_branch2).astype(BF16)
-    part_gate_up = contract_rows(normed2, grad_acts).astype(BF16)
-    grad_down = over_dp(part_down, 1)
-    grad_gate_up = over_dp(part_gate_up, 0)
-    grad_w_down = grad_down.astype(F32)
+    height = features // replicas
+    paired = replicas == PLANES * CORES
+
+    def weight_sum(identity, left, right):
+        if not paired:
+            partial = contract_rows(left, right).astype(BF16)
+            return over_dp(partial, 0), partial
+        steps, columns_in = PLANES // 2, right.shape[1]
+        pieces = max(columns_in // 1024, 1)
+        partial = pl.pallas_call(
+            pair_kernel,
+            name="pair",
+            cost_estimate=lasts(20),
+            out_shape=array((features // CORES, columns_in), BF16),
+            in_specs=[any_spec, any_spec],
+            out_specs=any_spec,
+            scratch_shapes=[
+                pltpu.VMEM((PLANES, CORES, tokens, height), BF16),
+                pltpu.VMEM((tokens, columns_in), BF16),
+                pltpu.VMEM((2 * height, tokens), BF16),
+                pltpu.VMEM((steps, 2 * height, columns_in), BF16),
+                pltpu.VMEM((steps, 2 * height, columns_in), BF16),
+                pltpu.VMEM((steps, 2 * height, columns_in), BF16),
+                dma(PLANES, CORES),
+                dma(pieces),
+                dma(steps),
+                dma(steps),
+                dma(steps),
+            ],
+            compiler_params=params(identity, 56),
+        )(left, right)
+        groups = [[CORES * plane + c for plane in range(PLANES)] for c in range(CORES)]
+        total = lax.psum_scatter(
+            partial, "dp", scatter_dimension=0, tiled=True, axis_index_groups=groups
+        )
+        return total, partial
+
+    grad_down, part_down = weight_sum(5, grad_branch2, hidden)
+    grad_gate_up, part_gate_up = weight_sum(6, normed2, grad_acts)
+    grad_w_down = jnp.transpose(grad_down).astype(F32)
     grad_w_gate = grad_gate_up[:, :units].astype(F32)
     grad_w_up = grad_gate_up[:, units:].astype(F32)
 
@@ -1419,7 +1548,7 @@
     )(
         queries, keys, values, seg_column, seg_row, cos_table, sin_table,
         w_output, w_query, w_key, w_value, w_down, stand1, scale1,
-        grad_branch1, hidden, normed1, part_output, grad_down,
+        grad_branch1, hidden, normed1, part_output, grad_w_down,
     )
 
     part_lin = contract_rows(normed1, grad_lin).astype(BF16)
@@ -1446,8 +1575,7 @@
         ],
         compiler_params=pltpu.CompilerParams(vmem_limit_bytes=48 * MIB),
     )(*mixes, planes, cot_planes, branch1, branch2, grad_entry1, grad_entry2)
-    height = features // replicas
-    if replicas == PLANES * CORES and stream_count == 4:
+    if paired:
         steps = PLANES - 1
         grad_w_query, grad_w_key, grad_w_value, grad_w_output, sums = pl.pallas_call(
             functools.partial(finish_kernel, n),

time: 559 us -> 579 us (1.036)
  Pallas kernels: 459 us -> 510 us
  matrix products: 57.3 us -> 18.4 us
  local copies, waits for them, and re-layouts: 11.7 us -> 18.1 us
    pallas_call x0 -> x2, Pallas kernels: none -> 44.5 us  [weight_sum(): pl.pallas_call(pair_kernel, name='pair', cost_estimate=lasts(20), out_sha...]
    dot_general x4 -> x2, matrix products: 53.7 us -> 14.8 us  [contract_rows(): lax.dot_general(left, right, (((0,), (0,)), ((), ())), preferred_element_...]
    pallas_call x1, Pallas kernels: 89.8 us -> 99.8 us  [on_device(): pl.pallas_call(functools.partial(attend_back_kernel, n), name='attend_bac...]
    pallas_call x0 -> x1, local copies, waits for them, and re-layouts: none -> 6.4 us  [weight_sum(): pl.pallas_call(pair_kernel, name='pair', cost_estimate=lasts(20), out_sha...]
  transfers between devices with their start and end apart: 2 -> 2, of which waited for: 0 -> 0; matrix products, arithmetic and copies ran while one was open for 9% -> 4% of each run, Pallas kernels for 51% -> 56%
where the time goes in v5:
time: 579 us; the launch traced here: 568 us
  Pallas kernels  510 us (88%)
  matrix products  18.4 us (3%)
  local copies, waits for them, and re-layouts  18.1 us (3%)
  between operations  14.4 us (2%)
  other arithmetic  6.88 us (1%)
    pallas_call x1, Pallas kernels, on_device(): pl.pallas_call(functools.partial(attend_back_kernel, n), name='attend_bac...  99.8 us
    pallas_call x1, Pallas kernels, on_device(): pl.pallas_call(functools.partial(attend_kernel, n), name='attend', cost_e...  93 us
    pallas_call x1, Pallas kernels, on_device(): pl.pallas_call(functools.partial(units_back_kernel, n), name='units_back'...  92.3 us
    pallas_call x1, Pallas kernels, on_device(): pl.pallas_call(functools.partial(project_kernel, n), name='project', cost...  83.9 us
    pallas_call x1, Pallas kernels, on_device(): pl.pallas_call(functools.partial(finish_kernel, n), name='finish', cost_e...  74.8 us
    pallas_call x2, Pallas kernels, weight_sum(): pl.pallas_call(pair_kernel, name='pair', cost_estimate=lasts(20), out_sha...  44.5 us
    pallas_call x1, Pallas kernels, on_device(): pl.pallas_call(streams_kernel, name='streams', cost_estimate=lasts(2), gr...  21.7 us
    dot_general x2, matrix products, contract_rows(): lax.dot_general(left, right, (((0,), (0,)), ((), ())), preferred_element_...  14.8 us
  transfers between devices with their start and end apart: 2, of which 0 were waited for; matrix products, arithmetic and copies ran while one was open for 4% of the time, Pallas kernels for 56%

profile of v5, /device:TPU:0, one launch (start us, length us, event | category | flops | bytes accessed | tf_op | source)
XLA Modules:
  0.0 568.1 jit_solution(5929190245869475541)
XLA Ops:
  7.2 0.0 reduce-scatter.3.cloned.1.call-start
  7.2 5.0 copy.36
  12.2 83.9 %project.1 = (bf16[1024,2048]{1,0:T(8,128)(2,1)}, bf16[1024,512]{1,0:T(8,128)(2,1)}, bf16[1024,512]{1,0:T(8,128)(2,1)}, bf16[1024,512]{1,0:T(8,128)(2,1)}, f32[1...) custom-call(f32[4]{0:T(128)} %in1.7, f32[4]{0:T(128)} %out2.7, ...), custom_call_target="tpu_custom_call" | custom-call | flops 99999997952 | bytes 360000000 | tf_op jit(solution)/shard_map/project/pallas_call | solution.py:1360
  96.1 93.0 %attend.1 = (bf16[1024,512]{1,0:T(8,128)(2,1)}, f32[1024,512]{1,0:T(8,128)}, bf16[1024,2048]{1,0:T(8,128)(2,1)}, f32[1024,512]{1,0:T(8,128)}, f32[1024,128]{1,0:...) custom-call(f32[4]{0:T(128)} %in1.7, f32[4]{0:T(128)} %out1.5, ...), custom_call_target="tpu_custom_call" | custom-call | flops 99999997952 | bytes 360000000 | tf_op jit(solution)/shard_map/attend/pallas_call | solution.py:1401
  189.1 15.4 %pair.2._down = bf16[1024,2048]{1,0:T(8,128)(2,1)} custom-call(bf16[1024,2048]{1,0:T(8,128)(2,1)} %get-tuple-element.53.gb2_hbm.left_hbm, bf16[1024,2048]{1,0:T(8,128)(2,1)} %get-tuple-element.63.right_hbm.hidden_hbm), custom_call_target="tpu_custom_call" | custom-call | flops 20000000000 | bytes 72000000 | tf_op jit(solution)/shard_map/pair/pallas_call | solution.py:1454
  204.6 6.4 %copy.33 = bf16[1024,2048]{0,1:T(8,128)(2,1)} copy(bf16[1024,2048]{1,0:T(8,128)(2,1)} %pair.2._down) | data formatting | bytes 8388608 | tf_op jit(solution)/shard_map/pair/pallas_call | solution.py:1454
  211.0 0.0 reduce-scatter.3.cloned.1.call-update
  211.0 0.0 reduce-scatter.5.cloned.1.call-start
  211.0 29.1 %pair.3._gate_up = bf16[1024,4096]{1,0:T(8,128)(2,1)} custom-call(bf16[1024,2048]{1,0:T(8,128)(2,1)} %get-tuple-element.60.left_hbm.normed_ref, bf16[1024,4096]{1,0:T(8,128)(2,1)} %get-tuple-element.59.right_hbm.acts_ref), custom_call_target="tpu_custom_call" | custom-call | flops 20000000000 | bytes 72000000 | tf_op jit(solution)/shard_map/pair/pallas_call | solution.py:1454
  240.2 0.0 reduce-scatter.5.cloned.1.call-update
  240.2 0.0 copy-start.11
  240.2 92.3 %units_back.1 = (f32[1024,512]{1,0:T(8,128)}, bf16[1024,2048]{1,0:T(8,128)(2,1)}) custom-call(f32[4]{0:T(128)} %in1.7, f32[4]{0:T(128)} %out1.5, f32[4]{0:T(128)} %in2.5, f32[4]{0:T(128)} %out2.7, f32[4,4]{1,0:T(4,128)} %res1.5, f32[4,4]{1,0:T(4,128)} %res2.5, bf16[1024,4096]{1,0:T(8,128)(2,1)} %get-tuple-element.59.right_hbm.acts_ref, ...), custom_call_target="tpu_custom_call" | custom-call | flops 399999991808 | bytes 1440000000 | tf_op jit(solution)/shard_map/units_back/pallas_call | solution.py:1488
  332.5 0.0 copy-done.11
  332.6 5.9 %convolution_convert_fusion.1._output.last_hbm = bf16[2048,512]{1,0:T(8,128)(2,1)} fusion(bf16[1024,2048]{1,0:T(8,128)(2,1)} %get-tuple-element.64.gb1_hbm, bf16[1024,512]{1,0:T(8,128)(2,1)S(1)} %copy-done.11), kind=kOutput, calls=%fused_computation.2 | convolution fusion | flops 2148532224 | bytes 7340032 | tf_op jit(solution)/shard_map/dot_general | solution.py:48
  338.4 2.7 convert_bitcast_fusion._down
  341.2 0.0 copy-start.6
  341.2 0.0 copy-start.7
  341.2 0.0 copy-start.8
  341.2 99.8 %attend_back.1 = (bf16[1024,1536]{1,0:T(8,128)(2,1)}, f32[1024,512]{1,0:T(8,128)}, f32[1024,512]{1,0:T(8,128)}) custom-call(bf16[1024,512]{1,0:T(8,128)(2,1)} %get-tuple-element.48.q_ref, bf16[1024,512]{1,0:T(8,128)(2,1)} %get-tuple-element.49.k_ref, bf16[1024,512]{1,0:T(8,128)(2,1)} %get-tuple-element.50.v_ref, f32[1024,128]{1,0:T(8,128)} %get-tuple-element.51.segc_ref, ...), custom_call_target="tpu_custom_call" | custom-call | flops 2000000000 | bytes 7200000 | tf_op jit(solution)/shard_map/attend_back/pallas_call | solution.py:1519
  441.1 0.0 copy-done.1
  441.1 0.0 copy-done.3
  441.1 0.0 copy-done.4
  441.1 0.0 copy-done.5
  441.1 0.0 copy-done.6
  441.1 0.0 copy-done.7
  441.1 0.0 copy-done.8
  441.1 0.0 copy-start.2
  441.1 1.6 copy-done.2
  442.7 21.7 %streams.1 = (bf16[1024,4,512]{2,1,0:T(4,128)(2,1)}, f32[1024,4,512]{2,1,0:T(4,128)}, f32[33,8,128]{2,1,0:T(8,128)S(1)}) custom-call(f32[4]{0:T(128)S(1)} %copy-done.5, f32[4]{0:T(128)S(1)} %copy-done.7, f32[4]{0:T(128)S(1)} %copy-done.8, f32[4]{0:T(128)S(1)} %copy-done.6, f32[4,4]{1,0:T(4,128)S(1)} %copy-done.3, f32[4,4]{1,0:T(4,128)S(1)} %copy-done.4, ...), custom_call_target="tpu_custom_call" | custom-call | flops 2000000000 | bytes 7200000 | tf_op jit(solution)/shard_map/streams/pallas_call | solution.py:1560
  464.4 0.0 copy-done.9
  464.5 0.0 copy-start
  464.5 8.9 %convolution_convert_fusion.first_hbm = bf16[2048,1536]{1,0:T(8,128)(2,1)} fusion(bf16[1024,2048]{1,0:T(8,128)(2,1)S(1)} %copy-done.9, bf16[1024,1536]{1,0:T(8,128)(2,1)S(1)} %copy-done.10), kind=kOutput, calls=%fused_computation | convolution fusion | flops 6445596672 | bytes 13631488 | tf_op jit(solution)/shard_map/dot_general | solution.py:48
  473.4 0.0 copy-done
  473.4 74.8 %finish.1 = (f32[256,512]{1,0:T(8,128)S(1)}, f32[256,512]{1,0:T(8,128)S(1)}, f32[256,512]{1,0:T(8,128)S(1)}, f32[512,256]{1,0:T(8,128)S(1)}, f32[40,128]{1,0:T(8,128)S(1)}) custom-call(bf16[2048,1536]{1,0:T(8,128)(2,1)} %convolution_convert_fusion.first_hbm, bf16[2048,512]{1,0:T(8,128)(2,1)S(1)} %copy-done, f32[33,8,128]{2,1,0:T(8,128)S(1)} %get-tuple-element.73.sums_ref), custom_call_target="tpu_custom_call" | custom-call | flops 2000000000 | bytes 7200000 | tf_op jit(solution)/shard_map/finish/pallas_call | solution.py:1580
  548.2 0.1 slice_reduce_fusion
  548.3 0.6 slice.34
  548.9 0.1 reshape.45
  548.9 0.6 fusion.7
  549.5 0.2 fusion
  549.7 0.7 copy.34
  550.4 1.4 fusion.2
  551.8 1.4 fusion.1
  553.1 0.7 convolution_add_fusion
  553.8 4.1 slice_convert_fusion
  557.9 0.8 copy.41
  558.7 0.8 copy.42
  559.5 0.8 copy.43
  560.3 0.8 copy.44
  (9 shorter events, 0.0 us)
Async XLA Ops:
  7.2 331.3 %reduce-scatter.3.cloned.1.call-start = ((), (), s32[]{:S(2)}) async-start(), calls=%async_computation.2 | async-start | bytes 5242880 | tf_op jit(solution)/shard_map/reduce_scatter | solution.py:1477
  211.0 342.8 %reduce-scatter.5.cloned.1.call-start = ((), (), s32[]{:S(2)}) async-start(), calls=%async_computation.3 | async-start | bytes 10485760 | tf_op jit(solution)/shard_map/reduce_scatter | solution.py:1477
  240.2 92.4 %copy-start.11 = (bf16[1024,512]{1,0:T(8,128)(2,1)S(1)}, bf16[1024,512]{1,0:T(8,128)(2,1)}, u32[]{:S(2)}) copy-start(bf16[1024,512]{1,0:T(8,128)(2,1)} %get-tuple-element.66) | copy-start | bytes 3145732
  341.2 99.9 %copy-start.1 = (f32[1024,512]{1,0:T(8,128)S(1)}, f32[1024,512]{1,0:T(8,128)}, u32[]{:S(2)}) copy-start(f32[1024,512]{1,0:T(8,128)} %get-tuple-element.54.b1_ref) | copy-start | bytes 6291460
  341.2 99.9 %copy-start.3 = (f32[4,4]{1,0:T(4,128)S(1)}, f32[4,4]{1,0:T(4,128)}, u32[]{:S(2)}) copy-start(f32[4,4]{1,0:T(4,128)} %res1.5) | copy-start | bytes 196
  341.2 99.9 %copy-start.4 = (f32[4,4]{1,0:T(4,128)S(1)}, f32[4,4]{1,0:T(4,128)}, u32[]{:S(2)}) copy-start(f32[4,4]{1,0:T(4,128)} %res2.5) | copy-start | bytes 196
  341.2 99.9 %copy-start.5 = (f32[4]{0:T(128)S(1)}, f32[4]{0:T(128)}, u32[]{:S(2)}) copy-start(f32[4]{0:T(128)} %in1.7) | copy-start | bytes 52
  341.2 99.9 %copy-start.6 = (f32[4]{0:T(128)S(1)}, f32[4]{0:T(128)}, u32[]{:S(2)}) copy-start(f32[4]{0:T(128)} %out2.7) | copy-start | bytes 52
  341.2 99.9 %copy-start.7 = (f32[4]{0:T(128)S(1)}, f32[4]{0:T(128)}, u32[]{:S(2)}) copy-start(f32[4]{0:T(128)} %out1.5) | copy-start | bytes 52
  341.2 99.9 %copy-start.8 = (f32[4]{0:T(128)S(1)}, f32[4]{0:T(128)}, u32[]{:S(2)}) copy-start(f32[4]{0:T(128)} %in2.5) | copy-start | bytes 52
  441.1 1.6 copy-start.2
  442.7 21.7 %copy-start.9 = (bf16[1024,2048]{1,0:T(8,128)(2,1)S(1)}, bf16[1024,2048]{1,0:T(8,128)(2,1)}, u32[]{:S(2)}) copy-start(bf16[1024,2048]{1,0:T(8,128)(2,1)} %get-tuple-element.65.normed_hbm) | copy-start | bytes 12582916
  442.7 21.7 %copy-start.10 = (bf16[1024,1536]{1,0:T(8,128)(2,1)S(1)}, bf16[1024,1536]{1,0:T(8,128)(2,1)}, u32[]{:S(2)}) copy-start(bf16[1024,1536]{1,0:T(8,128)(2,1)} %get-tuple-element.72) | copy-start | bytes 9437188
  464.5 8.9 %copy-start = (bf16[2048,512]{1,0:T(8,128)(2,1)S(1)}, bf16[2048,512]{1,0:T(8,128)(2,1)}, u32[]{:S(2)}) copy-start(bf16[2048,512]{1,0:T(8,128)(2,1)} %convolution_convert_fusion.1._output.last_hbm) | copy-start | bytes 6291460
Sparse Core Ops, SparseCore 0:
  211.1 77.5 reduce-scatter.2
  291.2 144.9 reduce-scatter.4

commit v6 on v5

--- a/solution.py
+++ b/solution.py
@@ -953,8 +953,13 @@
     loop(count, drain)
 
 
+def turn_kernel(source_ref, target_ref):
+    target_ref[...] = jnp.transpose(source_ref[...].astype(F32))
+
+
 def streams_kernel(
-    in1, out1, in2, out2, res1, res2, s_ref, c_ref, b1_ref, b2_ref, e1_ref, e2_ref, new_ref, grad_ref, sums_ref
+    in1, out1, in2, out2, res1, res2, s_ref, c_ref, b1_ref, b2_ref, e1_ref, e2_ref,
+    new_ref, grad_ref, mix_ref, sums_ref,
 ):
     @pl.when(pl.program_id(0) == 0)
     def _():
@@ -993,11 +998,33 @@
 
     loop(s_ref.shape[1] // 16, piece)
 
+    @pl.when(pl.program_id(0) == pl.num_programs(0) - 1)
+    def _():
+        sums = [sums_ref[place] for place in range(PRODUCTS)]
+        s_c = [sums[count * i : count * (i + 1)] for i in range(count)]
+        s_e1, s_e2, c_b1, c_b2 = (sums[16 + 4 * k : 20 + 4 * k] for k in range(4))
+        b_e = sums[32]
+        every = range(count)
+        row1, row2 = mixing.res1, mixing.res2
+        grads = [s_e1[i] for i in every]
+        grads += [inner(row2[j], s_c[i]) + mixing.in2[j] * s_e2[i] for i in every for j in every]
+        grads += [inner(row2[j], c_b1) + mixing.in2[j] * b_e for j in every]
+        turned1 = [[row1[k][i] for k in every] for i in every]
+        grads += [inner(turned1[i], s_e2) + mixing.out1[i] * b_e for i in every]
+        grads += [
+            inner(turned1[i], [s_c[k][j] for k in every]) + mixing.out1[i] * c_b1[j]
+            for i in every
+            for j in every
+        ]
+        grads += [c_b2[j] for j in every]
+        for place, field in enumerate(grads):
+            mix_ref[place] = field
+
 
 PLANES = 4
 CORES = 2
-SUMS = 33
-SUM_ROWS = 40
+PRODUCTS = 33
+SUMS = 48
 
 
 def pair_kernel(
@@ -1164,8 +1191,7 @@
         pl.semaphore_signal(barrier, inc=1, device_id={"tensor": peers[k]}, device_id_type=MESH)
     pl.semaphore_wait(barrier, 1 + PLANES - 1 + n - 1)
 
-    by_core[mine] = jnp.zeros((SUM_ROWS, 128), F32)
-    by_core[mine, 0:SUMS] = jnp.sum(sums_ref[...], axis=1)
+    by_core[mine] = jnp.sum(sums_ref[...], axis=1)
     over_dp(
         by_core.at[mine], by_core.at[mine], sum_send.at[0], sum_recv.at[0], partner
     ).start()
@@ -1339,9 +1365,6 @@
         return pltpu.CompilerParams(
             collective_id=identity, has_side_effects=True, vmem_limit_bytes=mib * MIB
         )
-
-    def small(form, left, right):
-        return jnp.einsum(form, left, right, precision=PRECISE)
 
     planes = jnp.transpose(streams, (1, 0, 2))
     mixes = (mix_in1, mix_out1, mix_in2, mix_out2, mix_res1, mix_res2)
@@ -1480,8 +1503,17 @@
         return total, partial
 
     grad_down, part_down = weight_sum(5, grad_branch2, hidden)
-    grad_gate_up, part_gate_up = weight_sum(6, normed2, grad_acts)
-    grad_w_down = jnp.transpose(grad_down).astype(F32)
+    part_gate_up = contract_rows(normed2, grad_acts).astype(BF16)
+    grad_gate_up = over_dp(part_gate_up, 0)
+    grad_w_down = pl.pallas_call(
+        turn_kernel,
+        name="turn",
+        cost_estimate=lasts(2),
+        out_shape=array((units, height), F32),
+        in_specs=[vmem],
+        out_specs=vmem,
+        compiler_params=pltpu.CompilerParams(vmem_limit_bytes=32 * MIB),
+    )(grad_down)
     grad_w_gate = grad_gate_up[:, :units].astype(F32)
     grad_w_up = grad_gate_up[:, units:].astype(F32)
 
@@ -1573,6 +1605,7 @@
             stream_spec,
             pl.BlockSpec((SUMS, 8, 128), lambda t: (0, 0, 0)),
         ],
+        scratch_shapes=[pltpu.VMEM((PRODUCTS, 8, 128), F32)],
         compiler_params=pltpu.CompilerParams(vmem_limit_bytes=48 * MIB),
     )(*mixes, planes, cot_planes, branch1, branch2, grad_entry1, grad_entry2)
     if paired:
@@ -1582,7 +1615,7 @@
             name="finish",
             cost_estimate=lasts(2),
             out_shape=[array((height, width), F32)] * 3
-            + [array((width, height), F32), array((SUM_ROWS, 128), F32)],
+            + [array((width, height), F32), array((SUMS, 128), F32)],
             in_specs=[any_spec, any_spec, vmem],
             out_specs=[vmem] * 5,
             scratch_shapes=[
@@ -1590,9 +1623,9 @@
                 pltpu.VMEM((PLANES, 4, height, width), BF16),
                 pltpu.VMEM((steps, 4, height, width), BF16),
                 pltpu.VMEM((steps, 4, height, width), BF16),
-                pltpu.VMEM((CORES, SUM_ROWS, 128), F32),
-                pltpu.VMEM((PLANES, SUM_ROWS, 128), F32),
-                pltpu.VMEM((n, SUM_ROWS, 128), F32),
+                pltpu.VMEM((CORES, SUMS, 128), F32),
+                pltpu.VMEM((PLANES, SUMS, 128), F32),
+                pltpu.VMEM((n, SUMS, 128), F32),
                 dma(PLANES, 4),
                 dma(PLANES, 4),
                 dma(PLANES, 4),
@@ -1605,21 +1638,16 @@
             ],
             compiler_params=params(4, 48),
         )(part_lin, part_output, sums)
-        sums = jnp.sum(sums[:SUMS], axis=1)
+        sums = jnp.sum(sums, axis=1)
     else:
         grad_w_query, grad_w_key, grad_w_value = (
             over_dp(part_lin[:, width * j : width * (j + 1)], 0).astype(F32) for j in range(3)
         )
         grad_w_output = jnp.transpose(over_dp(part_output, 0)).astype(F32)
         sums = lax.psum(jnp.sum(sums, axis=(1, 2)), ("dp", "tensor"))
-    s_c = sums[0:16].reshape(4, 4)
-    s_e1, s_e2, c_b1, c_b2, b_e = sums[16:20], sums[20:24], sums[24:28], sums[28:32], sums[32]
-    grad_mix_in1 = s_e1
-    grad_mix_res1 = small("ik,jk->ij", s_c, mix_res2) + s_e2[:, None] * mix_in2[None, :]
-    grad_mix_out1 = small("jk,k->j", mix_res2, c_b1) + mix_in2 * b_e
-    grad_mix_in2 = small("ki,k->i", mix_res1, s_e2) + mix_out1 * b_e
-    grad_mix_res2 = small("ki,kj->ij", mix_res1, s_c) + mix_out1[:, None] * c_b1[None, :]
-    grad_mix_out2 = c_b2
+    grad_mix_in1, grad_mix_res1 = sums[0:4], sums[4:20].reshape(4, 4)
+    grad_mix_out1, grad_mix_in2 = sums[20:24], sums[24:28]
+    grad_mix_res2, grad_mix_out2 = sums[28:44].reshape(4, 4), sums[44:48]
     return (
         new_streams,
         stream_grad,

time: 579 us -> 563 us (0.972)
  Pallas kernels: 510 us -> 487 us
  matrix products: 18.4 us -> 39.3 us
    pallas_call x2 -> x1, Pallas kernels: 44.5 us -> 15.5 us  [weight_sum(): pl.pallas_call(pair_kernel, name='pair', cost_estimate=lasts(20), out_sha...]
    dot_general x2 -> x3, matrix products: 14.8 us -> 39.3 us  [contract_rows(): lax.dot_general(left, right, (((0,), (0,)), ((), ())), preferred_element_...]
    pallas_call x1, Pallas kernels: 99.8 us -> 91.4 us  [on_device(): pl.pallas_call(functools.partial(attend_back_kernel, n), name='attend_bac...]
    pallas_call x1, Pallas kernels: 93 us -> 101 us  [on_device(): pl.pallas_call(functools.partial(attend_kernel, n), name='attend', cost_e...]
    pallas_call x1 -> x0, local copies, waits for them, and re-layouts: 6.4 us -> none  [weight_sum(): pl.pallas_call(pair_kernel, name='pair', cost_estimate=lasts(20), out_sha...]
  transfers between devices with their start and end apart: 2 -> 2, of which waited for: 0 -> 0; matrix products, arithmetic and copies ran while one was open for 4% -> 7% of each run, Pallas kernels for 56% -> 51%
where the time goes in v6:
time: 563 us; the launch traced here: 558 us
  Pallas kernels  487 us (87%)
  matrix products  39.3 us (7%)
  between operations  14.4 us (3%)
  local copies, waits for them, and re-layouts  13.1 us (2%)
    pallas_call x1, Pallas kernels, on_device(): pl.pallas_call(functools.partial(attend_kernel, n), name='attend', cost_e...  101 us
    pallas_call x1, Pallas kernels, on_device(): pl.pallas_call(functools.partial(units_back_kernel, n), name='units_back'...  93.9 us
    pallas_call x1, Pallas kernels, on_device(): pl.pallas_call(functools.partial(attend_back_kernel, n), name='attend_bac...  91.4 us
    pallas_call x1, Pallas kernels, on_device(): pl.pallas_call(functools.partial(project_kernel, n), name='project', cost...  83.8 us
    pallas_call x1, Pallas kernels, on_device(): pl.pallas_call(functools.partial(finish_kernel, n), name='finish', cost_e...  77.7 us
    dot_general x3, matrix products, contract_rows(): lax.dot_general(left, right, (((0,), (0,)), ((), ())), preferred_element_...  39.3 us
    pallas_call x1, Pallas kernels, on_device(): pl.pallas_call(streams_kernel, name='streams', cost_estimate=lasts(2), gr...  21.6 us
    pallas_call x1, Pallas kernels, weight_sum(): pl.pallas_call(pair_kernel, name='pair', cost_estimate=lasts(20), out_sha...  15.5 us
  transfers between devices with their start and end apart: 2, of which 0 were waited for; matrix products, arithmetic and copies ran while one was open for 7% of the time, Pallas kernels for 51%

profile of v6, /device:TPU:0, one launch (start us, length us, event | category | flops | bytes accessed | tf_op | source)
XLA Modules:
  0.0 557.7 jit_solution(16357209517183487690)
XLA Ops:
  7.2 0.0 reduce-scatter.3.cloned.1.call-start
  7.2 5.0 copy.34
  12.2 83.8 %project.1 = (bf16[1024,2048]{1,0:T(8,128)(2,1)}, bf16[1024,512]{1,0:T(8,128)(2,1)}, bf16[1024,512]{1,0:T(8,128)(2,1)}, bf16[1024,512]{1,0:T(8,128)(2,1)}, f32[1...) custom-call(f32[4]{0:T(128)} %in1.7, f32[4]{0:T(128)} %out2.7, ...), custom_call_target="tpu_custom_call" | custom-call | flops 99999997952 | bytes 360000000 | tf_op jit(solution)/shard_map/project/pallas_call | solution.py:1383
  96.0 101.1 %attend.1 = (bf16[1024,512]{1,0:T(8,128)(2,1)}, f32[1024,512]{1,0:T(8,128)}, bf16[1024,2048]{1,0:T(8,128)(2,1)}, f32[1024,512]{1,0:T(8,128)}, f32[1024,128]{1,0:...) custom-call(f32[4]{0:T(128)} %in1.7, f32[4]{0:T(128)} %out1.5, ...), custom_call_target="tpu_custom_call" | custom-call | flops 99999997952 | bytes 360000000 | tf_op jit(solution)/shard_map/attend/pallas_call | solution.py:1424
  197.1 15.5 %pair.1._down = bf16[1024,2048]{1,0:T(8,128)(2,1)} custom-call(bf16[1024,2048]{1,0:T(8,128)(2,1)} %get-tuple-element.53.gb2_hbm.left_hbm, bf16[1024,2048]{1,0:T(8,128)(2,1)} %get-tuple-element.63.right_hbm.hidden_hbm), custom_call_target="tpu_custom_call" | custom-call | flops 20000000000 | bytes 72000000 | tf_op jit(solution)/shard_map/pair/pallas_call | solution.py:1477
  212.6 0.0 reduce-scatter.3.cloned.1.call-update
  212.7 0.0 reduce-scatter.5.cloned.1.call-start
  212.7 24.6 %convolution_convert_fusion._gate_up = bf16[2048,4096]{1,0:T(8,128)(2,1)} fusion(bf16[1024,2048]{1,0:T(8,128)(2,1)} %get-tuple-element.60.normed_ref, bf16[1024,4096]{1,0:T(8,128)(2,1)} %get-tuple-element.59.acts_ref), kind=kOutput, calls=%fused_computation | convolution fusion | flops 17188257792 | bytes 29360128 | tf_op jit(solution)/shard_map/dot_general | solution.py:48
  237.3 0.0 reduce-scatter.5.cloned.1.call-update
  237.3 0.0 copy-start.12
  237.4 93.9 %units_back.1 = (f32[1024,512]{1,0:T(8,128)}, bf16[1024,2048]{1,0:T(8,128)(2,1)}) custom-call(f32[4]{0:T(128)} %in1.7, f32[4]{0:T(128)} %out1.5, f32[4]{0:T(128)} %in2.5, f32[4]{0:T(128)} %out2.7, f32[4,4]{1,0:T(4,128)} %res1.5, f32[4,4]{1,0:T(4,128)} %res2.5, bf16[1024,4096]{1,0:T(8,128)(2,1)} %get-tuple-element.59.acts_ref, bf16[2048,2048]{1,0:T(8,128)(2,1)} %wg_ref.1, ...), custom_call_target="tpu_custom_call" | custom-call | flops 399999991808 | bytes 1440000000 | tf_op jit(solution)/shard_map/units_back/pallas_call | solution.py:1520
  331.3 0.0 copy-done.12
  331.3 6.0 %convolution_convert_fusion.2._output.last_hbm = bf16[2048,512]{1,0:T(8,128)(2,1)} fusion(bf16[1024,2048]{1,0:T(8,128)(2,1)} %get-tuple-element.64.gb1_hbm, bf16[1024,512]{1,0:T(8,128)(2,1)S(1)} %copy-done.12), kind=kOutput, calls=%fused_computation.3 | convolution fusion | flops 2148532224 | bytes 7340032 | tf_op jit(solution)/shard_map/dot_general | solution.py:48
  337.3 0.0 reduce-scatter.3.cloned.1.call-done.source_ref
  337.3 0.0 copy-start.9
  337.3 1.3 copy-done.9
  338.5 1.7 turn.1._down
  340.2 0.0 copy-start.1
  340.2 0.0 copy-start.6
  340.2 0.0 copy-start.7
  340.2 0.0 copy-start.8
  340.2 91.4 %attend_back.1 = (bf16[1024,1536]{1,0:T(8,128)(2,1)}, f32[1024,512]{1,0:T(8,128)}, f32[1024,512]{1,0:T(8,128)}) custom-call(bf16[1024,512]{1,0:T(8,128)(2,1)} %get-tuple-element.48.q_ref, bf16[1024,512]{1,0:T(8,128)(2,1)} %get-tuple-element.49.k_ref, bf16[1024,512]{1,0:T(8,128)(2,1)} %get-tuple-element.50.v_ref, f32[1024,128]{1,0:T(8,128)} %get-tuple-element.51.segc_ref, ...), custom_call_target="tpu_custom_call" | custom-call | flops 2000000000 | bytes 7200000 | tf_op jit(solution)/shard_map/attend_back/pallas_call | solution.py:1551
  431.6 0.0 copy-done.1
  431.6 0.0 copy-done.3
  431.6 0.0 copy-done.4
  431.6 0.0 copy-done.5
  431.6 0.0 copy-done.6
  431.6 0.0 copy-done.7
  431.7 0.0 copy-done.8
  431.7 0.0 copy-start.2
  431.7 1.6 copy-done.2
  433.3 21.6 %streams.1 = (bf16[1024,4,512]{2,1,0:T(4,128)(2,1)}, f32[1024,4,512]{2,1,0:T(4,128)}, f32[48,8,128]{2,1,0:T(8,128)S(1)}) custom-call(f32[4]{0:T(128)S(1)} %copy-done.5, f32[4]{0:T(128)S(1)} %copy-done.6, f32[4]{0:T(128)S(1)} %copy-done.7, f32[4]{0:T(128)S(1)} %copy-done.8, f32[4,4]{1,0:T(4,128)S(1)} %copy-done.3, f32[4,4]{1,0:T(4,128)S(1)} %copy-done.4, ...), custom_call_target="tpu_custom_call" | custom-call | flops 2000000000 | bytes 7200000 | tf_op jit(solution)/shard_map/streams/pallas_call | solution.py:1592
  454.9 0.0 copy-done.10
  454.9 0.0 copy-done.11
  454.9 0.0 copy-start
  454.9 8.7 %convolution_convert_fusion.1.first_hbm = bf16[2048,1536]{1,0:T(8,128)(2,1)} fusion(bf16[1024,2048]{1,0:T(8,128)(2,1)S(1)} %copy-done.10, bf16[1024,1536]{1,0:T(8,128)(2,1)S(1)} %copy-done.11), kind=kOutput, calls=%fused_computation.1 | convolution fusion | flops 6445596672 | bytes 13631488 | tf_op jit(solution)/shard_map/dot_general | solution.py:48
  463.6 0.0 copy-done
  463.6 77.7 %finish.1 = (f32[256,512]{1,0:T(8,128)S(1)}, f32[256,512]{1,0:T(8,128)S(1)}, f32[256,512]{1,0:T(8,128)S(1)}, f32[512,256]{1,0:T(8,128)S(1)}, f32[48,128]{1,0:T(8,128)S(1)}) custom-call(bf16[2048,1536]{1,0:T(8,128)(2,1)} %convolution_convert_fusion.1.first_hbm, bf16[2048,512]{1,0:T(8,128)(2,1)S(1)} %copy-done, f32[48,8,128]{2,1,0:T(8,128)S(1)} %get-tuple-element.73.sums_ref), custom_call_target="tpu_custom_call" | custom-call | flops 2000000000 | bytes 7200000 | tf_op jit(solution)/shard_map/finish/pallas_call | solution.py:1613
  541.3 0.1 reduce_sum.9
  541.4 0.1 fusion.1
  541.5 0.7 reshape.60
  542.1 0.7 reshape.61
  542.8 0.6 fusion
  543.4 4.1 slice_convert_fusion
  547.5 0.8 copy.39
  548.3 0.8 copy.40
  549.1 0.8 copy.41
  549.8 0.8 copy.42
  (6 shorter events, 0.0 us)
Async XLA Ops:
  7.2 330.1 %reduce-scatter.3.cloned.1.call-start = ((), (), s32[]{:S(2)}) async-start(), calls=%async_computation.2 | async-start | bytes 5242880 | tf_op jit(solution)/shard_map/reduce_scatter | solution.py:1500
  212.7 330.7 %reduce-scatter.5.cloned.1.call-start = ((), (), s32[]{:S(2)}) async-start(), calls=%async_computation.3 | async-start | bytes 18874368 | tf_op jit(solution)/shard_map/reduce_scatter | solution.py:1466
  237.3 93.9 %copy-start.12 = (bf16[1024,512]{1,0:T(8,128)(2,1)S(1)}, bf16[1024,512]{1,0:T(8,128)(2,1)}, u32[]{:S(2)}) copy-start(bf16[1024,512]{1,0:T(8,128)(2,1)} %get-tuple-element.66) | copy-start | bytes 3145732
  337.3 1.3 copy-start.9
  340.2 91.4 %copy-start.1 = (f32[1024,512]{1,0:T(8,128)S(1)}, f32[1024,512]{1,0:T(8,128)}, u32[]{:S(2)}) copy-start(f32[1024,512]{1,0:T(8,128)} %get-tuple-element.54.b1_ref) | copy-start | bytes 6291460
  340.2 91.4 %copy-start.3 = (f32[4,4]{1,0:T(4,128)S(1)}, f32[4,4]{1,0:T(4,128)}, u32[]{:S(2)}) copy-start(f32[4,4]{1,0:T(4,128)} %res1.5) | copy-start | bytes 196
  340.2 91.4 %copy-start.4 = (f32[4,4]{1,0:T(4,128)S(1)}, f32[4,4]{1,0:T(4,128)}, u32[]{:S(2)}) copy-start(f32[4,4]{1,0:T(4,128)} %res2.5) | copy-start | bytes 196
  340.2 91.5 %copy-start.5 = (f32[4]{0:T(128)S(1)}, f32[4]{0:T(128)}, u32[]{:S(2)}) copy-start(f32[4]{0:T(128)} %in1.7) | copy-start | bytes 52
  340.2 91.5 %copy-start.6 = (f32[4]{0:T(128)S(1)}, f32[4]{0:T(128)}, u32[]{:S(2)}) copy-start(f32[4]{0:T(128)} %out1.5) | copy-start | bytes 52
  340.2 91.5 %copy-start.7 = (f32[4]{0:T(128)S(1)}, f32[4]{0:T(128)}, u32[]{:S(2)}) copy-start(f32[4]{0:T(128)} %in2.5) | copy-start | bytes 52
  340.2 91.5 %copy-start.8 = (f32[4]{0:T(128)S(1)}, f32[4]{0:T(128)}, u32[]{:S(2)}) copy-start(f32[4]{0:T(128)} %out2.7) | copy-start | bytes 52
  431.7 1.6 copy-start.2
  433.3 21.6 %copy-start.10 = (bf16[1024,2048]{1,0:T(8,128)(2,1)S(1)}, bf16[1024,2048]{1,0:T(8,128)(2,1)}, u32[]{:S(2)}) copy-start(bf16[1024,2048]{1,0:T(8,128)(2,1)} %get-tuple-element.65.normed_hbm) | copy-start | bytes 12582916
  433.3 21.6 %copy-start.11 = (bf16[1024,1536]{1,0:T(8,128)(2,1)S(1)}, bf16[1024,1536]{1,0:T(8,128)(2,1)}, u32[]{:S(2)}) copy-start(bf16[1024,1536]{1,0:T(8,128)(2,1)} %get-tuple-element.72) | copy-start | bytes 9437188
  454.9 8.7 %copy-start = (bf16[2048,512]{1,0:T(8,128)(2,1)S(1)}, bf16[2048,512]{1,0:T(8,128)(2,1)}, u32[]{:S(2)}) copy-start(bf16[2048,512]{1,0:T(8,128)(2,1)} %convolution_convert_fusion.2._output.last_hbm) | copy-start | bytes 6291460
Sparse Core Ops, SparseCore 0:
  212.8 77.5 reduce-scatter.2
  292.9 168.7 reduce-scatter.4

commit v7 on v6

--- a/solution.py
+++ b/solution.py
@@ -739,16 +739,39 @@
 
 
 def units_back_kernel(
-    n, in1, out1, in2, out2, res1, res2, acts_ref, wg_ref, wu_ref, normed_ref, stand_ref, scale_ref, c_hbm, _down, _gate_up,
+    n, in1, out1, in2, out2, res1, res2, scale_ref, acts_hbm, wg_hbm, wu_hbm, normed_hbm, stand_hbm, c_hbm, _down, _gate_up,
     entry_ref, gb1_hbm,
-    c_buf, part32, first, second, part, came, mine, others, all1, in_sem, out_sem,
+    acts_ref, wg_ref, wu_ref, normed_ref, stand_ref, c_buf, part32, first, second, part, came, mine, others, all1, acts_sem, in_sem, out_sem,
     send1, recv1, send2, recv2, send3, recv3,
 ):
     tokens, features = normed_ref.shape
     width = entry_ref.shape[1]
     count = tokens // CHUNK
     mixing = Mixing((in1, out1, in2, out2, res1, res2))
-    c_in = pltpu.make_async_copy(c_hbm, c_buf, in_sem)
+
+    def acts_in(c):
+        return pltpu.make_async_copy(
+            acts_hbm.at[chunk_rows(c)], acts_ref.at[chunk_rows(c)], acts_sem.at[c]
+        )
+
+    wg_in, wu_in, normed_in, stand_in, c_in = (
+        pltpu.make_async_copy(source, target, in_sem.at[i])
+        for i, (source, target) in enumerate(
+            (
+                (wg_hbm, wg_ref),
+                (wu_hbm, wu_ref),
+                (normed_hbm, normed_ref),
+                (stand_hbm, stand_ref),
+                (c_hbm, c_buf),
+            )
+        )
+    )
+    acts_in(0).start()
+    wg_in.start()
+    wu_in.start()
+    normed_in.start()
+    loop(count - 1, lambda c: acts_in(c + 1).start())
+    stand_in.start()
     c_in.start()
     scatter = Scatter(n, part, came, width, send1, recv1)
     stats = Stats(n, mine, others, send2, recv2)
@@ -758,7 +781,19 @@
     def work(c):
         rows = chunk_rows(c)
         units = wg_ref.shape[1]
+        acts_in(c).wait()
+
+        @pl.when(c == 0)
+        def _():
+            wg_in.wait()
+
         part32[...] = dot_nt(acts_ref[rows, 0:units], wg_ref[...])
+
+        @pl.when(c == 0)
+        def _():
+            wu_in.wait()
+            normed_in.wait()
+
         part32[...] += dot_nt(acts_ref[rows, units : 2 * units], wu_ref[...])
         stats_part(part32, normed_ref, lambda r: sub_rows(c, r), part, c, first, second)
         stats.put(c, first[...], second[...])
@@ -792,10 +827,13 @@
         loop(CHUNK // ROWS, piece)
         gather.start(c)
 
-    c_in.wait()
-
     def ahead(c):
         work(c)
+
+        @pl.when(c == 1)
+        def _():
+            stand_in.wait()
+            c_in.wait()
 
         @pl.when(c >= 2)
         def _():
@@ -830,11 +868,11 @@
 
 
 def attend_back_kernel(
-    n, q_ref, k_ref, v_ref, segc_ref, segr_ref, cos_ref, sin_ref, wo_ref, wq_ref, wk_ref, wv_ref,
-    wd_ref, stand_ref, scale_ref, gb1_hbm, hidden_hbm, normed_hbm, _output, _down,
+    n, q_ref, k_ref, v_ref, segc_ref, segr_ref, cos_ref, sin_ref, scale_ref,
+    wo_hbm, wq_hbm, wk_hbm, wv_hbm, wd_hbm, stand_hbm, gb1_hbm, hidden_hbm, normed_hbm, _output, _down,
     lin_ref, branch_ref, entry_ref,
-    gb1_buf, hidden_buf, normed_buf, bias, dk_t, dv_t, part32, first, second,
-    part1, came1, part2, came2, mine, others, in_sem,
+    wo_ref, wq_ref, wk_ref, wv_ref, wd_ref, stand_ref, gb1_buf, hidden_buf, normed_buf, bias, dk_t, dv_t, part32, first, second,
+    part1, came1, part2, came2, mine, others, in_sem, w_sem,
     send1, recv1, send2, recv2, send3, recv3,
 ):
     tokens, width = q_ref.shape
@@ -854,7 +892,22 @@
             )
         )
 
+    wd_in, wo_in, wq_in, wk_in, wv_in, stand_in = (
+        pltpu.make_async_copy(source, target, w_sem.at[i])
+        for i, (source, target) in enumerate(
+            (
+                (wd_hbm, wd_ref),
+                (wo_hbm, wo_ref),
+                (wq_hbm, wq_ref),
+                (wk_hbm, wk_ref),
+                (wv_hbm, wv_ref),
+                (stand_hbm, stand_ref),
+            )
+        )
+    )
     for copy in inputs(count - 1, 0):
+        copy.start()
+    for copy in (wd_in, wo_in, wq_in, wk_in, wv_in, stand_in):
         copy.start()
     dk_t[...] = jnp.zeros_like(dk_t)
     dv_t[...] = jnp.zeros_like(dv_t)
@@ -872,8 +925,19 @@
         for copy in inputs(c, slot):
             copy.wait()
         rows = chunk_rows(c)
+
+        @pl.when(i == 0)
+        def _():
+            wd_in.wait()
+
         part2[rows, :] = dot_nn(hidden_buf[slot], wd_ref[...]).astype(BF16)
         down.start(c)
+
+        @pl.when(i == 0)
+        def _():
+            for copy in (wo_in, wq_in, wk_in, wv_in):
+                copy.wait()
+
         grad = dot_nt(gb1_buf[slot], wo_ref[...]).astype(BF16)
         start, extent = window(c, tokens)
         keys = pl.ds(start, extent)
@@ -919,6 +983,7 @@
 
     loop(count, work)
     scatter.relay(0)
+    stand_in.wait()
 
     def last(i):
         c = count - 1 - i
@@ -1522,9 +1587,14 @@
         name="units_back",
         cost_estimate=lasts(400),
         out_shape=[array((tokens, width), F32), array((tokens, features), BF16)],
-        in_specs=[smem] * 6 + [vmem] * 6 + [any_spec] * 3,
+        in_specs=[smem] * 6 + [vmem] + [any_spec] * 8,
         out_specs=[vmem, any_spec],
         scratch_shapes=[
+            pltpu.VMEM((tokens, 2 * units), BF16),
+            pltpu.VMEM((features, units), BF16),
+            pltpu.VMEM((features, units), BF16),
+            pltpu.VMEM((tokens, features), BF16),
+            pltpu.VMEM((tokens, width), F32),
             pltpu.VMEM((stream_count, tokens, width), BF16),
             pltpu.VMEM((CHUNK, features), F32),
             pltpu.VMEM((CHUNK, 128), F32),
@@ -1534,7 +1604,8 @@
             pltpu.VMEM((chunks, 16, CHUNK), F32),
             pltpu.VMEM((n - 1, chunks, 16, CHUNK), F32),
             pltpu.VMEM((tokens, features), BF16),
-            pltpu.SemaphoreType.DMA,
+            dma(chunks),
+            dma(5),
             dma(chunks),
         ]
         + scatter_sems
@@ -1542,7 +1613,7 @@
         + gather_sems,
         compiler_params=params(2, 60),
     )(
-        *mixes, grad_acts, w_gate, w_up, normed2, stand2, scale2, cot_planes,
+        *mixes, scale2, grad_acts, w_gate, w_up, normed2, stand2, cot_planes,
         part_down, part_gate_up,
     )
 
@@ -1553,9 +1624,15 @@
         name="attend_back",
         cost_estimate=lasts(2),
         out_shape=[array((tokens, 3 * width), BF16)] + [array((tokens, width), F32)] * 2,
-        in_specs=[vmem] * 14 + [any_spec] * 5,
+        in_specs=[vmem] * 8 + [any_spec] * 11,
         out_specs=[vmem] * 3,
         scratch_shapes=[
+            pltpu.VMEM((width, features), BF16),
+            pltpu.VMEM((features, width), BF16),
+            pltpu.VMEM((features, width), BF16),
+            pltpu.VMEM((features, width), BF16),
+            pltpu.VMEM((units, features), BF16),
+            pltpu.VMEM((tokens, width), F32),
             pltpu.VMEM((2, CHUNK, features), BF16),
             pltpu.VMEM((2, CHUNK, units), BF16),
             pltpu.VMEM((2, CHUNK, features), BF16),
@@ -1572,14 +1649,15 @@
             pltpu.VMEM((chunks, 16, CHUNK), F32),
             pltpu.VMEM((n - 1, chunks, 16, CHUNK), F32),
             dma(3, 2),
+            dma(6),
         ]
         + scatter_sems
         + scatter_sems
         + stats_sems,
         compiler_params=params(3, 60),
     )(
-        queries, keys, values, seg_column, seg_row, cos_table, sin_table,
-        w_output, w_query, w_key, w_value, w_down, stand1, scale1,
+        queries, keys, values, seg_column, seg_row, cos_table, sin_table, scale1,
+        w_output, w_query, w_key, w_value, w_down, stand1,
         grad_branch1, hidden, normed1, part_output, grad_w_down,
     )
 

time: 563 us -> 557 us (0.989)
  Pallas kernels: 487 us -> 481 us
where the time goes in v7:
time: 557 us; the launch traced here: 552 us
  Pallas kernels  481 us (86%)
  matrix products  39.2 us (7%)
  between operations  14.4 us (3%)
  local copies, waits for them, and re-layouts  13.1 us (2%)
    pallas_call x1, Pallas kernels, on_device(): pl.pallas_call(functools.partial(attend_kernel, n), name='attend', cost_e...  101 us
    pallas_call x1, Pallas kernels, on_device(): pl.pallas_call(functools.partial(attend_back_kernel, n), name='attend_bac...  90.8 us
    pallas_call x1, Pallas kernels, on_device(): pl.pallas_call(functools.partial(units_back_kernel, n), name='units_back'...  88.9 us
    pallas_call x1, Pallas kernels, on_device(): pl.pallas_call(functools.partial(project_kernel, n), name='project', cost...  83.8 us
    pallas_call x1, Pallas kernels, on_device(): pl.pallas_call(functools.partial(finish_kernel, n), name='finish', cost_e...  77.7 us
    dot_general x3, matrix products, contract_rows(): lax.dot_general(left, right, (((0,), (0,)), ((), ())), preferred_element_...  39.2 us
    pallas_call x1, Pallas kernels, on_device(): pl.pallas_call(streams_kernel, name='streams', cost_estimate=lasts(2), gr...  21.6 us
    pallas_call x1, Pallas kernels, weight_sum(): pl.pallas_call(pair_kernel, name='pair', cost_estimate=lasts(20), out_sha...  15.5 us
  transfers between devices with their start and end apart: 2, of which 0 were waited for; matrix products, arithmetic and copies ran while one was open for 7% of the time, Pallas kernels for 51%

profile of v7, /device:TPU:0, one launch (start us, length us, event | category | flops | bytes accessed | tf_op | source)
XLA Modules:
  0.0 552.1 jit_solution(9586356994458518445)
XLA Ops:
  7.2 0.0 reduce-scatter.3.cloned.1.call-start
  7.2 5.0 copy.34
  12.2 83.8 %project.1 = (bf16[1024,2048]{1,0:T(8,128)(2,1)}, bf16[1024,512]{1,0:T(8,128)(2,1)}, bf16[1024,512]{1,0:T(8,128)(2,1)}, bf16[1024,512]{1,0:T(8,128)(2,1)}, f32[1...) custom-call(f32[4]{0:T(128)} %in1.7, f32[4]{0:T(128)} %out2.7, ...), custom_call_target="tpu_custom_call" | custom-call | flops 99999997952 | bytes 360000000 | tf_op jit(solution)/shard_map/project/pallas_call | solution.py:1448
  96.0 101.1 %attend.1 = (bf16[1024,512]{1,0:T(8,128)(2,1)}, f32[1024,512]{1,0:T(8,128)}, bf16[1024,2048]{1,0:T(8,128)(2,1)}, f32[1024,512]{1,0:T(8,128)}, f32[1024,128]{1,0:...) custom-call(f32[4]{0:T(128)} %in1.7, f32[4]{0:T(128)} %out1.5, ...), custom_call_target="tpu_custom_call" | custom-call | flops 99999997952 | bytes 360000000 | tf_op jit(solution)/shard_map/attend/pallas_call | solution.py:1489
  197.1 15.5 %pair.1._down = bf16[1024,2048]{1,0:T(8,128)(2,1)} custom-call(bf16[1024,2048]{1,0:T(8,128)(2,1)} %get-tuple-element.53.gb2_hbm.left_hbm, bf16[1024,2048]{1,0:T(8,128)(2,1)} %get-tuple-element.63.right_hbm.hidden_hbm), custom_call_target="tpu_custom_call" | custom-call | flops 20000000000 | bytes 72000000 | tf_op jit(solution)/shard_map/pair/pallas_call | solution.py:1542
  212.6 0.0 reduce-scatter.3.cloned.1.call-update
  212.7 0.0 reduce-scatter.5.cloned.1.call-start
  212.7 24.6 %convolution_convert_fusion._gate_up = bf16[2048,4096]{1,0:T(8,128)(2,1)} fusion(bf16[1024,2048]{1,0:T(8,128)(2,1)} %get-tuple-element.61.normed_hbm, bf16[1024,4096]{1,0:T(8,128)(2,1)} %get-tuple-element.60.acts_hbm), kind=kOutput, calls=%fused_computation | convolution fusion | flops 17188257792 | bytes 29360128 | tf_op jit(solution)/shard_map/dot_general | solution.py:48
  237.3 0.0 reduce-scatter.5.cloned.1.call-update
  237.3 0.0 copy-start.12
  237.4 88.9 %units_back.1 = (f32[1024,512]{1,0:T(8,128)}, bf16[1024,2048]{1,0:T(8,128)(2,1)}) custom-call(f32[4]{0:T(128)} %in1.7, f32[4]{0:T(128)} %out1.5, f32[4]{0:T(128)} %in2.5, f32[4]{0:T(128)} %out2.7, f32[4,4]{1,0:T(4,128)} %res1.5, f32[4,4]{1,0:T(4,128)} %res2.5, f32[1024,128]{1,0:T(8,128)} %get-tuple-element.59.scale_ref, ...), custom_call_target="tpu_custom_call" | custom-call | flops 399999991808 | bytes 1440000000 | tf_op jit(solution)/shard_map/units_back/pallas_call | solution.py:1585
  326.3 0.0 copy-done.12
  326.3 5.9 %convolution_convert_fusion.2._output.last_hbm = bf16[2048,512]{1,0:T(8,128)(2,1)} fusion(bf16[1024,2048]{1,0:T(8,128)(2,1)} %get-tuple-element.64.gb1_hbm, bf16[1024,512]{1,0:T(8,128)(2,1)S(1)} %copy-done.12), kind=kOutput, calls=%fused_computation.3 | convolution fusion | flops 2148532224 | bytes 7340032 | tf_op jit(solution)/shard_map/dot_general | solution.py:48
  332.2 0.0 reduce-scatter.3.cloned.1.call-done.source_ref
  332.3 0.0 copy-start.9
  332.3 1.2 copy-done.9
  333.5 1.7 turn.1._down
  335.2 0.0 copy-start.1
  335.2 0.0 copy-start.6
  335.2 0.0 copy-start.7
  335.2 0.0 copy-start.8
  335.2 90.8 %attend_back.1 = (bf16[1024,1536]{1,0:T(8,128)(2,1)}, f32[1024,512]{1,0:T(8,128)}, f32[1024,512]{1,0:T(8,128)}) custom-call(bf16[1024,512]{1,0:T(8,128)(2,1)} %get-tuple-element.48.q_ref, bf16[1024,512]{1,0:T(8,128)(2,1)} %get-tuple-element.49.k_ref, bf16[1024,512]{1,0:T(8,128)(2,1)} %get-tuple-element.50.v_ref, f32[1024,128]{1,0:T(8,128)} %get-tuple-element.51.segc_ref, ...), custom_call_target="tpu_custom_call" | custom-call | flops 2000000000 | bytes 7200000 | tf_op jit(solution)/shard_map/attend_back/pallas_call | solution.py:1622
  426.0 0.0 copy-done.1
  426.0 0.0 copy-done.3
  426.0 0.0 copy-done.4
  426.0 0.0 copy-done.5
  426.0 0.0 copy-done.6
  426.0 0.0 copy-done.7
  426.0 0.0 copy-done.8
  426.1 0.0 copy-start.2
  426.1 1.6 copy-done.2
  427.7 21.6 %streams.1 = (bf16[1024,4,512]{2,1,0:T(4,128)(2,1)}, f32[1024,4,512]{2,1,0:T(4,128)}, f32[48,8,128]{2,1,0:T(8,128)S(1)}) custom-call(f32[4]{0:T(128)S(1)} %copy-done.5, f32[4]{0:T(128)S(1)} %copy-done.6, f32[4]{0:T(128)S(1)} %copy-done.7, f32[4]{0:T(128)S(1)} %copy-done.8, f32[4,4]{1,0:T(4,128)S(1)} %copy-done.3, f32[4,4]{1,0:T(4,128)S(1)} %copy-done.4, ...), custom_call_target="tpu_custom_call" | custom-call | flops 2000000000 | bytes 7200000 | tf_op jit(solution)/shard_map/streams/pallas_call | solution.py:1670
  449.3 0.0 copy-done.10
  449.3 0.0 copy-done.11
  449.3 0.0 copy-start
  449.3 8.7 %convolution_convert_fusion.1.first_hbm = bf16[2048,1536]{1,0:T(8,128)(2,1)} fusion(bf16[1024,2048]{1,0:T(8,128)(2,1)S(1)} %copy-done.10, bf16[1024,1536]{1,0:T(8,128)(2,1)S(1)} %copy-done.11), kind=kOutput, calls=%fused_computation.1 | convolution fusion | flops 6445596672 | bytes 13631488 | tf_op jit(solution)/shard_map/dot_general | solution.py:48
  458.0 0.0 copy-done
  458.0 77.7 %finish.1 = (f32[256,512]{1,0:T(8,128)S(1)}, f32[256,512]{1,0:T(8,128)S(1)}, f32[256,512]{1,0:T(8,128)S(1)}, f32[512,256]{1,0:T(8,128)S(1)}, f32[48,128]{1,0:T(8,128)S(1)}) custom-call(bf16[2048,1536]{1,0:T(8,128)(2,1)} %convolution_convert_fusion.1.first_hbm, bf16[2048,512]{1,0:T(8,128)(2,1)S(1)} %copy-done, f32[48,8,128]{2,1,0:T(8,128)S(1)} %get-tuple-element.73.sums_ref), custom_call_target="tpu_custom_call" | custom-call | flops 2000000000 | bytes 7200000 | tf_op jit(solution)/shard_map/finish/pallas_call | solution.py:1691
  535.8 0.1 reduce_sum.9
  535.9 0.1 fusion.1
  535.9 0.7 reshape.60
  536.6 0.7 reshape.61
  537.3 0.6 fusion
  537.9 4.1 slice_convert_fusion
  541.9 0.8 copy.39
  542.7 0.8 copy.40
  543.5 0.8 copy.41
  544.3 0.8 copy.42
  (6 shorter events, 0.0 us)
Async XLA Ops:
  7.2 325.1 %reduce-scatter.3.cloned.1.call-start = ((), (), s32[]{:S(2)}) async-start(), calls=%async_computation.2 | async-start | bytes 5242880 | tf_op jit(solution)/shard_map/reduce_scatter | solution.py:1565
  212.7 325.2 %reduce-scatter.5.cloned.1.call-start = ((), (), s32[]{:S(2)}) async-start(), calls=%async_computation.3 | async-start | bytes 18874368 | tf_op jit(solution)/shard_map/reduce_scatter | solution.py:1531
  237.3 88.9 %copy-start.12 = (bf16[1024,512]{1,0:T(8,128)(2,1)S(1)}, bf16[1024,512]{1,0:T(8,128)(2,1)}, u32[]{:S(2)}) copy-start(bf16[1024,512]{1,0:T(8,128)(2,1)} %get-tuple-element.66) | copy-start | bytes 3145732
  332.3 1.3 copy-start.9
  335.2 90.8 %copy-start.1 = (f32[1024,512]{1,0:T(8,128)S(1)}, f32[1024,512]{1,0:T(8,128)}, u32[]{:S(2)}) copy-start(f32[1024,512]{1,0:T(8,128)} %get-tuple-element.54.b1_ref) | copy-start | bytes 6291460
  335.2 90.8 %copy-start.3 = (f32[4,4]{1,0:T(4,128)S(1)}, f32[4,4]{1,0:T(4,128)}, u32[]{:S(2)}) copy-start(f32[4,4]{1,0:T(4,128)} %res1.5) | copy-start | bytes 196
  335.2 90.8 %copy-start.4 = (f32[4,4]{1,0:T(4,128)S(1)}, f32[4,4]{1,0:T(4,128)}, u32[]{:S(2)}) copy-start(f32[4,4]{1,0:T(4,128)} %res2.5) | copy-start | bytes 196
  335.2 90.8 %copy-start.5 = (f32[4]{0:T(128)S(1)}, f32[4]{0:T(128)}, u32[]{:S(2)}) copy-start(f32[4]{0:T(128)} %in1.7) | copy-start | bytes 52
  335.2 90.9 %copy-start.6 = (f32[4]{0:T(128)S(1)}, f32[4]{0:T(128)}, u32[]{:S(2)}) copy-start(f32[4]{0:T(128)} %out1.5) | copy-start | bytes 52
  335.2 90.9 %copy-start.7 = (f32[4]{0:T(128)S(1)}, f32[4]{0:T(128)}, u32[]{:S(2)}) copy-start(f32[4]{0:T(128)} %in2.5) | copy-start | bytes 52
  335.2 90.8 %copy-start.8 = (f32[4]{0:T(128)S(1)}, f32[4]{0:T(128)}, u32[]{:S(2)}) copy-start(f32[4]{0:T(128)} %out2.7) | copy-start | bytes 52
  426.1 1.6 copy-start.2
  427.6 21.6 %copy-start.10 = (bf16[1024,2048]{1,0:T(8,128)(2,1)S(1)}, bf16[1024,2048]{1,0:T(8,128)(2,1)}, u32[]{:S(2)}) copy-start(bf16[1024,2048]{1,0:T(8,128)(2,1)} %get-tuple-element.65.normed_hbm) | copy-start | bytes 12582916
  427.6 21.6 %copy-start.11 = (bf16[1024,1536]{1,0:T(8,128)(2,1)S(1)}, bf16[1024,1536]{1,0:T(8,128)(2,1)}, u32[]{:S(2)}) copy-start(bf16[1024,1536]{1,0:T(8,128)(2,1)} %get-tuple-element.72) | copy-start | bytes 9437188
  449.3 8.7 %copy-start = (bf16[2048,512]{1,0:T(8,128)(2,1)S(1)}, bf16[2048,512]{1,0:T(8,128)(2,1)}, u32[]{:S(2)}) copy-start(bf16[2048,512]{1,0:T(8,128)(2,1)} %convolution_convert_fusion.2._output.last_hbm) | copy-start | bytes 6291460
Sparse Core Ops, SparseCore 0:
  212.8 77.5 reduce-scatter.2
  292.9 168.7 reduce-scatter.4

commit v8 on v7

--- a/solution.py
+++ b/solution.py
@@ -1042,7 +1042,7 @@
         return total
 
     def piece(r):
-        rows = pl.ds(pl.multiple_of(r * 16, 16), 16)
+        rows = local_rows(r)
         s = [s_ref[i, rows].astype(F32) for i in range(count)]
         c = [c_ref[i, rows].astype(F32) for i in range(count)]
         b1, b2, e1, e2 = b1_ref[rows, :], b2_ref[rows, :], e1_ref[rows, :], e2_ref[rows, :]
@@ -1061,7 +1061,7 @@
         for place, (left, right) in enumerate(pairs):
             sums_ref[place] += fold(left * right)
 
-    loop(s_ref.shape[1] // 16, piece)
+    loop(s_ref.shape[1] // ROWS, piece)
 
     @pl.when(pl.program_id(0) == pl.num_programs(0) - 1)
     def _():

time: 557 us -> 557 us (level)
  no operation moved by 1% of the time
where the time goes in v8:
time: 557 us; the launch traced here: 552 us
  Pallas kernels  481 us (86%)
  matrix products  39.2 us (7%)
  between operations  14.4 us (3%)
  local copies, waits for them, and re-layouts  13.1 us (2%)
    pallas_call x1, Pallas kernels, on_device(): pl.pallas_call(functools.partial(attend_kernel, n), name='attend', cost_e...  101 us
    pallas_call x1, Pallas kernels, on_device(): pl.pallas_call(functools.partial(attend_back_kernel, n), name='attend_bac...  90.8 us
    pallas_call x1, Pallas kernels, on_device(): pl.pallas_call(functools.partial(units_back_kernel, n), name='units_back'...  88.9 us
    pallas_call x1, Pallas kernels, on_device(): pl.pallas_call(functools.partial(project_kernel, n), name='project', cost...  83.8 us
    pallas_call x1, Pallas kernels, on_device(): pl.pallas_call(functools.partial(finish_kernel, n), name='finish', cost_e...  77.7 us
    dot_general x3, matrix products, contract_rows(): lax.dot_general(left, right, (((0,), (0,)), ((), ())), preferred_element_...  39.2 us
    pallas_call x1, Pallas kernels, on_device(): pl.pallas_call(streams_kernel, name='streams', cost_estimate=lasts(2), gr...  21.1 us
    pallas_call x1, Pallas kernels, weight_sum(): pl.pallas_call(pair_kernel, name='pair', cost_estimate=lasts(20), out_sha...  15.5 us
  transfers between devices with their start and end apart: 2, of which 0 were waited for; matrix products, arithmetic and copies ran while one was open for 7% of the time, Pallas kernels for 51%

profile of v8, /device:TPU:0, one launch (start us, length us, event | category | flops | bytes accessed | tf_op | source)
XLA Modules:
  0.0 551.6 jit_solution(1301227141406194162)
XLA Ops:
  7.2 0.0 reduce-scatter.3.cloned.1.call-start
  7.2 5.0 copy.34
  12.2 83.8 %project.1 = (bf16[1024,2048]{1,0:T(8,128)(2,1)}, bf16[1024,512]{1,0:T(8,128)(2,1)}, bf16[1024,512]{1,0:T(8,128)(2,1)}, bf16[1024,512]{1,0:T(8,128)(2,1)}, f32[1...) custom-call(f32[4]{0:T(128)} %in1.7, f32[4]{0:T(128)} %out2.7, ...), custom_call_target="tpu_custom_call" | custom-call | flops 99999997952 | bytes 360000000 | tf_op jit(solution)/shard_map/project/pallas_call | solution.py:1448
  96.0 101.1 %attend.1 = (bf16[1024,512]{1,0:T(8,128)(2,1)}, f32[1024,512]{1,0:T(8,128)}, bf16[1024,2048]{1,0:T(8,128)(2,1)}, f32[1024,512]{1,0:T(8,128)}, f32[1024,128]{1,0:...) custom-call(f32[4]{0:T(128)} %in1.7, f32[4]{0:T(128)} %out1.5, ...), custom_call_target="tpu_custom_call" | custom-call | flops 99999997952 | bytes 360000000 | tf_op jit(solution)/shard_map/attend/pallas_call | solution.py:1489
  197.1 15.5 %pair.1._down = bf16[1024,2048]{1,0:T(8,128)(2,1)} custom-call(bf16[1024,2048]{1,0:T(8,128)(2,1)} %get-tuple-element.53.gb2_hbm.left_hbm, bf16[1024,2048]{1,0:T(8,128)(2,1)} %get-tuple-element.63.right_hbm.hidden_hbm), custom_call_target="tpu_custom_call" | custom-call | flops 20000000000 | bytes 72000000 | tf_op jit(solution)/shard_map/pair/pallas_call | solution.py:1542
  212.6 0.0 reduce-scatter.3.cloned.1.call-update
  212.7 0.0 reduce-scatter.5.cloned.1.call-start
  212.7 24.6 %convolution_convert_fusion._gate_up = bf16[2048,4096]{1,0:T(8,128)(2,1)} fusion(bf16[1024,2048]{1,0:T(8,128)(2,1)} %get-tuple-element.61.normed_hbm, bf16[1024,4096]{1,0:T(8,128)(2,1)} %get-tuple-element.60.acts_hbm), kind=kOutput, calls=%fused_computation | convolution fusion | flops 17188257792 | bytes 29360128 | tf_op jit(solution)/shard_map/dot_general | solution.py:48
  237.3 0.0 reduce-scatter.5.cloned.1.call-update
  237.3 0.0 copy-start.12
  237.4 88.9 %units_back.1 = (f32[1024,512]{1,0:T(8,128)}, bf16[1024,2048]{1,0:T(8,128)(2,1)}) custom-call(f32[4]{0:T(128)} %in1.7, f32[4]{0:T(128)} %out1.5, f32[4]{0:T(128)} %in2.5, f32[4]{0:T(128)} %out2.7, f32[4,4]{1,0:T(4,128)} %res1.5, f32[4,4]{1,0:T(4,128)} %res2.5, f32[1024,128]{1,0:T(8,128)} %get-tuple-element.59.scale_ref, ...), custom_call_target="tpu_custom_call" | custom-call | flops 399999991808 | bytes 1440000000 | tf_op jit(solution)/shard_map/units_back/pallas_call | solution.py:1585
  326.3 0.0 copy-done.12
  326.3 5.9 %convolution_convert_fusion.2._output.last_hbm = bf16[2048,512]{1,0:T(8,128)(2,1)} fusion(bf16[1024,2048]{1,0:T(8,128)(2,1)} %get-tuple-element.64.gb1_hbm, bf16[1024,512]{1,0:T(8,128)(2,1)S(1)} %copy-done.12), kind=kOutput, calls=%fused_computation.3 | convolution fusion | flops 2148532224 | bytes 7340032 | tf_op jit(solution)/shard_map/dot_general | solution.py:48
  332.2 0.0 reduce-scatter.3.cloned.1.call-done.source_ref
  332.3 0.0 copy-start.9
  332.3 1.2 copy-done.9
  333.5 1.7 turn.1._down
  335.2 0.0 copy-start.1
  335.2 0.0 copy-start.6
  335.2 0.0 copy-start.7
  335.2 0.0 copy-start.8
  335.2 90.8 %attend_back.1 = (bf16[1024,1536]{1,0:T(8,128)(2,1)}, f32[1024,512]{1,0:T(8,128)}, f32[1024,512]{1,0:T(8,128)}) custom-call(bf16[1024,512]{1,0:T(8,128)(2,1)} %get-tuple-element.48.q_ref, bf16[1024,512]{1,0:T(8,128)(2,1)} %get-tuple-element.49.k_ref, bf16[1024,512]{1,0:T(8,128)(2,1)} %get-tuple-element.50.v_ref, f32[1024,128]{1,0:T(8,128)} %get-tuple-element.51.segc_ref, ...), custom_call_target="tpu_custom_call" | custom-call | flops 2000000000 | bytes 7200000 | tf_op jit(solution)/shard_map/attend_back/pallas_call | solution.py:1622
  426.0 0.0 copy-done.1
  426.0 0.0 copy-done.3
  426.0 0.0 copy-done.4
  426.0 0.0 copy-done.5
  426.0 0.0 copy-done.6
  426.0 0.0 copy-done.7
  426.0 0.0 copy-done.8
  426.1 0.0 copy-start.2
  426.1 1.6 copy-done.2
  427.7 21.1 %streams.1 = (bf16[1024,4,512]{2,1,0:T(4,128)(2,1)}, f32[1024,4,512]{2,1,0:T(4,128)}, f32[48,8,128]{2,1,0:T(8,128)S(1)}) custom-call(f32[4]{0:T(128)S(1)} %copy-done.5, f32[4]{0:T(128)S(1)} %copy-done.6, f32[4]{0:T(128)S(1)} %copy-done.7, f32[4]{0:T(128)S(1)} %copy-done.8, f32[4,4]{1,0:T(4,128)S(1)} %copy-done.3, f32[4,4]{1,0:T(4,128)S(1)} %copy-done.4, ...), custom_call_target="tpu_custom_call" | custom-call | flops 2000000000 | bytes 7200000 | tf_op jit(solution)/shard_map/streams/pallas_call | solution.py:1670
  448.8 0.0 copy-done.10
  448.8 0.0 copy-done.11
  448.8 0.0 copy-start
  448.8 8.7 %convolution_convert_fusion.1.first_hbm = bf16[2048,1536]{1,0:T(8,128)(2,1)} fusion(bf16[1024,2048]{1,0:T(8,128)(2,1)S(1)} %copy-done.10, bf16[1024,1536]{1,0:T(8,128)(2,1)S(1)} %copy-done.11), kind=kOutput, calls=%fused_computation.1 | convolution fusion | flops 6445596672 | bytes 13631488 | tf_op jit(solution)/shard_map/dot_general | solution.py:48
  457.5 0.0 copy-done
  457.5 77.7 %finish.1 = (f32[256,512]{1,0:T(8,128)S(1)}, f32[256,512]{1,0:T(8,128)S(1)}, f32[256,512]{1,0:T(8,128)S(1)}, f32[512,256]{1,0:T(8,128)S(1)}, f32[48,128]{1,0:T(8,128)S(1)}) custom-call(bf16[2048,1536]{1,0:T(8,128)(2,1)} %convolution_convert_fusion.1.first_hbm, bf16[2048,512]{1,0:T(8,128)(2,1)S(1)} %copy-done, f32[48,8,128]{2,1,0:T(8,128)S(1)} %get-tuple-element.73.sums_ref), custom_call_target="tpu_custom_call" | custom-call | flops 2000000000 | bytes 7200000 | tf_op jit(solution)/shard_map/finish/pallas_call | solution.py:1691
  535.2 0.1 reduce_sum.9
  535.4 0.1 fusion.1
  535.4 0.7 reshape.60
  536.1 0.7 reshape.61
  536.8 0.6 fusion
  537.4 4.1 slice_convert_fusion
  541.4 0.8 copy.39
  542.2 0.8 copy.40
  543.0 0.8 copy.41
  543.8 0.8 copy.42
  (6 shorter events, 0.0 us)
Async XLA Ops:
  7.2 325.1 %reduce-scatter.3.cloned.1.call-start = ((), (), s32[]{:S(2)}) async-start(), calls=%async_computation.2 | async-start | bytes 5242880 | tf_op jit(solution)/shard_map/reduce_scatter | solution.py:1565
  212.7 324.7 %reduce-scatter.5.cloned.1.call-start = ((), (), s32[]{:S(2)}) async-start(), calls=%async_computation.3 | async-start | bytes 18874368 | tf_op jit(solution)/shard_map/reduce_scatter | solution.py:1531
  237.3 88.9 %copy-start.12 = (bf16[1024,512]{1,0:T(8,128)(2,1)S(1)}, bf16[1024,512]{1,0:T(8,128)(2,1)}, u32[]{:S(2)}) copy-start(bf16[1024,512]{1,0:T(8,128)(2,1)} %get-tuple-element.66) | copy-start | bytes 3145732
  332.3 1.3 copy-start.9
  335.2 90.8 %copy-start.1 = (f32[1024,512]{1,0:T(8,128)S(1)}, f32[1024,512]{1,0:T(8,128)}, u32[]{:S(2)}) copy-start(f32[1024,512]{1,0:T(8,128)} %get-tuple-element.54.b1_ref) | copy-start | bytes 6291460
  335.2 90.8 %copy-start.3 = (f32[4,4]{1,0:T(4,128)S(1)}, f32[4,4]{1,0:T(4,128)}, u32[]{:S(2)}) copy-start(f32[4,4]{1,0:T(4,128)} %res1.5) | copy-start | bytes 196
  335.2 90.8 %copy-start.4 = (f32[4,4]{1,0:T(4,128)S(1)}, f32[4,4]{1,0:T(4,128)}, u32[]{:S(2)}) copy-start(f32[4,4]{1,0:T(4,128)} %res2.5) | copy-start | bytes 196
  335.2 90.8 %copy-start.5 = (f32[4]{0:T(128)S(1)}, f32[4]{0:T(128)}, u32[]{:S(2)}) copy-start(f32[4]{0:T(128)} %in1.7) | copy-start | bytes 52
  335.2 90.9 %copy-start.6 = (f32[4]{0:T(128)S(1)}, f32[4]{0:T(128)}, u32[]{:S(2)}) copy-start(f32[4]{0:T(128)} %out1.5) | copy-start | bytes 52
  335.2 90.9 %copy-start.7 = (f32[4]{0:T(128)S(1)}, f32[4]{0:T(128)}, u32[]{:S(2)}) copy-start(f32[4]{0:T(128)} %in2.5) | copy-start | bytes 52
  335.2 90.8 %copy-start.8 = (f32[4]{0:T(128)S(1)}, f32[4]{0:T(128)}, u32[]{:S(2)}) copy-start(f32[4]{0:T(128)} %out2.7) | copy-start | bytes 52
  426.1 1.6 copy-start.2
  427.6 21.1 %copy-start.10 = (bf16[1024,2048]{1,0:T(8,128)(2,1)S(1)}, bf16[1024,2048]{1,0:T(8,128)(2,1)}, u32[]{:S(2)}) copy-start(bf16[1024,2048]{1,0:T(8,128)(2,1)} %get-tuple-element.65.normed_hbm) | copy-start | bytes 12582916
  427.6 21.1 %copy-start.11 = (bf16[1024,1536]{1,0:T(8,128)(2,1)S(1)}, bf16[1024,1536]{1,0:T(8,128)(2,1)}, u32[]{:S(2)}) copy-start(bf16[1024,1536]{1,0:T(8,128)(2,1)} %get-tuple-element.72) | copy-start | bytes 9437188
  448.8 8.7 %copy-start = (bf16[2048,512]{1,0:T(8,128)(2,1)S(1)}, bf16[2048,512]{1,0:T(8,128)(2,1)}, u32[]{:S(2)}) copy-start(bf16[2048,512]{1,0:T(8,128)(2,1)} %convolution_convert_fusion.2._output.last_hbm) | copy-start | bytes 6291460
Sparse Core Ops, SparseCore 0:
  212.8 77.5 reduce-scatter.2
  292.9 168.7 reduce-scatter.4
